TPU v7x, 128 devices: a whole 4x4x4 slice. The times are simulated.
128 devices in a mesh: seg: 8 (over x, core), row: 16 (over y, z).
Axes of the slice: x: 4, y: 4, z: 4, core: 2. Of those that a mesh axis runs over, the one named last changes fastest.
Arguments:
- terminal_adjoint: float32 [8, 2, 2048, 2048], P('seg', None, 'row'), may hold values from -6 to 6
- midpoint_state: float32 [8, 1, 2, 2048, 2048], P('seg', None, None, 'row'), may hold values from -6 to 6
- controls: float32 [8, 1, 4], P('seg'), may hold values from -8 to 8
- detuning: float32 [4], replicated, may hold values from -3 to 3
- anharmonicity: float32 [4], replicated, may hold values from 0.2 to 1
- decay_rate: float32 [4], replicated, may hold values from 0.2 to 2
- dephasing: float32 [4], replicated, may hold values from 0.1 to 1
- cross_kerr: float32 [6], replicated, may hold values from 0.05 to 0.3
Outputs:
- start_adjoint: float32 [8, 2, 2048, 2048], P('seg', None, 'row')
- continuity_defect: float32 [8, 2, 2048, 2048], P('seg', None, 'row')
- control_gradient: float32 [8, 1, 4], P('seg')
All inputs are finite; a program needn't handle non-finite values.
Results may differ from a plain program's by a relative error of at most 0.00011.
Values sent between devices are 32-bit elements; how exact they have to be, the bound alone decides.
No kernel may reach another device: no remote copies, remote signals or barrier semaphores. Data moves between devices by JAX's collectives and lax.ppermute only.
A program may use at most 128 MiB of HBM per device.

v0:
```python
import jax
import jax.numpy as jnp
import numpy as np
from jax import lax
from jax.experimental import pallas as pl
from jax.experimental.pallas import tpu as pltpu
from jax.sharding import PartitionSpec as P


ORDER = 2048
STEP = 0.01
UNITS = 32
ROWS = 16
LANES = 128
TILES = 4
WIDTH = TILES * LANES
F32 = jnp.float32

GROUPS = [
    [4 * y + z for y in (0, 1) for z in (0, 1, 3, 2)],
    [4 * y + z for y in (3, 2) for z in (2, 3, 1, 0)],
]
Y_OUTER = {0: 3, 3: 0, 1: 2, 2: 1}
Y_INNER = {0: 1, 1: 0, 2: 3, 3: 2}


def pairs_y(flip):
    return [(4 * y + z, 4 * flip[y] + z) for y in range(4) for z in range(4)]


def pairs_z(flip):
    return [(4 * y + z, 4 * y + flip[z]) for y in range(4) for z in range(4)]


PERM_I0 = pairs_y(Y_OUTER)
PERM_I2 = pairs_y(Y_INNER)
PERM_J0 = pairs_z(Y_OUTER)
PERM_J1 = pairs_z(Y_INNER)
PERM_CORNER = [(4 * y + z, 4 * Y_OUTER[y] + Y_OUTER[z]) for y in (0, 1) for z in (0, 1)]
ROOTS = np.sqrt(np.arange(16)).astype(np.float32)


class Place:
    def __init__(self):
        row = lax.axis_index("row")
        y = row // 4
        z = row % 4
        self.upper = y // 2
        self.gi2 = jnp.where((y == 1) | (y == 2), 1, 0)
        self.gj0 = z // 2
        self.gj1 = jnp.where((z == 1) | (z == 2), 1, 0)


def unit_at(p, i1):
    h = i1 // 4
    odd = p % 2
    return ((p // 2) * 4 + jnp.where(odd == 1, 3 - h, h)) * 4 + i1 % 4


def iotas():
    lane = lax.broadcasted_iota(jnp.int32, (ROWS, LANES), 1)
    sub = lax.broadcasted_iota(jnp.int32, (ROWS, LANES), 0)
    return lane, sub


class Tables:
    def __init__(self, place):
        lane, sub = iotas()
        low1 = lane // 32
        self.j1 = (low1 + 4 * place.gj1).astype(F32)
        self.j2 = ((lane // 4) % 8).astype(F32)
        self.j3 = (lane % 4).astype(F32)
        low2 = sub // 4
        self.i2 = (low2 + 4 * place.gi2).astype(F32)
        self.i3 = (sub % 4).astype(F32)
        self.c1p = jnp.where(low1 > 0, jnp.sqrt(self.j1), 0.0)
        self.c1m = jnp.where(low1 < 3, jnp.sqrt(self.j1 + 1.0), 0.0)
        self.c2p = jnp.sqrt(self.j2)
        self.c2m = jnp.where(self.j2 < 7.0, jnp.sqrt(self.j2 + 1.0), 0.0)
        self.c3p = jnp.sqrt(self.j3)
        self.c3m = jnp.where(self.j3 < 3.0, jnp.sqrt(self.j3 + 1.0), 0.0)
        self.r2p = jnp.where(low2 > 0, jnp.sqrt(self.i2), 0.0)
        self.r2m = jnp.where(low2 < 3, jnp.sqrt(self.i2 + 1.0), 0.0)
        self.r3p = jnp.sqrt(self.i3)
        self.r3m = jnp.where(self.i3 < 3.0, jnp.sqrt(self.i3 + 1.0), 0.0)
        edge1 = jnp.where(place.gj1 == 1, 0, 3)
        edge2 = jnp.where(place.gi2 == 1, 0, 3)
        self.edge1 = edge1
        self.at1 = (low1 == edge1).astype(F32)
        self.at2 = (low2 == edge2).astype(F32)


def drift(levels, detuning, anharmonicity, cross_kerr):
    total = 0.0
    for q in range(4):
        n = levels[q]
        total = total + detuning[q] * n - 0.5 * anharmonicity[q] * n * (n - 1.0)
    k = 0
    for a in range(4):
        for b in range(a + 1, 4):
            total = total - cross_kerr[k] * levels[a] * levels[b]
            k += 1
    return total


def decay_part(levels, decay, dephasing):
    total = 0.0
    for q in range(4):
        n = levels[q]
        total = total - 0.5 * decay[q] * n - 0.5 * dephasing[q] * n * n
    return total


def tile(ref, unit, c, t):
    return ref[unit, c, :, t * LANES : (t + 1) * LANES]


def level_of(place, p):
    return jnp.where(place.upper == 1, 7 - p, p)


def local_kernel(scale, with_gradient, *refs):
    if with_gradient:
        (z, base, rho, amp, det, anh, dec, dep, kerr, roots, out, sums) = refs
    else:
        (z, base, amp, det, anh, dec, dep, kerr, roots, out) = refs
    place = Place()
    tb = Tables(place)
    up = place.upper == 1
    detuning = [det[0, q] for q in range(4)]
    anharm = [anh[0, q] for q in range(4)]
    decay = [dec[0, q] for q in range(4)]
    dephasing = [dep[0, q] for q in range(4)]
    cross = [kerr[0, k] for k in range(6)]
    u = [amp[0, q] for q in range(4)]
    column_energy = []
    column_decay = []
    for t in range(TILES):
        j0 = (4 * place.gj0 + t).astype(F32)
        levels = [j0, tb.j1, tb.j2, tb.j3]
        column_energy.append(drift(levels, detuning, anharm, cross))
        column_decay.append(decay_part(levels, decay, dephasing))
    cross2 = dephasing[2] * tb.i2
    cross3 = dephasing[3] * tb.i3
    s2p = decay[2] * tb.r2p
    s3p = decay[3] * tb.r3p

    def step(n, carry):
        p = n // 8
        i1 = n % 8
        here = unit_at(p, i1)
        i0 = level_of(place, p)
        below = jnp.where(up, p + 1, p - 1)
        above = jnp.where(up, p - 1, p + 1)
        below_in = (below >= 0) & (below <= 3)
        above_in = (above >= 0) & (above <= 3)
        at_below = unit_at(jnp.clip(below, 0, 3), i1)
        at_above = unit_at(jnp.clip(above, 0, 3), i1)
        root_below = jnp.where(below_in, roots[0, i0], 0.0)
        root_above = jnp.where(above_in, roots[0, i0 + 1], 0.0)
        at_less = unit_at(p, jnp.maximum(i1 - 1, 0))
        at_more = unit_at(p, jnp.minimum(i1 + 1, 7))
        root_less = roots[0, i1]
        root_more = jnp.where(i1 < 7, roots[0, i1 + 1], 0.0)
        i0f = i0.astype(F32)
        i1f = i1.astype(F32)
        rows = [i0f, i1f, tb.i2, tb.i3]
        row_energy = drift(rows, detuning, anharm, cross)
        row_decay = decay_part(rows, decay, dephasing)
        new_carry = list(carry)
        for t in range(TILES):
            j0 = 4 * place.gj0 + t
            root_left = roots[0, j0]
            root_right = roots[0, j0 + 1]
            comm = []
            sand = []
            values = []
            parts = []
            for c in range(2):
                m = tile(z, here, c, t)
                values.append(m)
                w1 = tb.c1p * pltpu.roll(m, 32, 1)
                w2 = tb.c2p * pltpu.roll(m, 4, 1)
                w3 = tb.c3p * pltpu.roll(m, 1, 1)
                less = tile(z, at_less, c, t)
                k0 = root_below * tile(z, at_below, c, t) + root_above * tile(z, at_above, c, t)
                if t > 0:
                    k0 = k0 - root_left * tile(z, here, c, t - 1)
                if t < TILES - 1:
                    k0 = k0 - root_right * tile(z, here, c, t + 1)
                k1 = (
                    root_less * less
                    + root_more * tile(z, at_more, c, t)
                    - w1
                    - tb.c1m * pltpu.roll(m, LANES - 32, 1)
                )
                k2 = (
                    tb.r2p * pltpu.roll(m, 4, 0)
                    + tb.r2m * pltpu.roll(m, ROWS - 4, 0)
                    - w2
                    - tb.c2m * pltpu.roll(m, LANES - 4, 1)
                )
                k3 = (
                    tb.r3p * pltpu.roll(m, 1, 0)
                    + tb.r3m * pltpu.roll(m, ROWS - 1, 0)
                    - w3
                    - tb.c3m * pltpu.roll(m, LANES - 1, 1)
                )
                parts.append((k0, k1, k2, k3))
                comm.append(u[0] * k0 + u[1] * k1 + u[2] * k2 + u[3] * k3)
                s = (
                    (decay[1] * root_less) * (tb.c1p * pltpu.roll(less, 32, 1))
                    + s2p * pltpu.roll(w2, 4, 0)
                    + s3p * pltpu.roll(w3, 1, 0)
                )
                if t > 0:
                    s = s + (decay[0] * root_below * root_left) * tile(z, at_below, c, t - 1)
                sand.append(s)
            phase = row_energy - column_energy[t]
            damping = (
                row_decay
                + column_decay[t]
                + (dephasing[0] * i0f) * j0.astype(F32)
                + (dephasing[1] * i1f) * tb.j1
                + cross2 * tb.j2
                + cross3 * tb.j3
            )
            x, y = values
            lanes = slice(t * LANES, (t + 1) * LANES)
            out[here, 0, :, lanes] = tile(base, here, 0, t) + scale * (
                damping * x - phase * y - comm[1] + sand[0]
            )
            out[here, 1, :, lanes] = tile(base, here, 1, t) + scale * (
                damping * y + phase * x + comm[0] + sand[1]
            )
            if with_gradient:
                re = tile(rho, here, 0, t)
                im = tile(rho, here, 1, t)
                for q in range(4):
                    new_carry[q] = new_carry[q] + parts[0][q] * im - parts[1][q] * re
        return tuple(new_carry)

    start = tuple(jnp.zeros((ROWS, LANES), F32) for _ in range(4)) if with_gradient else ()
    total = lax.fori_loop(0, UNITS, step, start)
    if with_gradient:
        for q in range(4):
            sums[q] = total[q]


def put_slabs(place, tb, p, pair, both, s_i0, s_i2, s_j0, s_j1, s_c):
    lane, _ = iotas()
    half = lax.broadcasted_iota(jnp.int32, (8, LANES), 0) < 4
    block = lane // 32
    gj0 = place.gj0 == 1
    gi2 = place.gi2 == 1
    for par in range(2):
        i1 = 2 * pair + par
        n = p * 8 + i1
        for c in range(2):
            tiles = both[par][c]
            if p == 3:
                for t in range(TILES):
                    s_i0[i1, c, :, t * LANES : (t + 1) * LANES] = tiles[t]
                s_c[i1, c] = tiles[TILES - 1]
            s_j0[n, c] = jnp.where(gj0, tiles[0], tiles[TILES - 1])
            packed = jnp.zeros((ROWS, LANES), F32)
            for t in range(TILES):
                turned = jnp.where(
                    place.gj1 == 1,
                    pltpu.roll(tiles[t], (32 * t) % LANES, 1) if t else tiles[t],
                    pltpu.roll(tiles[t], (32 * (t + 1)) % LANES, 1) if t < 3 else tiles[t],
                )
                packed = jnp.where(block == t, turned, packed)
            s_j1[n, c] = packed
    for c in range(2):
        for t in range(TILES):
            even, odd = both[0][c][t], both[1][c][t]
            first = jnp.where(gi2, even[0:8], pltpu.roll(even[8:16], 4, 0))
            second = jnp.where(gi2, pltpu.roll(odd[0:8], 4, 0), odd[8:16])
            s_i2[p * 4 + pair, c, :, t * LANES : (t + 1) * LANES] = jnp.where(half, first, second)


def slab_kernel(z, s_i0, s_i2, s_j0, s_j1, s_c):
    place = Place()
    tb = Tables(place)
    for p in range(4):

        def step(pair, carry, p=p):
            both = [
                [[tile(z, unit_at(p, 2 * pair + par), c, t) for t in range(TILES)] for c in range(2)]
                for par in range(2)
            ]
            put_slabs(place, tb, p, pair, both, s_i0, s_i2, s_j0, s_j1, s_c)
            return carry

        lax.fori_loop(0, 4, step, 0)


def edge_kernel(scale, last, *refs):
    if last:
        (part, h_i0, h_i2, h_j0, h_j1, h_c, rho, sums, amp, dec, roots, out, grad) = refs
    else:
        (part, h_i0, h_i2, h_j0, h_j1, h_c, amp, dec, roots, out, *slabs) = refs
    place = Place()
    tb = Tables(place)
    up = place.upper == 1
    upf = place.upper.astype(F32)
    gi2 = place.gi2 == 1
    gj0f = place.gj0.astype(F32)
    gj1f = place.gj1.astype(F32)
    gi2f = place.gi2.astype(F32)
    decay = [dec[0, q] for q in range(4)]
    u = [amp[0, q] for q in range(4)]
    total = tuple(jnp.zeros((ROWS, LANES), F32) for _ in range(3))
    s1_base = (decay[1] * 2.0 * gj1f) * tb.at1
    s2_base = (decay[2] * 2.0 * gi2f) * tb.at2 * tb.c2p
    k1_mask = -2.0 * tb.at1
    k2_mask = 2.0 * tb.at2
    for p in range(4):

        def step(pair, carry, p=p):
            i0 = jnp.where(up, 7 - p, p)
            below = jnp.where(up, p + 1, p - 1)
            below_in = (below >= 0) & (below <= 3)
            below = jnp.clip(below, 0, 3)
            root_below = jnp.where(below_in, roots[0, i0], 0.0)
            both = []
            acc = list(carry)
            for par in range(2):
                i1 = 2 * pair + par
                here = unit_at(p, i1)
                n = p * 8 + i1
                root_less = roots[0, i1]
                n_less = p * 8 + jnp.maximum(i1 - 1, 0)
                new = [[], []]
                for t in range(TILES):
                    j0 = 4 * place.gj0 + t
                    lanes = slice(t * LANES, (t + 1) * LANES)
                    comm = []
                    sand = []
                    parts = []
                    for c in range(2):
                        small = h_i2[p * 4 + pair, c, :, lanes]
                        turned = pltpu.roll(small, 4, 0)
                        small = jnp.where(gi2, turned, small) if par else jnp.where(gi2, small, turned)
                        both2 = jnp.concatenate([small, small], axis=0)
                        k2 = k2_mask * both2
                        s = s2_base * pltpu.roll(both2, 4, 1)
                        k1 = k1_mask * pltpu.roll(h_j1[n, c], (32 * (tb.edge1 - t)) % LANES, 1)
                        s = s + (root_less * s1_base) * pltpu.roll(h_j1[n_less, c], (32 * (tb.edge1 - t)) % LANES, 1)
                        k0 = None
                        if p == 3:
                            k0 = 2.0 * h_i0[i1, c, :, lanes]
                            if t > 0:
                                s = s + (decay[0] * 2.0 * upf * roots[0, j0]) * h_i0[
                                    i1, c, :, (t - 1) * LANES : t * LANES
                                ]
                            else:
                                s = s + (decay[0] * 4.0 * upf * gj0f) * h_c[i1, c]
                        if t == 0 or t == TILES - 1:
                            on = gj0f if t == 0 else 1.0 - gj0f
                            term = (2.0 * on) * h_j0[n, c]
                            k0 = -term if k0 is None else k0 - term
                        if t == 0:
                            s = s + (decay[0] * 2.0 * gj0f * root_below) * h_j0[below * 8 + i1, c]
                        k = u[1] * k1 + u[2] * k2
                        if k0 is not None:
                            k = k + u[0] * k0
                        comm.append(k)
                        sand.append(s)
                        parts.append((k0, k1, k2))
                    x = tile(part, here, 0, t) + scale * (sand[0] - comm[1])
                    y = tile(part, here, 1, t) + scale * (sand[1] + comm[0])
                    out[here, 0, :, lanes] = x
                    out[here, 1, :, lanes] = y
                    new[0].append(x)
                    new[1].append(y)
                    if last:
                        re = tile(rho, here, 0, t)
                        im = tile(rho, here, 1, t)
                        for q in range(3):
                            if parts[0][q] is not None:
                                acc[q] = acc[q] + parts[0][q] * im - parts[1][q] * re
                both.append(new)
            if not last:
                put_slabs(place, tb, p, pair, both, *slabs)
            return tuple(acc)

        total = lax.fori_loop(0, 4, step, total)
    if last:
        for q in range(4):
            value = sums[q] + total[q] if q < 3 else sums[q]
            grad[q : q + 1] = jnp.sum(value, axis=0, keepdims=True)
        grad[4:8] = jnp.zeros((4, LANES), F32)


def pack_kernel(x, out):
    upper = lax.axis_index("row") // 8
    for gi2 in range(2):
        for g in range(4):
            k = 4 * gi2 + jnp.where(upper == 1, 3 - g, g)
            gj0, gj1 = g // 2, g % 2
            for c in range(2):
                for t in range(TILES):
                    start = gj0 * 1024 + t * 256 + gj1 * 128
                    out[k, 0, c, :, t * LANES : (t + 1) * LANES] = x[
                        c, gi2 * 16 : gi2 * 16 + 16, start : start + LANES
                    ]


def unpack_kernel(subtract, *refs):
    if subtract:
        x, base, out = refs
    else:
        x, out = refs
    upper = lax.axis_index("row") // 8
    for gi2 in range(2):
        for g in range(4):
            k = 4 * gi2 + jnp.where(upper == 1, 3 - g, g)
            gj0, gj1 = g // 2, g % 2
            for c in range(2):
                for t in range(TILES):
                    start = gj0 * 1024 + t * 256 + gj1 * 128
                    value = x[k, 0, c, :, t * LANES : (t + 1) * LANES]
                    rows = slice(gi2 * 16, gi2 * 16 + 16)
                    if subtract:
                        value = base[c, rows, start : start + LANES] - value
                    out[c, rows, start : start + LANES] = value


VMEM = pl.BlockSpec(memory_space=pltpu.VMEM)
SMEM = pl.BlockSpec(memory_space=pltpu.SMEM)
PARAMS = pltpu.CompilerParams(vmem_limit_bytes=48 * 1024 * 1024)
UNIT_SHAPE = (UNITS, 2, ROWS, WIDTH)
SLAB_SHAPES = [
    (8, 2, ROWS, WIDTH),
    (16, 2, 8, WIDTH),
    (UNITS, 2, ROWS, LANES),
    (UNITS, 2, ROWS, LANES),
    (8, 2, ROWS, LANES),
]


def shape(dims):
    return jax.ShapeDtypeStruct(dims, F32)


def cost(flops, bytes_accessed):
    return pl.CostEstimate(flops=flops, bytes_accessed=bytes_accessed, transcendentals=0)


PACKED_BLOCK = pl.BlockSpec((8, 1, 2, ROWS, WIDTH), lambda a: (0, a, 0, 0, 0))
PLAIN_BLOCK = pl.BlockSpec((2, 32, ORDER), lambda a: (0, a, 0))
PACKED_SHAPE = (8, 4, 2, ROWS, WIDTH)


def pack(x):
    return pl.pallas_call(
        pack_kernel,
        out_shape=shape(PACKED_SHAPE),
        grid=(4,),
        in_specs=[PLAIN_BLOCK],
        out_specs=PACKED_BLOCK,
        compiler_params=PARAMS,
        cost_estimate=cost(0, 4 << 20),
        name="pack_blocks",
    )(x)


def unpack(x, base=None):
    subtract = base is not None
    args = (x, base) if subtract else (x,)

    def kernel(*refs):
        unpack_kernel(subtract, *refs)

    return pl.pallas_call(
        kernel,
        out_shape=shape((2, 128, ORDER)),
        grid=(4,),
        in_specs=[PACKED_BLOCK] + ([PLAIN_BLOCK] if subtract else []),
        out_specs=PLAIN_BLOCK,
        compiler_params=PARAMS,
        cost_estimate=cost(0, 4 << 20),
        name="unpack_blocks",
    )(*args)


def regroup(x):
    return lax.all_to_all(x, "row", 0, 0, axis_index_groups=GROUPS, tiled=True)


def exchange(slabs):
    s_i0, s_i2, s_j0, s_j1, s_c = slabs
    return (
        lax.ppermute(s_i0, "row", PERM_I0),
        lax.ppermute(s_i2, "row", PERM_I2),
        lax.ppermute(s_j0, "row", PERM_J0),
        lax.ppermute(s_j1, "row", PERM_J1),
        lax.ppermute(s_c, "row", PERM_CORNER),
    )


def slabs_of(z):
    return pl.pallas_call(
        slab_kernel,
        out_shape=[shape(s) for s in SLAB_SHAPES],
        in_specs=[VMEM],
        out_specs=[VMEM] * 5,
        compiler_params=PARAMS,
        cost_estimate=cost(0, 4 << 20),
        name="slabs",
    )(z)


def local_terms(scale, z, base, scalars, rho=None):
    grad = rho is not None
    args = [z, base] + ([rho] if grad else []) + list(scalars)
    outs = [shape(UNIT_SHAPE)] + ([shape((4, ROWS, LANES))] if grad else [])

    def kernel(*refs):
        local_kernel(scale, grad, *refs)

    return pl.pallas_call(
        kernel,
        out_shape=outs,
        in_specs=[VMEM] * (3 if grad else 2) + [SMEM] * len(scalars),
        out_specs=[VMEM] * len(outs),
        compiler_params=PARAMS,
        cost_estimate=cost(60 * 512 * 1024, 6 << 20),
        name="local_terms",
    )(*args)


def edge_terms(scale, part, halos, scalars, rho=None, sums=None):
    last = rho is not None
    args = [part, *halos] + ([rho, sums] if last else []) + list(scalars)
    outs = [shape(UNIT_SHAPE)]
    if last:
        outs += [shape((8, LANES))]
    else:
        outs += [shape(s) for s in SLAB_SHAPES]

    def kernel(*refs):
        edge_kernel(scale, last, *refs)

    return pl.pallas_call(
        kernel,
        out_shape=outs,
        in_specs=[VMEM] * (len(args) - len(scalars)) + [SMEM] * len(scalars),
        out_specs=[VMEM] * len(outs),
        compiler_params=PARAMS,
        cost_estimate=cost(10 * 512 * 1024, 6 << 20),
        name="edge_terms",
    )(*args)


def body(
    terminal_adjoint,
    midpoint_state,
    controls,
    detuning,
    anharmonicity,
    decay_rate,
    dephasing,
    cross_kerr,
):
    amp = controls[0]
    dec = decay_rate[None]
    roots = jnp.asarray(ROOTS)[None]
    full = (amp, detuning[None], anharmonicity[None], dec, dephasing[None], cross_kerr[None], roots)
    few = (amp, dec, roots)
    terminal = terminal_adjoint[0]
    base = regroup(pack(terminal)).reshape(UNIT_SHAPE)
    slabs = slabs_of(base)
    rho = regroup(pack(midpoint_state[0, 0])).reshape(UNIT_SHAPE)
    current = base
    for sweep in range(2):
        halos = exchange(slabs)
        (part,) = local_terms(0.5 * STEP, current, base, full)
        current, *slabs = edge_terms(0.5 * STEP, part, halos, few)
    halos = exchange(slabs)
    part, sums = local_terms(STEP, current, base, full, rho)
    final, grad = edge_terms(STEP, part, halos, few, rho, sums)
    back = regroup(final.reshape(PACKED_SHAPE))
    for perm in (PERM_I0, PERM_I2, PERM_J0, PERM_J1):
        grad = grad + lax.ppermute(grad, "row", perm)
    following = lax.ppermute(back, "seg", [(i + 1, i) for i in range(7)])
    start = unpack(back)
    defect = unpack(following, terminal)
    totals = jnp.sum(grad[:4], axis=1) / ORDER
    return start[None], defect[None], totals[None, None]


def solution(mesh):
    return jax.shard_map(
        body,
        mesh=mesh,
        in_specs=(
            P("seg", None, "row", None),
            P("seg", None, None, "row", None),
            P("seg", None, None),
            P(),
            P(),
            P(),
            P(),
            P(),
        ),
        out_specs=(P("seg", None, "row", None), P("seg", None, "row", None), P("seg", None, None)),
        check_vma=False,
    )
```

profile of v0, /device:TPU:1, one launch (start us, length us, event | category | flops | bytes accessed | tf_op | source)
XLA Modules:
  0.0 198.7 jit_solution(15197306416036564014)
XLA Ops:
  0.6 0.0 copy-start.1
  0.6 1.6 copy-done.1
  2.2 0.6 pack_blocks.2
  2.8 1.3 copy-done.6
  4.1 6.9 %all-to-all-start = ((f32[8,4,2,16,512]{4,3,2,1,0:T(8,128)}), f32[8,4,2,16,512]{4,3,2,1,0:T(8,128)S(1)}, u32[]{:S(2)}, u32[]{:S(2)}) async-start(f32[8,4,2,16,512]{4,3,2,1,0:T(8,128)} %copy-done.6), calls=%async_computation | async-start | bytes 4194304 | tf_op jit(solution)/shard_map/all_to_all | solution.py:490
  11.0 1.6 copy-done.7
  12.6 0.6 pack_blocks.3
  13.2 1.4 copy-done.5
  14.5 22.9 %all-to-all-done = f32[8,4,2,16,512]{4,3,2,1,0:T(8,128)S(1)} async-done(((f32[8,4,2,16,512]{4,3,2,1,0:T(8,128)}), f32[8,4,2,16,512]{4,3,2,1,0:T(8,128)S(1)}, u32[]{:S(2)}, u32[]{:S(2)}) %all-to-all-start) | async-done | bytes 2097184 | tf_op jit(solution)/shard_map/all_to_all | solution.py:490
  37.5 5.8 %all-to-all-start.1 = ((f32[8,4,2,16,512]{4,3,2,1,0:T(8,128)}), f32[8,4,2,16,512]{4,3,2,1,0:T(8,128)}, u32[]{:S(2)}, u32[]{:S(2)}) async-start(f32[8,4,2,16,512]{4,3,2,1,0:T(8,128)} %copy-done.5), calls=%async_computation.1 | async-start | bytes 4194304 | tf_op jit(solution)/shard_map/all_to_all | solution.py:490
  43.3 0.0 copy-start.13
  43.3 1.9 slabs.1
  45.3 3.0 %collective-permute-start = (f32[8,2,16,512]{3,2,1,0:T(8,128)S(1)}, f32[8,2,16,512]{3,2,1,0:T(8,128)S(1)}, u32[]{:S(2)}, u32[]{:S(2)}) collective-permute-start(f32[8,2,16,512]{3,2,1,0:T(8,128)S(1)} %get-tuple-element.24), channel_id=1, source_target_pairs={{0,12},{1,13},{2,14},{3,15},{4,8},{5,9},{6,10},{7,11},{8,4},{9,5},... | collective-permute-start | bytes 1572872 | tf_op jit(solution)/shard_map/ppermute | solution.py:496
  48.3 0.5 collective-permute-start.1
  48.8 0.5 collective-permute-start.2
  49.3 4.5 %collective-permute-start.4 = (f32[8,2,16,128]{3,2,1,0:T(8,128)S(1)}, f32[8,2,16,128]{3,2,1,0:T(8,128)S(1)}, u32[]{:S(2)}, u32[]{:S(2)}) collective-permute-start(f32[8,2,16,128]{3,2,1,0:T(8,128)S(1)} %get-tuple-element.28), channel_id=1, source_target_pairs={{0,15},{1,14},{4,11},{5,10},{16,31},{17,30},{20,27},{21,26},{32,47... | collective-permute-start | bytes 393224 | tf_op jit(solution)/shard_map/ppermute | solution.py:500
  53.9 7.5 %local_terms.3.refs_0_ = f32[32,2,16,512]{3,2,1,0:T(8,128)S(1)} custom-call(f32[32,2,16,512]{3,2,1,0:T(8,128)S(1)} %bitcast.16, f32[32,2,16,512]{3,2,1,0:T(8,128)S(1)} %bitcast.17, f32[1,4]{1,0:T(1,128)S(1)} %bitcast.24, f32[1,4]{1,0:T(1,128)S(1)} %bitcast.36, f32[1,4]{1,0:T(1,128)S(1)} %bitcast.39, f32[1,4]{1,0:T(1,128)S(1)} %bitcast.30, ...), custom_call_target="tpu_custom_call" | custom-call | flops 31457280 | bytes 6291456 | tf_op jit(solution)/shard_map/local_terms/pallas_call | solution.py:524
  61.4 1.3 copy-done.4
  62.7 16.0 %collective-permute-done.1.refs_2_ = f32[16,2,8,512]{3,2,1,0:T(8,128)S(1)} collective-permute-done((f32[16,2,8,512]{3,2,1,0:T(8,128)S(1)}, f32[16,2,8,512]{3,2,1,0:T(8,128)S(1)}, u32[]{:S(2)}, u32[]{:S(2)}) %collective-permute-start.1) | collective-permute-done | bytes 524320 | tf_op jit(solution)/shard_map/ppermute | solution.py:497
  78.8 1.1 collective-permute-done.2.refs_3_
  79.9 6.7 %edge_terms.3 = (f32[32,2,16,512]{3,2,1,0:T(8,128)}, f32[8,2,16,512]{3,2,1,0:T(8,128)S(1)}, f32[16,2,8,512]{3,2,1,0:T(8,128)S(1)}, f32[32,2,16,128]{3,2,1,0:T(8,...) custom-call(f32[32,2,16,512]{3,2,1,0:T(8,128)} %copy-done.4, ...), custom_call_target="tpu_custom_call" | custom-call | flops 5242880 | bytes 6291456 | tf_op jit(solution)/shard_map/edge_terms/pallas_call | solution.py:547
  86.6 2.9 %collective-permute-start.5 = (f32[8,2,16,512]{3,2,1,0:T(8,128)S(1)}, f32[8,2,16,512]{3,2,1,0:T(8,128)S(1)}, u32[]{:S(2)}, u32[]{:S(2)}) collective-permute-start(f32[8,2,16,512]{3,2,1,0:T(8,128)S(1)} %get-tuple-element.30), channel_id=1, source_target_pairs={{0,12},{1,13},{2,14},{3,15},{4,8},{5,9},{6,10},{7,11},{8,4},{9,5},... | collective-permute-start | bytes 1572872 | tf_op jit(solution)/shard_map/ppermute | solution.py:496
  89.5 0.8 collective-permute-start.6
  90.3 3.0 %collective-permute-start.7 = (f32[32,2,16,128]{3,2,1,0:T(8,128)S(1)}, f32[32,2,16,128]{3,2,1,0:T(8,128)S(1)}, u32[]{:S(2)}, u32[]{:S(2)}) collective-permute-start(f32[32,2,16,128]{3,2,1,0:T(8,128)S(1)} %get-tuple-element.32), channel_id=1, source_target_pairs={{0,3},{1,2},{2,1},{3,0},{4,7},{5,6},{6,5},{7,4},{8,11},{9,10},{10,... | collective-permute-start | bytes 1572872 | tf_op jit(solution)/shard_map/ppermute | solution.py:498
  93.4 3.5 %collective-permute-start.9 = (f32[8,2,16,128]{3,2,1,0:T(8,128)S(1)}, f32[8,2,16,128]{3,2,1,0:T(8,128)S(1)}, u32[]{:S(2)}, u32[]{:S(2)}) collective-permute-start(f32[8,2,16,128]{3,2,1,0:T(8,128)S(1)} %get-tuple-element.34), channel_id=1, source_target_pairs={{0,15},{1,14},{4,11},{5,10},{16,31},{17,30},{20,27},{21,26},{32,47... | collective-permute-start | bytes 393224 | tf_op jit(solution)/shard_map/ppermute | solution.py:500
  96.9 1.6 copy-done.10
  98.4 8.5 %local_terms.4.refs_0_ = f32[32,2,16,512]{3,2,1,0:T(8,128)S(1)} custom-call(f32[32,2,16,512]{3,2,1,0:T(8,128)S(1)} %copy-done.10, f32[32,2,16,512]{3,2,1,0:T(8,128)} %bitcast.18, f32[1,4]{1,0:T(1,128)S(1)} %bitcast.26, f32[1,4]{1,0:T(1,128)S(1)} %bitcast.37, f32[1,4]{1,0:T(1,128)S(1)} %bitcast.40, f32[1,4]{1,0:T(1,128)S(1)} %bitcast.32, ...), custom_call_target="tpu_custom_call" | custom-call | flops 31457280 | bytes 6291456 | tf_op jit(solution)/shard_map/local_terms/pallas_call | solution.py:524
  107.0 1.3 copy-done.3
  108.3 7.1 %edge_terms.4 = (f32[32,2,16,512]{3,2,1,0:T(8,128)}, f32[8,2,16,512]{3,2,1,0:T(8,128)}, f32[16,2,8,512]{3,2,1,0:T(8,128)}, f32[32,2,16,128]{3,2,1,0:T(8,128)S(1)...) custom-call(f32[32,2,16,512]{3,2,1,0:T(8,128)} %copy-done.3, ...), custom_call_target="tpu_custom_call" | custom-call | flops 5242880 | bytes 6291456 | tf_op jit(solution)/shard_map/edge_terms/pallas_call | solution.py:547
  115.4 2.3 %collective-permute-start.12 = (f32[32,2,16,128]{3,2,1,0:T(8,128)S(1)}, f32[32,2,16,128]{3,2,1,0:T(8,128)S(1)}, u32[]{:S(2)}, u32[]{:S(2)}) collective-permute-start(f32[32,2,16,128]{3,2,1,0:T(8,128)S(1)} %get-tuple-element.39), channel_id=1, source_target_pairs={{0,3},{1,2},{2,1},{3,0},{4,7},{5,6},{6,5},{7,4},{8,11},{9,10},{10,... | collective-permute-start | bytes 1572872 | tf_op jit(solution)/shard_map/ppermute | solution.py:498
  117.7 4.6 %collective-permute-start.14 = (f32[8,2,16,128]{3,2,1,0:T(8,128)S(1)}, f32[8,2,16,128]{3,2,1,0:T(8,128)S(1)}, u32[]{:S(2)}, u32[]{:S(2)}) collective-permute-start(f32[8,2,16,128]{3,2,1,0:T(8,128)S(1)} %get-tuple-element.41), channel_id=1, source_target_pairs={{0,15},{1,14},{4,11},{5,10},{16,31},{17,30},{20,27},{21,26},{32,47... | collective-permute-start | bytes 393224 | tf_op jit(solution)/shard_map/ppermute | solution.py:500
  122.4 1.6 copy-done.8
  124.0 9.4 %local_terms.5 = (f32[32,2,16,512]{3,2,1,0:T(8,128)S(1)}, f32[4,16,128]{2,1,0:T(8,128)S(1)}) custom-call(f32[32,2,16,512]{3,2,1,0:T(8,128)S(1)} %copy-done.8, f32[32,2,16,512]{3,2,1,0:T(8,128)} %bitcast.19, f32[32,2,16,512]{3,2,1,0:T(8,128)} %bitcast.9.refs_2_.refs_6_, f32[1,4]{1,0:T(1,128)S(1)} %bitcast.28, f32[1,4]{1,0:T(1,128)S(1)} %bitcast.38, ...), custom_call_target="tpu_custom_call" | custom-call | flops 31457280 | bytes 6291456 | tf_op jit(solution)/shard_map/local_terms/pallas_call | solution.py:524
  133.4 1.3 copy-done.9
  134.7 4.8 %edge_terms.5 = (f32[32,2,16,512]{3,2,1,0:T(8,128)S(1)}, f32[8,128]{1,0:T(8,128)S(1)}) custom-call(f32[32,2,16,512]{3,2,1,0:T(8,128)} %copy-done.9, f32[8,2,16,512]{3,2,1,0:T(8,128)S(1)} %collective-permute-done.10.refs_1_, f32[16,2,8,512]{3,2,1,0:T(8,128)S(1)} %collective-permute-done.11.refs_2_, f32[32,2,16,128]{3,2,1,0:T(8,128)S(1)} %collective-permute-done.12.refs_3_, ...), custom_call_target="tpu_custom_call" | custom-call | flops 5242880 | bytes 6291456 | tf_op jit(solution)/shard_map/edge_terms/pallas_call | solution.py:547
  139.6 25.3 %all_to_all.15.refs_0_ = f32[8,4,2,16,512]{4,3,2,1,0:T(8,128)S(1)} all-to-all(f32[8,4,2,16,512]{4,3,2,1,0:T(8,128)S(1)} %bitcast.23), channel_id=1, replica_groups={{0,1,3,2,4,5,7,6},{14,15,13,12,10,11,9,8},{16,17,19,18,20,21,23,22},{30..., dimensions={0} | all-to-all | bytes 4194304 | tf_op jit(solution)/shard_map/all_to_all | solution.py:490
  164.9 6.9 %collective-permute-start.15 = (f32[8,4,2,16,512]{4,3,2,1,0:T(8,128)S(1)}, f32[8,4,2,16,512]{4,3,2,1,0:T(8,128)S(1)}, u32[]{:S(2)}, u32[]{:S(2)}) collective-permute-start(f32[8,4,2,16,512]{4,3,2,1,0:T(8,128)S(1)} %all_to_all.15.refs_0_), channel_id=1, source_target_pairs={{16,0},{32,16},{48,32},{64,48},{80,64},{96,80},{112,96},{17,1},{33... | collective-permute-start | bytes 6291464 | tf_op jit(solution)/shard_map/ppermute | solution.py:588
  171.8 0.1 collective-permute-start.16
  171.9 3.8 %collective-permute-done.16 = f32[8,128]{1,0:T(8,128)S(1)} collective-permute-done((f32[8,128]{1,0:T(8,128)S(1)}, f32[8,128]{1,0:T(8,128)S(1)}, u32[]{:S(2)}, u32[]{:S(2)}) %collective-permute-start.16) | collective-permute-done | bytes 4128 | tf_op jit(solution)/shard_map/ppermute | solution.py:587
  175.7 2.5 %collective-permute-done.17 = f32[8,128]{1,0:T(8,128)S(1)} collective-permute-done((f32[8,128]{1,0:T(8,128)S(1)}, f32[8,128]{1,0:T(8,128)S(1)}, u32[]{:S(2)}, u32[]{:S(2)}) %collective-permute-start.17) | collective-permute-done | bytes 4128 | tf_op jit(solution)/shard_map/ppermute | solution.py:587
  178.2 0.9 collective-permute-start.18
  179.1 2.8 %collective-permute-done.18 = f32[8,128]{1,0:T(8,128)S(1)} collective-permute-done((f32[8,128]{1,0:T(8,128)S(1)}, f32[8,128]{1,0:T(8,128)S(1)}, u32[]{:S(2)}, u32[]{:S(2)}) %collective-permute-start.18) | collective-permute-done | bytes 4128 | tf_op jit(solution)/shard_map/ppermute | solution.py:587
  181.8 2.5 %collective-permute-done.19 = f32[8,128]{1,0:T(8,128)S(1)} collective-permute-done((f32[8,128]{1,0:T(8,128)S(1)}, f32[8,128]{1,0:T(8,128)S(1)}, u32[]{:S(2)}, u32[]{:S(2)}) %collective-permute-start.19) | collective-permute-done | bytes 4128 | tf_op jit(solution)/shard_map/ppermute | solution.py:587
  184.3 0.1 slice_reduce_fusion
  184.4 0.5 multiply_bitcast_fusion
  184.9 2.0 unpack_blocks.2
  186.9 9.7 %collective-permute-done.15.refs_0_ = f32[8,4,2,16,512]{4,3,2,1,0:T(8,128)S(1)} collective-permute-done((f32[8,4,2,16,512]{4,3,2,1,0:T(8,128)S(1)}, f32[8,4,2,16,512]{4,3,2,1,0:T(8,128)S(1)}, u32[]{:S(2)}, u32[]{:S(2)}) %collective-permute-start.15) | collective-permute-done | bytes 2097184 | tf_op jit(solution)/shard_map/ppermute | solution.py:588
  196.6 2.1 %unpack_blocks.3 = f32[2,128,2048]{2,1,0:T(8,128)} custom-call(f32[8,4,2,16,512]{4,3,2,1,0:T(8,128)S(1)} %collective-permute-done.15.refs_0_, f32[2,128,2048]{2,1,0:T(8,128)S(1)} %bitcast.21), custom_call_target="tpu_custom_call" | custom-call | bytes 4194304 | tf_op jit(solution)/shard_map/unpack_blocks/pallas_call | solution.py:477
  (50 shorter events, 0.1 us)
Async XLA Ops:
  0.6 1.6 copy-start.1
  2.8 1.3 copy-start.6
  4.1 33.4 %all-to-all-start = ((f32[8,4,2,16,512]{4,3,2,1,0:T(8,128)}), f32[8,4,2,16,512]{4,3,2,1,0:T(8,128)S(1)}, u32[]{:S(2)}, u32[]{:S(2)}) async-start(f32[8,4,2,16,512]{4,3,2,1,0:T(8,128)} %copy-done.6), calls=%async_computation | async-start | bytes 4194304 | tf_op jit(solution)/shard_map/all_to_all | solution.py:490
  11.0 1.6 copy-start.7
  13.1 1.4 copy-start.5
  37.5 16.3 %copy-start = (f32[8,4,2,16,512]{4,3,2,1,0:T(8,128)}, f32[8,4,2,16,512]{4,3,2,1,0:T(8,128)S(1)}, u32[]{:S(2)}) copy-start(f32[8,4,2,16,512]{4,3,2,1,0:T(8,128)S(1)} %all-to-all-done) | copy-start | bytes 6291460
  37.5 84.9 %all-to-all-start.1 = ((f32[8,4,2,16,512]{4,3,2,1,0:T(8,128)}), f32[8,4,2,16,512]{4,3,2,1,0:T(8,128)}, u32[]{:S(2)}, u32[]{:S(2)}) async-start(f32[8,4,2,16,512]{4,3,2,1,0:T(8,128)} %copy-done.5), calls=%async_computation.1 | async-start | bytes 4194304 | tf_op jit(solution)/shard_map/all_to_all | solution.py:490
  43.2 10.6 %copy-start.11 = (f32[1,1,4]{2,1,0:T(1,128)S(1)}, f32[1,1,4]{2,1,0:T(1,128)}, u32[]{:S(2)}) copy-start(f32[1,1,4]{2,1,0:T(1,128)} %param.11) | copy-start | bytes 52
  43.2 10.6 %copy-start.12 = (f32[4]{0:T(128)S(1)}, f32[4]{0:T(128)}, u32[]{:S(2)}) copy-start(f32[4]{0:T(128)} %param.14) | copy-start | bytes 52
  43.3 10.6 %copy-start.13 = (f32[1,16]{1,0:T(1,128)S(1)}, f32[1,16]{1,0:T(1,128)}, u32[]{:S(2)}) copy-start(f32[1,16]{1,0:T(1,128)} %constant.11.refs_8_.refs_9_.refs_10_) | copy-start | bytes 196
  43.3 10.6 %copy-start.14 = (f32[4]{0:T(128)S(1)}, f32[4]{0:T(128)}, u32[]{:S(2)}) copy-start(f32[4]{0:T(128)} %param.12) | copy-start | bytes 52
  43.3 10.6 %copy-start.15 = (f32[4]{0:T(128)S(1)}, f32[4]{0:T(128)}, u32[]{:S(2)}) copy-start(f32[4]{0:T(128)} %param.13) | copy-start | bytes 52
  43.3 10.6 %copy-start.16 = (f32[4]{0:T(128)S(1)}, f32[4]{0:T(128)}, u32[]{:S(2)}) copy-start(f32[4]{0:T(128)} %param.15) | copy-start | bytes 52
  43.3 10.6 %copy-start.17 = (f32[6]{0:T(128)S(1)}, f32[6]{0:T(128)}, u32[]{:S(2)}) copy-start(f32[6]{0:T(128)} %param.16) | copy-start | bytes 76
  45.3 17.5 %collective-permute-start = (f32[8,2,16,512]{3,2,1,0:T(8,128)S(1)}, f32[8,2,16,512]{3,2,1,0:T(8,128)S(1)}, u32[]{:S(2)}, u32[]{:S(2)}) collective-permute-start(f32[8,2,16,512]{3,2,1,0:T(8,128)S(1)} %get-tuple-element.24), channel_id=1, source_target_pairs={{0,12},{1,13},{2,14},{3,15},{4,8},{5,9},{6,10},{7,11},{8,4},{9,5},... | collective-permute-start | bytes 1572872 | tf_op jit(solution)/shard_map/ppermute | solution.py:496
  48.3 30.5 %collective-permute-start.1 = (f32[16,2,8,512]{3,2,1,0:T(8,128)S(1)}, f32[16,2,8,512]{3,2,1,0:T(8,128)S(1)}, u32[]{:S(2)}, u32[]{:S(2)}) collective-permute-start(f32[16,2,8,512]{3,2,1,0:T(8,128)S(1)} %get-tuple-element.25), channel_id=1, source_target_pairs={{0,4},{1,5},{2,6},{3,7},{4,0},{5,1},{6,2},{7,3},{8,12},{9,13},{10,... | collective-permute-start | bytes 1572872 | tf_op jit(solution)/shard_map/ppermute | solution.py:497
  48.8 31.1 %collective-permute-start.2 = (f32[32,2,16,128]{3,2,1,0:T(8,128)S(1)}, f32[32,2,16,128]{3,2,1,0:T(8,128)S(1)}, u32[]{:S(2)}, u32[]{:S(2)}) collective-permute-start(f32[32,2,16,128]{3,2,1,0:T(8,128)S(1)} %get-tuple-element.26), channel_id=1, source_target_pairs={{0,3},{1,2},{2,1},{3,0},{4,7},{5,6},{6,5},{7,4},{8,11},{9,10},{10,... | collective-permute-start | bytes 1572872 | tf_op jit(solution)/shard_map/ppermute | solution.py:498
  49.3 30.6 %collective-permute-start.3 = (f32[32,2,16,128]{3,2,1,0:T(8,128)S(1)}, f32[32,2,16,128]{3,2,1,0:T(8,128)S(1)}, u32[]{:S(2)}, u32[]{:S(2)}) collective-permute-start(f32[32,2,16,128]{3,2,1,0:T(8,128)S(1)} %get-tuple-element.27), channel_id=1, source_target_pairs={{0,1},{1,0},{2,3},{3,2},{4,5},{5,4},{6,7},{7,6},{8,9},{9,8},{10,11... | collective-permute-start | bytes 1572872 | tf_op jit(solution)/shard_map/ppermute | solution.py:499
  49.3 13.5 %collective-permute-start.4 = (f32[8,2,16,128]{3,2,1,0:T(8,128)S(1)}, f32[8,2,16,128]{3,2,1,0:T(8,128)S(1)}, u32[]{:S(2)}, u32[]{:S(2)}) collective-permute-start(f32[8,2,16,128]{3,2,1,0:T(8,128)S(1)} %get-tuple-element.28), channel_id=1, source_target_pairs={{0,15},{1,14},{4,11},{5,10},{16,31},{17,30},{20,27},{21,26},{32,47... | collective-permute-start | bytes 393224 | tf_op jit(solution)/shard_map/ppermute | solution.py:500
  61.4 1.3 copy-start.4
  86.6 21.7 %collective-permute-start.5 = (f32[8,2,16,512]{3,2,1,0:T(8,128)S(1)}, f32[8,2,16,512]{3,2,1,0:T(8,128)S(1)}, u32[]{:S(2)}, u32[]{:S(2)}) collective-permute-start(f32[8,2,16,512]{3,2,1,0:T(8,128)S(1)} %get-tuple-element.30), channel_id=1, source_target_pairs={{0,12},{1,13},{2,14},{3,15},{4,8},{5,9},{6,10},{7,11},{8,4},{9,5},... | collective-permute-start | bytes 1572872 | tf_op jit(solution)/shard_map/ppermute | solution.py:496
  89.5 18.8 %collective-permute-start.6 = (f32[16,2,8,512]{3,2,1,0:T(8,128)S(1)}, f32[16,2,8,512]{3,2,1,0:T(8,128)S(1)}, u32[]{:S(2)}, u32[]{:S(2)}) collective-permute-start(f32[16,2,8,512]{3,2,1,0:T(8,128)S(1)} %get-tuple-element.31), channel_id=1, source_target_pairs={{0,4},{1,5},{2,6},{3,7},{4,0},{5,1},{6,2},{7,3},{8,12},{9,13},{10,... | collective-permute-start | bytes 1572872 | tf_op jit(solution)/shard_map/ppermute | solution.py:497
  90.3 18.0 %collective-permute-start.7 = (f32[32,2,16,128]{3,2,1,0:T(8,128)S(1)}, f32[32,2,16,128]{3,2,1,0:T(8,128)S(1)}, u32[]{:S(2)}, u32[]{:S(2)}) collective-permute-start(f32[32,2,16,128]{3,2,1,0:T(8,128)S(1)} %get-tuple-element.32), channel_id=1, source_target_pairs={{0,3},{1,2},{2,1},{3,0},{4,7},{5,6},{6,5},{7,4},{8,11},{9,10},{10,... | collective-permute-start | bytes 1572872 | tf_op jit(solution)/shard_map/ppermute | solution.py:498
  93.4 14.9 %collective-permute-start.8 = (f32[32,2,16,128]{3,2,1,0:T(8,128)S(1)}, f32[32,2,16,128]{3,2,1,0:T(8,128)S(1)}, u32[]{:S(2)}, u32[]{:S(2)}) collective-permute-start(f32[32,2,16,128]{3,2,1,0:T(8,128)S(1)} %get-tuple-element.33), channel_id=1, source_target_pairs={{0,1},{1,0},{2,3},{3,2},{4,5},{5,4},{6,7},{7,6},{8,9},{9,8},{10,11... | collective-permute-start | bytes 1572872 | tf_op jit(solution)/shard_map/ppermute | solution.py:499
  93.4 14.9 %collective-permute-start.9 = (f32[8,2,16,128]{3,2,1,0:T(8,128)S(1)}, f32[8,2,16,128]{3,2,1,0:T(8,128)S(1)}, u32[]{:S(2)}, u32[]{:S(2)}) collective-permute-start(f32[8,2,16,128]{3,2,1,0:T(8,128)S(1)} %get-tuple-element.34), channel_id=1, source_target_pairs={{0,15},{1,14},{4,11},{5,10},{16,31},{17,30},{20,27},{21,26},{32,47... | collective-permute-start | bytes 393224 | tf_op jit(solution)/shard_map/ppermute | solution.py:500
  96.8 1.6 copy-start.10
  107.0 1.3 copy-start.3
  115.4 19.3 %collective-permute-start.10 = (f32[8,2,16,512]{3,2,1,0:T(8,128)}, f32[8,2,16,512]{3,2,1,0:T(8,128)S(1)}, u32[]{:S(2)}, u32[]{:S(2)}) collective-permute-start(f32[8,2,16,512]{3,2,1,0:T(8,128)} %get-tuple-element.37), channel_id=1, source_target_pairs={{0,12},{1,13},{2,14},{3,15},{4,8},{5,9},{6,10},{7,11},{8,4},{9,5},... | collective-permute-start | bytes 1572872 | tf_op jit(solution)/shard_map/ppermute | solution.py:496
  115.4 19.3 %collective-permute-start.11 = (f32[16,2,8,512]{3,2,1,0:T(8,128)}, f32[16,2,8,512]{3,2,1,0:T(8,128)S(1)}, u32[]{:S(2)}, u32[]{:S(2)}) collective-permute-start(f32[16,2,8,512]{3,2,1,0:T(8,128)} %get-tuple-element.38), channel_id=1, source_target_pairs={{0,4},{1,5},{2,6},{3,7},{4,0},{5,1},{6,2},{7,3},{8,12},{9,13},{10,... | collective-permute-start | bytes 1572872 | tf_op jit(solution)/shard_map/ppermute | solution.py:497
  115.4 19.3 %collective-permute-start.12 = (f32[32,2,16,128]{3,2,1,0:T(8,128)S(1)}, f32[32,2,16,128]{3,2,1,0:T(8,128)S(1)}, u32[]{:S(2)}, u32[]{:S(2)}) collective-permute-start(f32[32,2,16,128]{3,2,1,0:T(8,128)S(1)} %get-tuple-element.39), channel_id=1, source_target_pairs={{0,3},{1,2},{2,1},{3,0},{4,7},{5,6},{6,5},{7,4},{8,11},{9,10},{10,... | collective-permute-start | bytes 1572872 | tf_op jit(solution)/shard_map/ppermute | solution.py:498
  117.7 17.0 %collective-permute-start.13 = (f32[32,2,16,128]{3,2,1,0:T(8,128)S(1)}, f32[32,2,16,128]{3,2,1,0:T(8,128)S(1)}, u32[]{:S(2)}, u32[]{:S(2)}) collective-permute-start(f32[32,2,16,128]{3,2,1,0:T(8,128)S(1)} %get-tuple-element.40), channel_id=1, source_target_pairs={{0,1},{1,0},{2,3},{3,2},{4,5},{5,4},{6,7},{7,6},{8,9},{9,8},{10,11... | collective-permute-start | bytes 1572872 | tf_op jit(solution)/shard_map/ppermute | solution.py:499
  117.7 17.0 %collective-permute-start.14 = (f32[8,2,16,128]{3,2,1,0:T(8,128)S(1)}, f32[8,2,16,128]{3,2,1,0:T(8,128)S(1)}, u32[]{:S(2)}, u32[]{:S(2)}) collective-permute-start(f32[8,2,16,128]{3,2,1,0:T(8,128)S(1)} %get-tuple-element.41), channel_id=1, source_target_pairs={{0,15},{1,14},{4,11},{5,10},{16,31},{17,30},{20,27},{21,26},{32,47... | collective-permute-start | bytes 393224 | tf_op jit(solution)/shard_map/ppermute | solution.py:500
  122.4 1.6 copy-start.8
  133.4 1.3 copy-start.9
  164.9 31.7 %collective-permute-start.15 = (f32[8,4,2,16,512]{4,3,2,1,0:T(8,128)S(1)}, f32[8,4,2,16,512]{4,3,2,1,0:T(8,128)S(1)}, u32[]{:S(2)}, u32[]{:S(2)}) collective-permute-start(f32[8,4,2,16,512]{4,3,2,1,0:T(8,128)S(1)} %all_to_all.15.refs_0_), channel_id=1, source_target_pairs={{16,0},{32,16},{48,32},{64,48},{80,64},{96,80},{112,96},{17,1},{33... | collective-permute-start | bytes 6291464 | tf_op jit(solution)/shard_map/ppermute | solution.py:588
  171.8 3.9 %collective-permute-start.16 = (f32[8,128]{1,0:T(8,128)S(1)}, f32[8,128]{1,0:T(8,128)S(1)}, u32[]{:S(2)}, u32[]{:S(2)}) collective-permute-start(f32[8,128]{1,0:T(8,128)S(1)} %get-tuple-element.44), channel_id=1, source_target_pairs={{0,12},{1,13},{2,14},{3,15},{4,8},{5,9},{6,10},{7,11},{8,4},{9,5},... | collective-permute-start | bytes 12296 | tf_op jit(solution)/shard_map/ppermute | solution.py:587
  175.7 2.5 %collective-permute-start.17 = (f32[8,128]{1,0:T(8,128)S(1)}, f32[8,128]{1,0:T(8,128)S(1)}, u32[]{:S(2)}, u32[]{:S(2)}) collective-permute-start(f32[8,128]{1,0:T(8,128)S(1)} %add.12), channel_id=1, source_target_pairs={{0,4},{1,5},{2,6},{3,7},{4,0},{5,1},{6,2},{7,3},{8,12},{9,13},{10,... | collective-permute-start | bytes 12296 | tf_op jit(solution)/shard_map/ppermute | solution.py:587
  178.2 3.7 %collective-permute-start.18 = (f32[8,128]{1,0:T(8,128)S(1)}, f32[8,128]{1,0:T(8,128)S(1)}, u32[]{:S(2)}, u32[]{:S(2)}) collective-permute-start(f32[8,128]{1,0:T(8,128)S(1)} %add.13), channel_id=1, source_target_pairs={{0,3},{1,2},{2,1},{3,0},{4,7},{5,6},{6,5},{7,4},{8,11},{9,10},{10,... | collective-permute-start | bytes 12296 | tf_op jit(solution)/shard_map/ppermute | solution.py:587
  181.8 2.5 %collective-permute-start.19 = (f32[8,128]{1,0:T(8,128)S(1)}, f32[8,128]{1,0:T(8,128)S(1)}, u32[]{:S(2)}, u32[]{:S(2)}) collective-permute-start(f32[8,128]{1,0:T(8,128)S(1)} %add.14), channel_id=1, source_target_pairs={{0,1},{1,0},{2,3},{3,2},{4,5},{5,4},{6,7},{7,6},{8,9},{9,8},{10,11... | collective-permute-start | bytes 12296 | tf_op jit(solution)/shard_map/ppermute | solution.py:587
  184.9 11.7 %copy-start.2 = (f32[1,2,128,2048]{3,2,1,0:T(8,128)S(1)}, f32[1,2,128,2048]{3,2,1,0:T(8,128)}, u32[]{:S(2)}) copy-start(f32[1,2,128,2048]{3,2,1,0:T(8,128)} %param.9) | copy-start | bytes 6291460
where the time goes:
time: 199 us
  waiting for transfers between devices  61.3 us (31%)
  Pallas kernels  51.2 us (26%)
  starting transfers between devices  46.2 us (23%)
  blocking collectives  25.3 us (13%)
  local copies, waits for them, and re-layouts  13 us (7%)
    pallas_call x3, Pallas kernels, local_terms(): pl.pallas_call(kernel, out_shape=outs, in_specs=[VMEM] * (3 if grad else...  25.5 us
    all_to_all x1, blocking collectives, regroup(): return lax.all_to_all(x, 'row', 0, 0, axis_index_groups=GROUPS, tiled=True)  25.3 us
    all_to_all x2, waiting for transfers between devices, regroup(): return lax.all_to_all(x, 'row', 0, 0, axis_index_groups=GROUPS, tiled=True)  22.9 us
    pallas_call x3, Pallas kernels, edge_terms(): pl.pallas_call(kernel, out_shape=outs, in_specs=[VMEM] * (len(args) - len...  18.6 us
    ppermute x3, waiting for transfers between devices, exchange(): lax.ppermute(s_i2, 'row', PERM_I2)  16 us
    unnamed x36, local copies, waits for them, and re-layouts  13 us
    all_to_all x2, starting transfers between devices, regroup(): return lax.all_to_all(x, 'row', 0, 0, axis_index_groups=GROUPS, tiled=True)  12.6 us
    ppermute x3, starting transfers between devices, exchange(): lax.ppermute(s_c, 'row', PERM_CORNER)  12.6 us
  transfers between devices with their start and end apart: 22, of which 8 were waited for; matrix products, arithmetic and copies ran while one was open for 0% of the time, Pallas kernels for 22%

commit v1 on v0

v1 whole, which is shorter than its diff:
```python
import jax
import jax.numpy as jnp
import numpy as np
from jax import lax
from jax.experimental import pallas as pl
from jax.experimental.pallas import tpu as pltpu
from jax.sharding import PartitionSpec as P


ORDER = 2048
STEP = 0.01
UNITS = 32
ROWS = 16
LANES = 128
TILES = 4
WIDTH = TILES * LANES
F32 = jnp.float32

GROUPS = [
    [4 * y + z for y in (0, 1) for z in (0, 1, 3, 2)],
    [4 * y + z for y in (3, 2) for z in (2, 3, 1, 0)],
]
Y_OUTER = {0: 3, 3: 0, 1: 2, 2: 1}
Y_INNER = {0: 1, 1: 0, 2: 3, 3: 2}


def pairs_y(flip):
    return [(4 * y + z, 4 * flip[y] + z) for y in range(4) for z in range(4)]


def pairs_z(flip):
    return [(4 * y + z, 4 * y + flip[z]) for y in range(4) for z in range(4)]


PERM_I0 = pairs_y(Y_OUTER)
PERM_I2 = pairs_y(Y_INNER)
PERM_J0 = pairs_z(Y_OUTER)
PERM_J1 = pairs_z(Y_INNER)
PERM_CORNER = [(4 * y + z, 4 * Y_OUTER[y] + Y_OUTER[z]) for y in (0, 1) for z in (0, 1)]
ROOTS = np.sqrt(np.arange(16)).astype(np.float32)


class Place:
    def __init__(self):
        row = lax.axis_index("row")
        y = row // 4
        z = row % 4
        self.upper = y // 2
        self.gi2 = jnp.where((y == 1) | (y == 2), 1, 0)
        self.gj0 = z // 2
        self.gj1 = jnp.where((z == 1) | (z == 2), 1, 0)
        gray = z ^ (z // 2)
        self.slot = jnp.where(self.upper == 1, 4 * (3 - y) + 3 - gray, 4 * y + gray)


def unit_at(p, i1):
    h = i1 // 4
    odd = p % 2
    return ((p // 2) * 4 + jnp.where(odd == 1, 3 - h, h)) * 4 + i1 % 4


def iotas():
    lane = lax.broadcasted_iota(jnp.int32, (ROWS, LANES), 1)
    sub = lax.broadcasted_iota(jnp.int32, (ROWS, LANES), 0)
    return lane, sub


class Tables:
    def __init__(self, place):
        lane, sub = iotas()
        low1 = lane // 32
        self.j1 = (low1 + 4 * place.gj1).astype(F32)
        self.j2 = ((lane // 4) % 8).astype(F32)
        self.j3 = (lane % 4).astype(F32)
        low2 = sub // 4
        self.i2 = (low2 + 4 * place.gi2).astype(F32)
        self.i3 = (sub % 4).astype(F32)
        self.c1p = jnp.where(low1 > 0, jnp.sqrt(self.j1), 0.0)
        self.c1m = jnp.where(low1 < 3, jnp.sqrt(self.j1 + 1.0), 0.0)
        self.c2p = jnp.sqrt(self.j2)
        self.c2m = jnp.where(self.j2 < 7.0, jnp.sqrt(self.j2 + 1.0), 0.0)
        self.c3p = jnp.sqrt(self.j3)
        self.c3m = jnp.where(self.j3 < 3.0, jnp.sqrt(self.j3 + 1.0), 0.0)
        self.r2p = jnp.where(low2 > 0, jnp.sqrt(self.i2), 0.0)
        self.r2m = jnp.where(low2 < 3, jnp.sqrt(self.i2 + 1.0), 0.0)
        self.r3p = jnp.sqrt(self.i3)
        self.r3m = jnp.where(self.i3 < 3.0, jnp.sqrt(self.i3 + 1.0), 0.0)
        edge1 = jnp.where(place.gj1 == 1, 0, 3)
        edge2 = jnp.where(place.gi2 == 1, 0, 3)
        self.edge1 = edge1
        self.at1 = (low1 == edge1).astype(F32)
        self.at2 = (low2 == edge2).astype(F32)


def drift(levels, detuning, anharmonicity, cross_kerr):
    total = 0.0
    for q in range(4):
        n = levels[q]
        total = total + detuning[q] * n - 0.5 * anharmonicity[q] * n * (n - 1.0)
    k = 0
    for a in range(4):
        for b in range(a + 1, 4):
            total = total - cross_kerr[k] * levels[a] * levels[b]
            k += 1
    return total


def decay_part(levels, decay, dephasing):
    total = 0.0
    for q in range(4):
        n = levels[q]
        total = total - 0.5 * decay[q] * n - 0.5 * dephasing[q] * n * n
    return total


def tile(ref, unit, c, t):
    return ref[unit, c, :, t * LANES : (t + 1) * LANES]


def level_of(place, p):
    return jnp.where(place.upper == 1, 7 - p, p)


def unit_neighbours(place, roots, p, i1):
    up = place.upper == 1
    i0 = level_of(place, p)
    below = jnp.where(up, p + 1, p - 1)
    above = jnp.where(up, p - 1, p + 1)
    root_below = jnp.where((below >= 0) & (below <= 3), roots[0, i0], 0.0)
    root_above = jnp.where((above >= 0) & (above <= 3), roots[0, i0 + 1], 0.0)
    return (
        i0,
        (unit_at(jnp.clip(below, 0, 3), i1), root_below),
        (unit_at(jnp.clip(above, 0, 3), i1), root_above),
        (unit_at(p, jnp.maximum(i1 - 1, 0)), roots[0, i1]),
        (unit_at(p, jnp.minimum(i1 + 1, 7)), jnp.where(i1 < 7, roots[0, i1 + 1], 0.0)),
    )


def local_kernel(scale, n, *refs):
    z, base = refs[:2]
    if n:
        state, *received = refs[2:6]
        *scalars, out, next_state = refs[6:15] if n == 1 else (*refs[6:14], refs[16])
        copy_state(n - 1, state, received, next_state, lambda r: r)
    else:
        *scalars, out = refs[2:]
    writes = []
    if n == 2:
        z_out, state_out = refs[14:16]
        sems = refs[17]
        writes = [
            pltpu.make_async_copy(z, z_out, sems.at[0]),
            pltpu.make_async_copy(next_state, state_out, sems.at[1]),
        ]
    start_all(writes)
    amp, det, anh, dec, dep, kerr, roots = scalars
    place = Place()
    tb = Tables(place)
    detuning = [det[0, q] for q in range(4)]
    anharm = [anh[0, q] for q in range(4)]
    decay = [dec[0, q] for q in range(4)]
    dephasing = [dep[0, q] for q in range(4)]
    cross = [kerr[0, k] for k in range(6)]
    u = [amp[0, q] for q in range(4)]
    column_energy = []
    column_decay = []
    for t in range(TILES):
        j0 = (4 * place.gj0 + t).astype(F32)
        levels = [j0, tb.j1, tb.j2, tb.j3]
        column_energy.append(drift(levels, detuning, anharm, cross))
        column_decay.append(decay_part(levels, decay, dephasing))
    cross2 = dephasing[2] * tb.i2
    cross3 = dephasing[3] * tb.i3
    c1m, c2m, c3m = u[1] * tb.c1m, u[2] * tb.c2m, u[3] * tb.c3m
    c1p, c2p, c3p = u[1] * tb.c1p, u[2] * tb.c2p, u[3] * tb.c3p
    r2m, r3m = u[2] * tb.r2m, u[3] * tb.r3m
    r2p, r3p = u[2] * tb.r2p, u[3] * tb.r3p
    d2p, d3p = decay[2] * tb.r2p, decay[3] * tb.r3p

    def step(n, carry):
        p = n // 8
        i1 = n % 8
        here = unit_at(p, i1)
        i0, below, above, less, more = unit_neighbours(place, roots, p, i1)
        i0f = i0.astype(F32)
        i1f = i1.astype(F32)
        rows = [i0f, i1f, tb.i2, tb.i3]
        row_energy = drift(rows, detuning, anharm, cross)
        row_decay = decay_part(rows, decay, dephasing)
        d1p = (decay[1] * less[1]) * tb.c1p
        for t in range(TILES):
            j0 = 4 * place.gj0 + t
            root_left = roots[0, j0]
            root_right = roots[0, j0 + 1]
            comm = []
            sand = []
            values = []
            for c in range(2):
                m = tile(z, here, c, t)
                values.append(m)
                turned2 = pltpu.roll(m, 4, 1)
                turned3 = pltpu.roll(m, 1, 1)
                row1 = tile(z, less[0], c, t)
                row0 = tile(z, below[0], c, t)
                k = (u[0] * below[1]) * row0 + (u[0] * above[1]) * tile(z, above[0], c, t)
                k = k + (u[1] * less[1]) * row1 + (u[1] * more[1]) * tile(z, more[0], c, t)
                if t > 0:
                    k = k - (u[0] * root_left) * tile(z, here, c, t - 1)
                if t < TILES - 1:
                    k = k - (u[0] * root_right) * tile(z, here, c, t + 1)
                k = k + r2p * pltpu.roll(m, 4, 0) + r2m * pltpu.roll(m, ROWS - 4, 0)
                k = k + r3p * pltpu.roll(m, 1, 0) + r3m * pltpu.roll(m, ROWS - 1, 0)
                k = k - c1p * pltpu.roll(m, 32, 1) - c1m * pltpu.roll(m, LANES - 32, 1)
                k = k - c2p * turned2 - c2m * pltpu.roll(m, LANES - 4, 1)
                k = k - c3p * turned3 - c3m * pltpu.roll(m, LANES - 1, 1)
                comm.append(k)
                s = (
                    d1p * pltpu.roll(row1, 32, 1)
                    + d2p * pltpu.roll(tb.c2p * turned2, 4, 0)
                    + d3p * pltpu.roll(tb.c3p * turned3, 1, 0)
                )
                if t > 0:
                    s = s + (decay[0] * below[1] * root_left) * tile(z, below[0], c, t - 1)
                sand.append(s)
            phase = row_energy - column_energy[t]
            damping = (
                row_decay
                + (column_decay[t] + (dephasing[0] * i0f) * j0.astype(F32))
                + (dephasing[1] * i1f) * tb.j1
                + cross2 * tb.j2
                + cross3 * tb.j3
            )
            x, y = values
            lanes = slice(t * LANES, (t + 1) * LANES)
            out[here, 0, :, lanes] = tile(base, here, 0, t) + scale * (
                damping * x - phase * y - comm[1] + sand[0]
            )
            out[here, 1, :, lanes] = tile(base, here, 1, t) + scale * (
                damping * y + phase * x + comm[0] + sand[1]
            )
        return carry

    lax.fori_loop(0, UNITS, step, 0)
    wait_all(writes)


PARTS = ((0, 1, 2), (3, 4, 5), (6, 7))
ROUTES = ((0, 1, 2), (2, 0, 1), (1, 2, 0))
EDGE = 64


def sent_slots(bit):
    return [r for r in range(8) if r >> bit & 1]


def merged_state(n, part, r):
    bit = ROUTES[n].index(part) if n >= 0 else 0
    if n < 0 or not r >> bit & 1:
        return None
    return bit, EDGE + sent_slots(bit).index(r) * len(PARTS[part]) * TILES


def state_entry(part, r):
    return (r * 8 + PARTS[part][0]) * TILES


def copy_state(n, state, received, out, slots):
    for r in range(8):
        for part in range(3):
            size = len(PARTS[part]) * TILES
            found = merged_state(n, part, r)
            source, first = (state, state_entry(part, r)) if found is None else (received[found[0]], found[1])
            out[pl.ds(state_entry(part, slots(r)), size)] = source[first : first + size]


def load_riders(n, state, received, carriers):
    for bit in range(3):
        part = ROUTES[n][bit]
        size = len(PARTS[part]) * TILES
        for at, r in enumerate(sent_slots(bit)):
            found = merged_state(n - 1, part, r)
            source, first = (state, state_entry(part, r)) if found is None else (received[found[0]], found[1])
            start = EDGE + at * size
            carriers[bit][start : start + size] = source[first : first + size]


def start_all(copies):
    for copy in copies:
        copy.start()


def wait_all(copies):
    for copy in copies:
        copy.wait()


def put_slabs(place, tb, p, pair, both, s_i0, s_j1, s_j0, s_i2, s_c):
    lane, _ = iotas()
    half = lax.broadcasted_iota(jnp.int32, (8, LANES), 0) < 4
    block = lane // 32
    gj0 = place.gj0 == 1
    gi2 = place.gi2 == 1
    for par in range(2):
        i1 = 2 * pair + par
        n = p * 8 + i1
        for c in range(2):
            tiles = both[par][c]
            if p == 3:
                for t in range(TILES):
                    s_i0[i1, c, :, t * LANES : (t + 1) * LANES] = tiles[t]
                s_c[i1, c] = tiles[TILES - 1]
            s_j0[2 * n + c] = jnp.where(gj0, tiles[0], tiles[TILES - 1])
            packed = None
            for t in range(TILES):
                turned = pltpu.roll(tiles[t], (32 * (t - tb.edge1)) % LANES, 1)
                packed = turned if packed is None else jnp.where(block == t, turned, packed)
            s_j1[2 * n + c] = packed
    for c in range(2):
        for t in range(TILES):
            even, odd = both[0][c][t], both[1][c][t]
            first = jnp.where(gi2, even[0:8], pltpu.roll(even[8:16], 4, 0))
            second = jnp.where(gi2, pltpu.roll(odd[0:8], 4, 0), odd[8:16])
            entry = ((p * 4 + pair) * 2 + c) * 2 + t // 2
            s_i2[entry, (t % 2) * 8 : (t % 2) * 8 + 8] = jnp.where(half, first, second)


def slab_kernel(z, state, s_i0, s_j1, s_j0, s_i2, s_c):
    place = Place()
    tb = Tables(place)
    load_riders(0, state, None, (s_j1, s_j0, s_i2))
    for p in range(4):

        def step(pair, carry, p=p):
            both = [
                [[tile(z, unit_at(p, 2 * pair + par), c, t) for t in range(TILES)] for c in range(2)]
                for par in range(2)
            ]
            put_slabs(place, tb, p, pair, both, s_i0, s_j1, s_j0, s_i2, s_c)
            return carry

        lax.fori_loop(0, 4, step, 0)


def i2_halo(place, h_i2, p, pair, par, c, t):
    small = h_i2[((p * 4 + pair) * 2 + c) * 2 + t // 2, (t % 2) * 8 : (t % 2) * 8 + 8]
    small = pltpu.roll(small, 4 * ((par + 1 + place.gi2) % 2), 0)
    return jnp.concatenate([small, small], axis=0)


def edge_kernel(scale, sent, *refs):
    last = sent is None
    part, h_i0, h_j1, h_j0, h_i2, h_c = refs[:6]
    if last:
        amp, dec, roots, out_all, out_rest, block, sems = refs[6:]
    else:
        state, amp, dec, roots, out, *slabs = refs[6:]
        load_riders(sent, state, (h_j1, h_j0, h_i2), slabs[1:4])
    place = Place()
    tb = Tables(place)
    up = place.upper == 1
    upf = place.upper.astype(F32)
    gj0f = place.gj0.astype(F32)
    gj1f = place.gj1.astype(F32)
    gi2f = place.gi2.astype(F32)
    copies = []
    decay = [scale * dec[0, q] for q in range(4)]
    u = [scale * amp[0, q] for q in range(4)]
    s1_base = (decay[1] * 2.0 * gj1f) * tb.at1
    s2_base = (decay[2] * 2.0 * gi2f) * tb.at2 * tb.c2p
    k1_mask = (-2.0 * u[1]) * tb.at1
    k2_mask = (2.0 * u[2]) * tb.at2

    def one(p, pair, par):
        i0 = jnp.where(up, 7 - p, p)
        below = jnp.where(up, p + 1, p - 1)
        below_in = (below >= 0) & (below <= 3)
        below = jnp.clip(below, 0, 3)
        root_below = jnp.where(below_in, roots[0, i0], 0.0)
        i1 = 2 * pair + par
        here = unit_at(p, i1)
        n = p * 8 + i1
        s1_less = roots[0, i1] * s1_base
        n_less = p * 8 + jnp.maximum(i1 - 1, 0)
        new = [[], []]
        for t in range(TILES):
            j0 = 4 * place.gj0 + t
            lanes = slice(t * LANES, (t + 1) * LANES)
            turn = (32 * (tb.edge1 - t)) % LANES
            comm = []
            sand = []
            for c in range(2):
                across = i2_halo(place, h_i2, p, pair, par, c, t)
                k = k2_mask * across + k1_mask * pltpu.roll(h_j1[2 * n + c], turn, 1)
                s = s2_base * pltpu.roll(across, 4, 1) + s1_less * pltpu.roll(h_j1[2 * n_less + c], turn, 1)
                if p == 3:
                    k = k + (2.0 * u[0]) * h_i0[i1, c, :, lanes]
                    if t > 0:
                        s = s + (decay[0] * 2.0 * upf * roots[0, j0]) * h_i0[
                            i1, c, :, (t - 1) * LANES : t * LANES
                        ]
                    else:
                        s = s + (decay[0] * 4.0 * upf * gj0f) * h_c[i1, c]
                if t == 0 or t == TILES - 1:
                    on = gj0f if t == 0 else 1.0 - gj0f
                    k = k - (2.0 * u[0] * on) * h_j0[2 * n + c]
                if t == 0:
                    s = s + (decay[0] * 2.0 * gj0f * root_below) * h_j0[2 * (below * 8 + i1) + c]
                comm.append(k)
                sand.append(s)
            new[0].append(tile(part, here, 0, t) + (sand[0] - comm[1]))
            new[1].append(tile(part, here, 1, t) + (sand[1] + comm[0]))
        return here, new

    for p in range(4):

        def step(pair, carry, p=p):
            both = []
            for par in range(2):
                here, new = one(p, pair, par)
                for c in range(2):
                    for t in range(TILES):
                        out[here, c, :, t * LANES : (t + 1) * LANES] = new[c][t]
                both.append(new)
            put_slabs(place, tb, p, pair, both, *slabs)
            return carry

        def last_step(h, carry, p=p):
            for a in range(4):
                here, new = one(p, 2 * h + a // 2, a % 2)
                for c in range(2):
                    for t in range(TILES):
                        lanes = slice(t * LANES, (t + 1) * LANES)
                        at = (2 * a + c) * ROWS
                        block[here // 4, at : at + ROWS, lanes] = new[c][t]
                        if 2 * a + c >= MOST:
                            at -= MOST * ROWS
                            out_rest[here // 4, at : at + ROWS, lanes] = new[c][t]
            return carry

        if last:
            lax.fori_loop(0, 2, last_step, 0)
            slots = pl.ds(2 * p, 2)
            copies.append(pltpu.make_async_copy(block.at[slots], out_all.at[slots], sems.at[p]))
            copies[-1].start()
        else:
            lax.fori_loop(0, 4, step, 0)
    wait_all(copies)


def gradient_kernel(z_in, h_i0, state_in, h_j1, h_j0, h_i2, roots, grad, z, state, rho, sems):
    reads = [pltpu.make_async_copy(state_in, state, sems.at[0]), pltpu.make_async_copy(z_in, z, sems.at[1])]
    start_all(reads)
    place = Place()
    tb = Tables(place)
    gj0f = place.gj0.astype(F32)
    wait_all(reads)
    copy_state(2, state, (h_j1, h_j0, h_i2), rho, lambda r: r ^ place.slot)
    k1_mask = -2.0 * tb.at1
    k2_mask = 2.0 * tb.at2

    def half_step(n, par, acc):
        p = n // 4
        pair = n % 4
        i1 = 2 * pair + par
        unit = p * 8 + i1
        here = unit_at(p, i1)
        _, below, above, less, more = unit_neighbours(place, roots, p, i1)
        outer = jnp.where(p == 3, 2.0, 0.0)
        for t in range(TILES):
            j0 = 4 * place.gj0 + t
            turn = (32 * (tb.edge1 - t)) % LANES
            for c in range(2):
                m = tile(z, here, c, t)
                k0 = below[1] * tile(z, below[0], c, t) + above[1] * tile(z, above[0], c, t)
                k0 = k0 + outer * h_i0[i1, c, :, t * LANES : (t + 1) * LANES]
                if t > 0:
                    k0 = k0 - roots[0, j0] * tile(z, here, c, t - 1)
                if t < TILES - 1:
                    k0 = k0 - roots[0, j0 + 1] * tile(z, here, c, t + 1)
                if t == 0 or t == TILES - 1:
                    on = gj0f if t == 0 else 1.0 - gj0f
                    k0 = k0 - (2.0 * on) * h_j0[2 * unit + c]
                k1 = less[1] * tile(z, less[0], c, t) + more[1] * tile(z, more[0], c, t)
                k1 = k1 - tb.c1p * pltpu.roll(m, 32, 1) - tb.c1m * pltpu.roll(m, LANES - 32, 1)
                k1 = k1 + k1_mask * pltpu.roll(h_j1[2 * unit + c], turn, 1)
                k2 = tb.r2p * pltpu.roll(m, 4, 0) + tb.r2m * pltpu.roll(m, ROWS - 4, 0)
                k2 = k2 - tb.c2p * pltpu.roll(m, 4, 1) - tb.c2m * pltpu.roll(m, LANES - 4, 1)
                k2 = k2 + k2_mask * i2_halo(place, h_i2, p, pair, par, c, t)
                k3 = tb.r3p * pltpu.roll(m, 1, 0) + tb.r3m * pltpu.roll(m, ROWS - 1, 0)
                k3 = k3 - tb.c3p * pltpu.roll(m, 1, 1) - tb.c3m * pltpu.roll(m, LANES - 1, 1)
                other = rho[(2 * here + 1 - c) * TILES + t]
                if c == 1:
                    other = -other
                acc = [acc[q] + k * other for q, k in enumerate((k0, k1, k2, k3))]
        return acc

    def step(n, carry):
        acc = list(carry)
        for par in range(2):
            acc = half_step(n, par, acc)
        return tuple(acc)

    total = lax.fori_loop(0, UNITS // 2, step, tuple(jnp.zeros((ROWS, LANES), F32) for _ in range(4)))
    for q in range(4):
        grad[:, q * LANES : (q + 1) * LANES] = total[q][0:8] + total[q][8:16]


def chunk_lanes(g, t):
    start = (g // 2) * 1024 + t * 256 + (g % 2) * 128
    return slice(start, start + LANES)


def slice_rows(a):
    return pl.ds(32 * a, 32)


def pack_kernel(x, out, plain, block, sems):
    upper = lax.axis_index("row") // 8
    reads = [
        pltpu.make_async_copy(x.at[:, slice_rows(a)], plain.at[:, slice_rows(a)], sems.at[a]) for a in range(4)
    ]
    writes = [pltpu.make_async_copy(block.at[:, a], out.at[:, a], sems.at[4 + a]) for a in range(4)]
    start_all(reads)
    for a in range(4):
        reads[a].wait()
        for gi2 in range(2):
            for g in range(4):
                k = 4 * gi2 + jnp.where(upper == 1, 3 - g, g)
                for c in range(2):
                    for t in range(TILES):
                        block[k, a, c, :, t * LANES : (t + 1) * LANES] = plain[
                            c, 32 * a + 16 * gi2 : 32 * a + 16 * gi2 + 16, chunk_lanes(g, t)
                        ]
        writes[a].start()
    wait_all(writes)


def deal_kernel(x, state):
    place = Place()
    for gi2 in range(2):
        for g in range(4):
            k = 4 * gi2 + jnp.where(place.upper == 1, 3 - g, g)
            r = k ^ place.slot
            for a in range(4):
                rows = slice(a * 32 + gi2 * 16, a * 32 + gi2 * 16 + 16)
                for c in range(2):
                    for t in range(TILES):
                        state[(r * 8 + a * 2 + c) * TILES + t] = x[c, rows, chunk_lanes(g, t)]


def join_kernel(blocks, grad, out, sems):
    rows = 16 * (8 - MOST)
    copies = [pltpu.make_async_copy(blocks, out.at[:, pl.ds(0, rows)], sems.at[8])]
    for k in range(8):
        copies.append(pltpu.make_async_copy(grad, out.at[k, pl.ds(rows, 8)], sems.at[k]))
    start_all(copies)
    wait_all(copies)


def undeal(upper, index, source, first, out, base=None):
    a, c = index // 2, index % 2
    for gi2 in range(2):
        rows = slice(32 * a + 16 * gi2, 32 * a + 16 * gi2 + 16)
        for g in range(4):
            k = 4 * gi2 + jnp.where(upper == 1, 3 - g, g)
            for t in range(TILES):
                lanes = chunk_lanes(g, t)
                value = source[k, first : first + 16, t * LANES : (t + 1) * LANES]
                if base is not None:
                    value = base[c, rows, lanes] - value
                out[c, rows, lanes] = value


def start_kernel(blocks, start, held, plain, sems):
    upper = lax.axis_index("row") // 8
    reads = [
        pltpu.make_async_copy(blocks.at[:, pl.ds(32 * a, 32)], held.at[:, pl.ds(32 * a, 32)], sems.at[a])
        for a in range(4)
    ]
    writes = [
        pltpu.make_async_copy(plain.at[:, slice_rows(a)], start.at[:, slice_rows(a)], sems.at[4 + a])
        for a in range(4)
    ]
    start_all(reads)
    for a in range(4):
        reads[a].wait()
        for c in range(2):
            undeal(upper, 2 * a + c, held, 32 * a + 16 * c, plain)
        writes[a].start()
    wait_all(writes)


def finish_kernel(most, rest, base, defect, held_most, held_rest, held_base, plain, sems):
    upper = lax.axis_index("row") // 8
    rows = 16 * (8 - MOST)
    reads = [
        pltpu.make_async_copy(rest.at[:, pl.ds(0, rows)], held_rest, sems.at[0]),
        pltpu.make_async_copy(most, held_most, sems.at[1]),
    ]
    order = (3, 2, 1, 0)
    for a in order:
        reads.append(
            pltpu.make_async_copy(base.at[:, slice_rows(a)], held_base.at[:, slice_rows(a)], sems.at[2 + a])
        )
    writes = [
        pltpu.make_async_copy(plain.at[:, slice_rows(a)], defect.at[:, slice_rows(a)], sems.at[6 + a])
        for a in order
    ]
    start_all(reads)
    reads[0].wait()
    for at, a in enumerate(order):
        if at == 1:
            reads[1].wait()
        reads[2 + at].wait()
        for c in range(2):
            index = 2 * a + c
            if index < MOST:
                undeal(upper, index, held_most, 16 * index, plain, held_base)
            else:
                undeal(upper, index, held_rest, 16 * (index - MOST), plain, held_base)
        writes[at].start()
    wait_all(writes)


VMEM = pl.BlockSpec(memory_space=pltpu.VMEM)
SMEM = pl.BlockSpec(memory_space=pltpu.SMEM)
ANY = pl.BlockSpec(memory_space=pl.ANY)
PARAMS = pltpu.CompilerParams(vmem_limit_bytes=16 * 1024 * 1024)
MOST = 5
UNIT_SHAPE = (UNITS, 2, ROWS, WIDTH)
PACKED_SHAPE = (8, 4, 2, ROWS, WIDTH)
STATE_SHAPE = (64 * TILES, ROWS, LANES)
PLAIN_SHAPE = (2, 128, ORDER)
BLOCKS_SHAPE = (8, 128, WIDTH)
MOST_SHAPE = (8, 16 * MOST, WIDTH)
REST_SHAPE = (8, 16 * (8 - MOST), WIDTH)
JOINED_SHAPE = (8, 16 * (8 - MOST) + 8, WIDTH)


def slab_shapes(n):
    riders = [4 * len(PARTS[ROUTES[n][bit]]) * TILES for bit in range(3)]
    return (
        [(8, 2, ROWS, WIDTH)]
        + [(EDGE + extra, ROWS, LANES) for extra in riders]
        + [(8, 2, ROWS, LANES)]
    )


def shape(dims):
    return jax.ShapeDtypeStruct(dims, F32)


def copies(count):
    return pltpu.SemaphoreType.DMA((count,))


def room(dims):
    return pltpu.VMEM(dims, F32)


def call(kernel, outs, args, scalars=(), flops=0, size=4 << 20, scratch=(), name=None, specs=None, out_specs=None, **more):
    out_shape = [shape(s) if isinstance(s, tuple) else s for s in outs]
    return pl.pallas_call(
        kernel,
        out_shape=out_shape,
        in_specs=(specs or [VMEM] * len(args)) + [SMEM] * len(scalars),
        out_specs=out_specs or [VMEM] * len(outs),
        scratch_shapes=list(scratch),
        compiler_params=PARAMS,
        cost_estimate=pl.CostEstimate(flops=flops, bytes_accessed=size, transcendentals=0),
        name=name,
        **more,
    )(*args, *scalars)


def in_hbm(x):
    return pltpu.with_memory_space_constraint(x, pltpu.HBM)


def hbm(dims):
    return pltpu.HBM(dims, F32)


def regroup(x):
    return lax.all_to_all(x, "row", 0, 0, axis_index_groups=GROUPS, tiled=True)


def earlier(x):
    return lax.ppermute(x, "seg", [(i + 1, i) for i in range(7)])


def exchange(slabs):
    perms = (PERM_I0, PERM_J1, PERM_J0, PERM_I2, PERM_CORNER)
    return [lax.ppermute(s, "row", perm) for s, perm in zip(slabs, perms)]


def body(
    terminal_adjoint,
    midpoint_state,
    controls,
    detuning,
    anharmonicity,
    decay_rate,
    dephasing,
    cross_kerr,
):
    amp = controls[0]
    dec = decay_rate[None]
    roots = jnp.asarray(ROOTS)[None]
    full = (amp, detuning[None], anharmonicity[None], dec, dephasing[None], cross_kerr[None], roots)
    few = (amp, dec, roots)
    terminal = terminal_adjoint[0]
    (packed,) = call(
        pack_kernel,
        [hbm(PACKED_SHAPE)],
        [in_hbm(terminal)],
        specs=[ANY],
        out_specs=[ANY],
        scratch=[room(PLAIN_SHAPE), room(PACKED_SHAPE), copies(8)],
        name="pack_blocks",
    )
    base = regroup(packed).reshape(UNIT_SHAPE)
    (state,) = call(deal_kernel, [STATE_SHAPE], [midpoint_state[0, 0]], name="deal_state")
    slabs = call(
        slab_kernel, slab_shapes(0), [base, state], name="slabs"
    )
    current = base
    for n in range(3):
        scale = STEP if n == 2 else 0.5 * STEP
        before = halos[1:4] if n else []
        halos = exchange(slabs)
        results = call(
            lambda *refs, n=n, scale=scale: local_kernel(scale, n, *refs),
            [UNIT_SHAPE] + [[], [STATE_SHAPE], [hbm(UNIT_SHAPE), hbm(STATE_SHAPE)]][n],
            [current, base] + ([state, *before] if n else []),
            full,
            flops=30 << 20,
            size=6 << 20,
            out_specs=[VMEM] + [[], [VMEM], [ANY, ANY]][n],
            scratch=[room(STATE_SHAPE), copies(2)] if n == 2 else [],
            name="local_terms",
        )
        part = results[0]
        if n:
            *middle, state = results[1:]
        if n < 2:
            current, *slabs = call(
                lambda *refs, n=n, scale=scale: edge_kernel(scale, n + 1, *refs),
                [UNIT_SHAPE, *slab_shapes(n + 1)],
                [part, *halos, state],
                few,
                flops=5 << 20,
                size=8 << 20,
                name="edge_terms",
            )
    final, rest = call(
        lambda *refs: edge_kernel(STEP, None, *refs),
        [hbm(BLOCKS_SHAPE), REST_SHAPE],
        [part, *halos],
        few,
        flops=5 << 20,
        size=6 << 20,
        out_specs=[ANY, VMEM],
        scratch=[room(BLOCKS_SHAPE), copies(4)],
        name="edge_terms",
    )
    here = regroup(final)
    rest_next = earlier(rest)
    (grad,) = call(
        gradient_kernel,
        [(8, WIDTH)],
        [*middle, halos[0], state, *halos[1:4]],
        (roots,),
        flops=30 << 20,
        size=6 << 20,
        specs=[ANY, VMEM, ANY, VMEM, VMEM, VMEM],
        scratch=[room(UNIT_SHAPE), room(STATE_SHAPE), room(STATE_SHAPE), copies(2)],
        name="gradient",
    )
    (joined,) = call(
        join_kernel,
        [hbm(JOINED_SHAPE)],
        [rest_next, grad],
        out_specs=[ANY],
        scratch=[copies(9)],
        name="join_blocks",
    )
    here, joined = lax.optimization_barrier((here, joined))
    rest_here = regroup(joined)
    most_next = earlier(here[:, : 16 * MOST])
    (start,) = call(
        start_kernel,
        [hbm(PLAIN_SHAPE)],
        [here],
        specs=[ANY],
        out_specs=[ANY],
        scratch=[room(BLOCKS_SHAPE), room(PLAIN_SHAPE), copies(8)],
        name="start_rows",
    )
    start, rest_here, most_next = lax.optimization_barrier((start, rest_here, most_next))
    (defect,) = call(
        finish_kernel,
        [hbm(PLAIN_SHAPE)],
        [most_next, rest_here, terminal],
        specs=[ANY] * 3,
        out_specs=[ANY],
        scratch=[room(MOST_SHAPE), room(REST_SHAPE), room(PLAIN_SHAPE), room(PLAIN_SHAPE), copies(10)],
        name="defect_rows",
    )
    grad = jnp.sum(rest_here[:, 16 * (8 - MOST) :], axis=0)
    grad = grad + lax.ppermute(grad, "row", PERM_I0)
    totals = jnp.sum(grad.reshape(8, 4, LANES), axis=(0, 2)) / ORDER
    return start[None], defect[None], totals[None, None]


def solution(mesh):
    return jax.shard_map(
        body,
        mesh=mesh,
        in_specs=(
            P("seg", None, "row", None),
            P("seg", None, None, "row", None),
            P("seg", None, None),
            P(),
            P(),
            P(),
            P(),
            P(),
        ),
        out_specs=(P("seg", None, "row", None), P("seg", None, "row", None), P("seg", None, None)),
        check_vma=False,
    )
```

time: 199 us -> 183 us (0.920)
  blocking collectives: 25.3 us -> 0 us
  starting transfers between devices: 46.2 us -> 59.5 us
  waiting for transfers between devices: 61.3 us -> 54.7 us
    ppermute x20 -> x18, waiting for transfers between devices: 38.4 us -> 11 us  [the longest x15 11 us: exchange(): return [lax.ppermute(s, 'row', perm) for s, perm in zip(slabs, perms)]]
    all_to_all x1 -> x0, blocking collectives: 25.3 us -> none  [regroup(): return lax.all_to_all(x, 'row', 0, 0, axis_index_groups=GROUPS, tiled=True)]
    all_to_all x2 -> x3, waiting for transfers between devices: 22.9 us -> 43.8 us  [regroup(): return lax.all_to_all(x, 'row', 0, 0, axis_index_groups=GROUPS, tiled=True)]
    ppermute x20 -> x18, starting transfers between devices: 33.6 us -> 43.5 us  [the longest x15 29.8 us: exchange(): return [lax.ppermute(s, 'row', perm) for s, perm in zip(slabs, perms)]]
    all_to_all x2 -> x3, starting transfers between devices: 12.6 us -> 16 us  [regroup(): return lax.all_to_all(x, 'row', 0, 0, axis_index_groups=GROUPS, tiled=True)]
    pallas_call x11 -> x13, Pallas kernels: 51.2 us -> 53 us  [call(): pl.pallas_call(kernel, out_shape=out_shape, in_specs=(specs or [VMEM] * l...]
    unnamed x36 -> x38, local copies, waits for them, and re-layouts: 13 us -> 12.5 us
  transfers between devices with their start and end apart: 22 -> 21, of which waited for: 8 -> 12; matrix products, arithmetic and copies ran while one was open for 0% -> 0% of each run, Pallas kernels for 22% -> 20%
where the time goes in v1:
time: 183 us
  starting transfers between devices  59.5 us (33%)
  waiting for transfers between devices  54.7 us (30%)
  Pallas kernels  53 us (29%)
  local copies, waits for them, and re-layouts  13.7 us (7%)
    pallas_call x13, Pallas kernels, call(): pl.pallas_call(kernel, out_shape=out_shape, in_specs=(specs or [VMEM] * l...  53 us
    all_to_all x3, waiting for transfers between devices, regroup(): return lax.all_to_all(x, 'row', 0, 0, axis_index_groups=GROUPS, tiled=True)  43.8 us
    ppermute x15, starting transfers between devices, exchange(): return [lax.ppermute(s, 'row', perm) for s, perm in zip(slabs, perms)]  29.8 us
    all_to_all x3, starting transfers between devices, regroup(): return lax.all_to_all(x, 'row', 0, 0, axis_index_groups=GROUPS, tiled=True)  16 us
    unnamed x38, local copies, waits for them, and re-layouts  12.5 us
    ppermute x15, waiting for transfers between devices, exchange(): return [lax.ppermute(s, 'row', perm) for s, perm in zip(slabs, perms)]  11 us
    ppermute x2, starting transfers between devices, earlier(): return lax.ppermute(x, 'seg', [(i + 1, i) for i in range(7)])  10.1 us
  transfers between devices with their start and end apart: 21, of which 12 were waited for; matrix products, arithmetic and copies ran while one was open for 0% of the time, Pallas kernels for 20%

profile of v1, /device:TPU:1, one launch (start us, length us, event | category | flops | bytes accessed | tf_op | source)
XLA Modules:
  0.0 182.6 jit_solution(5766659806040552442)
XLA Ops:
  0.6 2.5 %pack_blocks.1 = f32[8,4,2,16,512]{4,3,2,1,0:T(8,128)} custom-call(f32[2,128,2048]{2,1,0:T(8,128)} %bitcast.20), custom_call_target="tpu_custom_call" | custom-call | bytes 4194304 | tf_op jit(solution)/shard_map/pack_blocks/pallas_call | solution.py:664
  3.1 6.9 %all-to-all-start = ((f32[8,4,2,16,512]{4,3,2,1,0:T(8,128)}), f32[8,4,2,16,512]{4,3,2,1,0:T(8,128)S(1)}, u32[]{:S(2)}, u32[]{:S(2)}) async-start(f32[8,4,2,16,512]{4,3,2,1,0:T(8,128)} %pack_blocks.1), calls=%async_computation | async-start | bytes 4194304 | tf_op jit(solution)/shard_map/all_to_all | solution.py:686
  10.0 1.6 copy-done.8
  11.8 1.3 copy-done
  13.1 23.4 %all-to-all-done = f32[8,4,2,16,512]{4,3,2,1,0:T(8,128)S(1)} async-done(((f32[8,4,2,16,512]{4,3,2,1,0:T(8,128)}), f32[8,4,2,16,512]{4,3,2,1,0:T(8,128)S(1)}, u32[]{:S(2)}, u32[]{:S(2)}) %all-to-all-start) | async-done | bytes 2097184 | tf_op jit(solution)/shard_map/all_to_all | solution.py:686
  36.5 1.6 copy-done.1
  38.1 1.8 slabs.1
  39.9 1.3 collective-permute-start.1
  41.2 1.8 %collective-permute-start.2 = (f32[112,16,128]{2,1,0:T(8,128)S(1)}, f32[112,16,128]{2,1,0:T(8,128)S(1)}, u32[]{:S(2)}, u32[]{:S(2)}) collective-permute-start(f32[112,16,128]{2,1,0:T(8,128)S(1)} %get-tuple-element.34), channel_id=1, source_target_pairs={{0,3},{1,2},{2,1},{3,0},{4,7},{5,6},{6,5},{7,4},{8,11},{9,10},{10,... | collective-permute-start | bytes 2752520 | tf_op jit(solution)/shard_map/ppermute | solution.py:695
  43.0 2.0 %collective-permute-start.3 = (f32[96,16,128]{2,1,0:T(8,128)S(1)}, f32[96,16,128]{2,1,0:T(8,128)S(1)}, u32[]{:S(2)}, u32[]{:S(2)}) collective-permute-start(f32[96,16,128]{2,1,0:T(8,128)S(1)} %get-tuple-element.35), channel_id=1, source_target_pairs={{0,4},{1,5},{2,6},{3,7},{4,0},{5,1},{6,2},{7,3},{8,12},{9,13},{10,... | collective-permute-start | bytes 2359304 | tf_op jit(solution)/shard_map/ppermute | solution.py:695
  45.5 3.8 %collective-permute-start.4 = (f32[8,2,16,128]{3,2,1,0:T(8,128)S(1)}, f32[8,2,16,128]{3,2,1,0:T(8,128)S(1)}, u32[]{:S(2)}, u32[]{:S(2)}) collective-permute-start(f32[8,2,16,128]{3,2,1,0:T(8,128)S(1)} %get-tuple-element.36), channel_id=1, source_target_pairs={{0,15},{1,14},{4,11},{5,10},{16,31},{17,30},{20,27},{21,26},{32,47... | collective-permute-start | bytes 393224 | tf_op jit(solution)/shard_map/ppermute | solution.py:695
  49.4 8.1 %local_terms.3.refs_0_ = f32[32,2,16,512]{3,2,1,0:T(8,128)S(1)} custom-call(f32[32,2,16,512]{3,2,1,0:T(8,128)S(1)} %bitcast.16, f32[32,2,16,512]{3,2,1,0:T(8,128)S(1)} %bitcast.17, f32[1,4]{1,0:T(1,128)S(1)} %bitcast.23, f32[1,4]{1,0:T(1,128)S(1)} %bitcast.35, f32[1,4]{1,0:T(1,128)S(1)} %bitcast.38, f32[1,4]{1,0:T(1,128)S(1)} %bitcast.29, ...), custom_call_target="tpu_custom_call" | custom-call | flops 31457280 | bytes 6291456 | tf_op jit(solution)/shard_map/local_terms/pallas_call | solution.py:664
  58.3 2.5 %collective-permute-done.3.refs_4_.refs_5_ = f32[96,16,128]{2,1,0:T(8,128)S(1)} collective-permute-done((f32[96,16,128]{2,1,0:T(8,128)S(1)}, f32[96,16,128]{2,1,0:T(8,128)S(1)}, u32[]{:S(2)}, u32[]{:S(2)}) %collective-permute-start.3) | collective-permute-done | bytes 786464 | tf_op jit(solution)/shard_map/ppermute | solution.py:695
  60.8 1.3 collective-permute-done.2.refs_3_.refs_4_
  62.1 4.3 %edge_terms.3 = (f32[32,2,16,512]{3,2,1,0:T(8,128)S(1)}, f32[8,2,16,512]{3,2,1,0:T(8,128)S(1)}, f32[96,16,128]{2,1,0:T(8,128)S(1)}, f32[112,16,128]{2,1,0:T(8,12...) custom-call(f32[32,2,16,512]{3,2,1,0:T(8,128)S(1)} %local_terms.3.refs_0_, ...), custom_call_target="tpu_custom_call" | custom-call | flops 5242880 | bytes 8388608 | tf_op jit(solution)/shard_map/edge_terms/pallas_call | solution.py:664
  66.4 1.9 %collective-permute-start.7 = (f32[112,16,128]{2,1,0:T(8,128)S(1)}, f32[112,16,128]{2,1,0:T(8,128)S(1)}, u32[]{:S(2)}, u32[]{:S(2)}) collective-permute-start(f32[112,16,128]{2,1,0:T(8,128)S(1)} %get-tuple-element.41), channel_id=1, source_target_pairs={{0,3},{1,2},{2,1},{3,0},{4,7},{5,6},{6,5},{7,4},{8,11},{9,10},{10,... | collective-permute-start | bytes 2752520 | tf_op jit(solution)/shard_map/ppermute | solution.py:695
  68.3 3.4 %collective-permute-start.8 = (f32[112,16,128]{2,1,0:T(8,128)S(1)}, f32[112,16,128]{2,1,0:T(8,128)S(1)}, u32[]{:S(2)}, u32[]{:S(2)}) collective-permute-start(f32[112,16,128]{2,1,0:T(8,128)S(1)} %get-tuple-element.42), channel_id=1, source_target_pairs={{0,4},{1,5},{2,6},{3,7},{4,0},{5,1},{6,2},{7,3},{8,12},{9,13},{10,... | collective-permute-start | bytes 2752520 | tf_op jit(solution)/shard_map/ppermute | solution.py:695
  71.7 3.1 %collective-permute-start.5 = (f32[8,2,16,512]{3,2,1,0:T(8,128)S(1)}, f32[8,2,16,512]{3,2,1,0:T(8,128)S(1)}, u32[]{:S(2)}, u32[]{:S(2)}) collective-permute-start(f32[8,2,16,512]{3,2,1,0:T(8,128)S(1)} %get-tuple-element.39), channel_id=1, source_target_pairs={{0,12},{1,13},{2,14},{3,15},{4,8},{5,9},{6,10},{7,11},{8,4},{9,5},... | collective-permute-start | bytes 1572872 | tf_op jit(solution)/shard_map/ppermute | solution.py:695
  74.8 1.7 collective-permute-start.9
  76.6 8.4 %local_terms.4 = (f32[32,2,16,512]{3,2,1,0:T(8,128)S(1)}, f32[256,16,128]{2,1,0:T(8,128)S(1)}) custom-call(f32[32,2,16,512]{3,2,1,0:T(8,128)S(1)} %get-tuple-element.37.refs_0_, f32[32,2,16,512]{3,2,1,0:T(8,128)S(1)} %bitcast.18, f32[256,16,128]{2,1,0:T(8,128)S(1)} %copy-done.2, f32[112,16,128]{2,1,0:T(8,128)S(1)} %collective-permute-done.1.refs_2_.refs_3_, ...), custom_call_target="tpu_custom_call" | custom-call | flops 31457280 | bytes 6291456 | tf_op jit(solution)/shard_map/local_terms/pallas_call | solution.py:664
  85.0 1.5 collective-permute-done.9.refs_5_
  86.5 2.0 %collective-permute-done.6.refs_2_.refs_3_ = f32[96,16,128]{2,1,0:T(8,128)S(1)} collective-permute-done((f32[96,16,128]{2,1,0:T(8,128)S(1)}, f32[96,16,128]{2,1,0:T(8,128)S(1)}, u32[]{:S(2)}, u32[]{:S(2)}) %collective-permute-start.6) | collective-permute-done | bytes 786464 | tf_op jit(solution)/shard_map/ppermute | solution.py:695
  88.5 1.9 %collective-permute-done.8.refs_4_.refs_5_ = f32[112,16,128]{2,1,0:T(8,128)S(1)} collective-permute-done((f32[112,16,128]{2,1,0:T(8,128)S(1)}, f32[112,16,128]{2,1,0:T(8,128)S(1)}, u32[]{:S(2)}, u32[]{:S(2)}) %collective-permute-start.8) | collective-permute-done | bytes 917536 | tf_op jit(solution)/shard_map/ppermute | solution.py:695
  90.4 4.3 %edge_terms.4 = (f32[32,2,16,512]{3,2,1,0:T(8,128)S(1)}, f32[8,2,16,512]{3,2,1,0:T(8,128)S(1)}, f32[112,16,128]{2,1,0:T(8,128)S(1)}, f32[96,16,128]{2,1,0:T(8,12...) custom-call(f32[32,2,16,512]{3,2,1,0:T(8,128)S(1)} %get-tuple-element.38.refs_0_, ...), custom_call_target="tpu_custom_call" | custom-call | flops 5242880 | bytes 8388608 | tf_op jit(solution)/shard_map/edge_terms/pallas_call | solution.py:664
  94.8 1.3 collective-permute-start.13
  96.0 1.5 collective-permute-start.12
  97.5 5.8 %collective-permute-start.10 = (f32[8,2,16,512]{3,2,1,0:T(8,128)S(1)}, f32[8,2,16,512]{3,2,1,0:T(8,128)S(1)}, u32[]{:S(2)}, u32[]{:S(2)}) collective-permute-start(f32[8,2,16,512]{3,2,1,0:T(8,128)S(1)} %get-tuple-element.47), channel_id=1, source_target_pairs={{0,12},{1,13},{2,14},{3,15},{4,8},{5,9},{6,10},{7,11},{8,4},{9,5},... | collective-permute-start | bytes 1572872 | tf_op jit(solution)/shard_map/ppermute | solution.py:695
  103.3 1.6 collective-permute-start.14
  104.9 8.3 %local_terms.5 = (f32[32,2,16,512]{3,2,1,0:T(8,128)S(1)}, f32[32,2,16,512]{3,2,1,0:T(8,128)}, f32[256,16,128]{2,1,0:T(8,128)}) custom-call(f32[32,2,16,512]{3,2,1,0:T(8,128)S(1)} %get-tuple-element.45.refs_0_, f32[32,2,16,512]{3,2,1,0:T(8,128)S(1)} %bitcast.19, f32[256,16,128]{2,1,0:T(8,128)S(1)} %get-tuple-element.44.refs_6_.refs_2_, ...), custom_call_target="tpu_custom_call" | custom-call | flops 31457280 | bytes 6291456 | tf_op jit(solution)/shard_map/local_terms/pallas_call | solution.py:664
  114.1 3.4 %edge_terms.5 = (f32[8,128,512]{2,1,0:T(8,128)}, f32[8,48,512]{2,1,0:T(8,128)S(1)}) custom-call(f32[32,2,16,512]{3,2,1,0:T(8,128)S(1)} %get-tuple-element.46.refs_0_, f32[8,2,16,512]{3,2,1,0:T(8,128)S(1)} %collective-permute-done.10.refs_1_.h_i0, f32[112,16,128]{2,1,0:T(8,128)S(1)} %collective-permute-done.11.refs_2_.h_j1, ...), custom_call_target="tpu_custom_call" | custom-call | flops 5242880 | bytes 6291456 | tf_op jit(solution)/shard_map/edge_terms/pallas_call | solution.py:664
  117.5 0.9 copy-done.18
  118.4 4.5 %all-to-all-start.1 = ((f32[8,128,512]{2,1,0:T(8,128)}), f32[8,128,512]{2,1,0:T(8,128)S(1)}, u32[]{:S(2)}, u32[]{:S(2)}) async-start(f32[8,128,512]{2,1,0:T(8,128)} %get-tuple-element.52), calls=%async_computation.1 | async-start | bytes 4194304 | tf_op jit(solution)/shard_map/all_to_all | solution.py:686
  122.9 6.0 %collective-permute-start.15 = (f32[8,48,512]{2,1,0:T(8,128)}, f32[8,48,512]{2,1,0:T(8,128)S(1)}, u32[]{:S(2)}, u32[]{:S(2)}) collective-permute-start(f32[8,48,512]{2,1,0:T(8,128)} %copy-done.18), channel_id=1, source_target_pairs={{16,0},{32,16},{48,32},{64,48},{80,64},{96,80},{112,96},{17,1},{33... | collective-permute-start | bytes 2359304 | tf_op jit(solution)/shard_map/ppermute | solution.py:690
  128.9 1.2 copy-done.5
  130.1 1.1 copy-done.7
  131.2 1.6 copy-done.9
  132.8 1.6 copy-done.10
  134.4 6.4 %gradient.1.grad = f32[8,512]{1,0:T(8,128)S(1)} custom-call(f32[32,2,16,512]{3,2,1,0:T(8,128)S(1)} %copy-done.9, f32[8,2,16,512]{3,2,1,0:T(8,128)S(1)} %collective-permute-done.10.refs_1_.h_i0, f32[256,16,128]{2,1,0:T(8,128)S(1)} %copy-done.10, f32[112,16,128]{2,1,0:T(8,128)S(1)} %collective-permute-done.11.refs_2_.h_j1, f32[96,16,128]{2,1,0:T(8,128)S(1)} %copy-done.7, ...), custom_call_target="tpu_custom_call" | custom-call | flops 31457280 | bytes 6291456 | tf_op jit(solution)/shard_map/gradient/pallas_call | solution.py:664
  140.8 1.0 join_blocks.1
  141.9 7.2 %all-to-all-done.1.blocks = f32[8,128,512]{2,1,0:T(8,128)S(1)} async-done(((f32[8,128,512]{2,1,0:T(8,128)}), f32[8,128,512]{2,1,0:T(8,128)S(1)}, u32[]{:S(2)}, u32[]{:S(2)}) %all-to-all-start.1) | async-done | bytes 2097184 | tf_op jit(solution)/shard_map/all_to_all | solution.py:686
  149.0 1.2 slice.6
  150.2 4.1 %collective-permute-start.16 = (f32[8,80,512]{2,1,0:T(8,128)}, f32[8,80,512]{2,1,0:T(8,128)}, u32[]{:S(2)}, u32[]{:S(2)}) collective-permute-start(f32[8,80,512]{2,1,0:T(8,128)} %slice.6), channel_id=1, source_target_pairs={{16,0},{32,16},{48,32},{64,48},{80,64},{96,80},{112,96},{17,1},{33... | collective-permute-start | bytes 3932168 | tf_op jit(solution)/shard_map/ppermute | solution.py:690
  154.4 4.7 %all-to-all-start.2 = ((f32[8,56,512]{2,1,0:T(8,128)}), f32[8,56,512]{2,1,0:T(8,128)S(1)}, u32[]{:S(2)}, u32[]{:S(2)}) async-start(f32[8,56,512]{2,1,0:T(8,128)} %join_blocks.1), calls=%async_computation.2 | async-start | bytes 1835008 | tf_op jit(solution)/shard_map/all_to_all | solution.py:686
  159.0 1.6 start_rows.1
  160.6 13.2 %all-to-all-done.2.rest = f32[8,56,512]{2,1,0:T(8,128)S(1)} async-done(((f32[8,56,512]{2,1,0:T(8,128)}), f32[8,56,512]{2,1,0:T(8,128)S(1)}, u32[]{:S(2)}, u32[]{:S(2)}) %all-to-all-start.2) | async-done | bytes 917536 | tf_op jit(solution)/shard_map/all_to_all | solution.py:686
  173.8 3.6 %collective-permute-start.17 = (f32[8,512]{1,0:T(8,128)S(1)}, f32[8,512]{1,0:T(8,128)S(1)}, u32[]{:S(2)}, u32[]{:S(2)}) collective-permute-start(f32[8,512]{1,0:T(8,128)S(1)} %slice_reduce_fusion), channel_id=1, source_target_pairs={{0,12},{1,13},{2,14},{3,15},{4,8},{5,9},{6,10},{7,11},{8,4},{9,5},... | collective-permute-start | bytes 49160 | tf_op jit(solution)/shard_map/ppermute | solution.py:812
  177.5 1.6 copy-done.3
  179.1 2.8 %defect_rows.1 = f32[2,128,2048]{2,1,0:T(8,128)} custom-call(f32[8,80,512]{2,1,0:T(8,128)} %collective-permute-done.16.most, f32[8,56,512]{2,1,0:T(8,128)S(1)} %all-to-all-done.2.rest, f32[2,128,2048]{2,1,0:T(8,128)S(1)} %bitcast.21), custom_call_target="tpu_custom_call" | custom-call | bytes 4194304 | tf_op jit(solution)/shard_map/defect_rows/pallas_call | solution.py:664
  (50 shorter events, 3.2 us)
Async XLA Ops:
  3.1 33.4 %all-to-all-start = ((f32[8,4,2,16,512]{4,3,2,1,0:T(8,128)}), f32[8,4,2,16,512]{4,3,2,1,0:T(8,128)S(1)}, u32[]{:S(2)}, u32[]{:S(2)}) async-start(f32[8,4,2,16,512]{4,3,2,1,0:T(8,128)} %pack_blocks.1), calls=%async_computation | async-start | bytes 4194304 | tf_op jit(solution)/shard_map/all_to_all | solution.py:686
  10.0 1.6 copy-start.8
  11.8 1.3 copy-start
  36.5 1.6 copy-start.1
  38.1 11.3 %copy-start.11 = (f32[1,16]{1,0:T(1,128)S(1)}, f32[1,16]{1,0:T(1,128)}, u32[]{:S(2)}) copy-start(f32[1,16]{1,0:T(1,128)} %constant.11.refs_8_.refs_9_.refs_12_.roots) | copy-start | bytes 196
  38.1 11.3 %copy-start.12 = (f32[1,1,4]{2,1,0:T(1,128)S(1)}, f32[1,1,4]{2,1,0:T(1,128)}, u32[]{:S(2)}) copy-start(f32[1,1,4]{2,1,0:T(1,128)} %param.11) | copy-start | bytes 52
  38.1 11.3 %copy-start.13 = (f32[4]{0:T(128)S(1)}, f32[4]{0:T(128)}, u32[]{:S(2)}) copy-start(f32[4]{0:T(128)} %param.14) | copy-start | bytes 52
  38.1 11.3 %copy-start.14 = (f32[4]{0:T(128)S(1)}, f32[4]{0:T(128)}, u32[]{:S(2)}) copy-start(f32[4]{0:T(128)} %param.12) | copy-start | bytes 52
  38.1 11.3 %copy-start.15 = (f32[4]{0:T(128)S(1)}, f32[4]{0:T(128)}, u32[]{:S(2)}) copy-start(f32[4]{0:T(128)} %param.13) | copy-start | bytes 52
  38.1 11.3 %copy-start.16 = (f32[4]{0:T(128)S(1)}, f32[4]{0:T(128)}, u32[]{:S(2)}) copy-start(f32[4]{0:T(128)} %param.15) | copy-start | bytes 52
  38.1 11.3 %copy-start.17 = (f32[6]{0:T(128)S(1)}, f32[6]{0:T(128)}, u32[]{:S(2)}) copy-start(f32[6]{0:T(128)} %param.16) | copy-start | bytes 76
  39.9 20.9 %collective-permute-start.1 = (f32[112,16,128]{2,1,0:T(8,128)S(1)}, f32[112,16,128]{2,1,0:T(8,128)S(1)}, u32[]{:S(2)}, u32[]{:S(2)}) collective-permute-start(f32[112,16,128]{2,1,0:T(8,128)S(1)} %get-tuple-element.33), channel_id=1, source_target_pairs={{0,1},{1,0},{2,3},{3,2},{4,5},{5,4},{6,7},{7,6},{8,9},{9,8},{10,11... | collective-permute-start | bytes 2752520 | tf_op jit(solution)/shard_map/ppermute | solution.py:695
  41.2 21.0 %collective-permute-start.2 = (f32[112,16,128]{2,1,0:T(8,128)S(1)}, f32[112,16,128]{2,1,0:T(8,128)S(1)}, u32[]{:S(2)}, u32[]{:S(2)}) collective-permute-start(f32[112,16,128]{2,1,0:T(8,128)S(1)} %get-tuple-element.34), channel_id=1, source_target_pairs={{0,3},{1,2},{2,1},{3,0},{4,7},{5,6},{6,5},{7,4},{8,11},{9,10},{10,... | collective-permute-start | bytes 2752520 | tf_op jit(solution)/shard_map/ppermute | solution.py:695
  43.0 17.8 %collective-permute-start.3 = (f32[96,16,128]{2,1,0:T(8,128)S(1)}, f32[96,16,128]{2,1,0:T(8,128)S(1)}, u32[]{:S(2)}, u32[]{:S(2)}) collective-permute-start(f32[96,16,128]{2,1,0:T(8,128)S(1)} %get-tuple-element.35), channel_id=1, source_target_pairs={{0,4},{1,5},{2,6},{3,7},{4,0},{5,1},{6,2},{7,3},{8,12},{9,13},{10,... | collective-permute-start | bytes 2359304 | tf_op jit(solution)/shard_map/ppermute | solution.py:695
  45.0 13.3 %collective-permute-start = (f32[8,2,16,512]{3,2,1,0:T(8,128)S(1)}, f32[8,2,16,512]{3,2,1,0:T(8,128)S(1)}, u32[]{:S(2)}, u32[]{:S(2)}) collective-permute-start(f32[8,2,16,512]{3,2,1,0:T(8,128)S(1)} %get-tuple-element.32), channel_id=1, source_target_pairs={{0,12},{1,13},{2,14},{3,15},{4,8},{5,9},{6,10},{7,11},{8,4},{9,5},... | collective-permute-start | bytes 1572872 | tf_op jit(solution)/shard_map/ppermute | solution.py:695
  45.5 12.5 %collective-permute-start.4 = (f32[8,2,16,128]{3,2,1,0:T(8,128)S(1)}, f32[8,2,16,128]{3,2,1,0:T(8,128)S(1)}, u32[]{:S(2)}, u32[]{:S(2)}) collective-permute-start(f32[8,2,16,128]{3,2,1,0:T(8,128)S(1)} %get-tuple-element.36), channel_id=1, source_target_pairs={{0,15},{1,14},{4,11},{5,10},{16,31},{17,30},{20,27},{21,26},{32,47... | collective-permute-start | bytes 393224 | tf_op jit(solution)/shard_map/ppermute | solution.py:695
  49.4 12.8 %copy-start.2 = (f32[256,16,128]{2,1,0:T(8,128)S(1)}, f32[256,16,128]{2,1,0:T(8,128)}, u32[]{:S(2)}) copy-start(f32[256,16,128]{2,1,0:T(8,128)} %copy-done) | copy-start | bytes 6291460
  66.4 22.1 %collective-permute-start.7 = (f32[112,16,128]{2,1,0:T(8,128)S(1)}, f32[112,16,128]{2,1,0:T(8,128)S(1)}, u32[]{:S(2)}, u32[]{:S(2)}) collective-permute-start(f32[112,16,128]{2,1,0:T(8,128)S(1)} %get-tuple-element.41), channel_id=1, source_target_pairs={{0,3},{1,2},{2,1},{3,0},{4,7},{5,6},{6,5},{7,4},{8,11},{9,10},{10,... | collective-permute-start | bytes 2752520 | tf_op jit(solution)/shard_map/ppermute | solution.py:695
  68.3 22.1 %collective-permute-start.8 = (f32[112,16,128]{2,1,0:T(8,128)S(1)}, f32[112,16,128]{2,1,0:T(8,128)S(1)}, u32[]{:S(2)}, u32[]{:S(2)}) collective-permute-start(f32[112,16,128]{2,1,0:T(8,128)S(1)} %get-tuple-element.42), channel_id=1, source_target_pairs={{0,4},{1,5},{2,6},{3,7},{4,0},{5,1},{6,2},{7,3},{8,12},{9,13},{10,... | collective-permute-start | bytes 2752520 | tf_op jit(solution)/shard_map/ppermute | solution.py:695
  71.7 16.8 %collective-permute-start.6 = (f32[96,16,128]{2,1,0:T(8,128)S(1)}, f32[96,16,128]{2,1,0:T(8,128)S(1)}, u32[]{:S(2)}, u32[]{:S(2)}) collective-permute-start(f32[96,16,128]{2,1,0:T(8,128)S(1)} %get-tuple-element.40), channel_id=1, source_target_pairs={{0,1},{1,0},{2,3},{3,2},{4,5},{5,4},{6,7},{7,6},{8,9},{9,8},{10,11... | collective-permute-start | bytes 2359304 | tf_op jit(solution)/shard_map/ppermute | solution.py:695
  71.7 14.8 %collective-permute-start.5 = (f32[8,2,16,512]{3,2,1,0:T(8,128)S(1)}, f32[8,2,16,512]{3,2,1,0:T(8,128)S(1)}, u32[]{:S(2)}, u32[]{:S(2)}) collective-permute-start(f32[8,2,16,512]{3,2,1,0:T(8,128)S(1)} %get-tuple-element.39), channel_id=1, source_target_pairs={{0,12},{1,13},{2,14},{3,15},{4,8},{5,9},{6,10},{7,11},{8,4},{9,5},... | collective-permute-start | bytes 1572872 | tf_op jit(solution)/shard_map/ppermute | solution.py:695
  74.8 11.6 %collective-permute-start.9 = (f32[8,2,16,128]{3,2,1,0:T(8,128)S(1)}, f32[8,2,16,128]{3,2,1,0:T(8,128)S(1)}, u32[]{:S(2)}, u32[]{:S(2)}) collective-permute-start(f32[8,2,16,128]{3,2,1,0:T(8,128)S(1)} %get-tuple-element.43), channel_id=1, source_target_pairs={{0,15},{1,14},{4,11},{5,10},{16,31},{17,30},{20,27},{21,26},{32,47... | collective-permute-start | bytes 393224 | tf_op jit(solution)/shard_map/ppermute | solution.py:695
  94.7 19.3 %collective-permute-start.11 = (f32[112,16,128]{2,1,0:T(8,128)S(1)}, f32[112,16,128]{2,1,0:T(8,128)S(1)}, u32[]{:S(2)}, u32[]{:S(2)}) collective-permute-start(f32[112,16,128]{2,1,0:T(8,128)S(1)} %get-tuple-element.48), channel_id=1, source_target_pairs={{0,1},{1,0},{2,3},{3,2},{4,5},{5,4},{6,7},{7,6},{8,9},{9,8},{10,11... | collective-permute-start | bytes 2752520 | tf_op jit(solution)/shard_map/ppermute | solution.py:695
  94.8 19.3 %collective-permute-start.13 = (f32[112,16,128]{2,1,0:T(8,128)S(1)}, f32[112,16,128]{2,1,0:T(8,128)S(1)}, u32[]{:S(2)}, u32[]{:S(2)}) collective-permute-start(f32[112,16,128]{2,1,0:T(8,128)S(1)} %get-tuple-element.50), channel_id=1, source_target_pairs={{0,4},{1,5},{2,6},{3,7},{4,0},{5,1},{6,2},{7,3},{8,12},{9,13},{10,... | collective-permute-start | bytes 2752520 | tf_op jit(solution)/shard_map/ppermute | solution.py:695
  96.0 18.0 %collective-permute-start.12 = (f32[96,16,128]{2,1,0:T(8,128)S(1)}, f32[96,16,128]{2,1,0:T(8,128)S(1)}, u32[]{:S(2)}, u32[]{:S(2)}) collective-permute-start(f32[96,16,128]{2,1,0:T(8,128)S(1)} %get-tuple-element.49), channel_id=1, source_target_pairs={{0,3},{1,2},{2,1},{3,0},{4,7},{5,6},{6,5},{7,4},{8,11},{9,10},{10,... | collective-permute-start | bytes 2359304 | tf_op jit(solution)/shard_map/ppermute | solution.py:695
  97.5 16.5 %collective-permute-start.10 = (f32[8,2,16,512]{3,2,1,0:T(8,128)S(1)}, f32[8,2,16,512]{3,2,1,0:T(8,128)S(1)}, u32[]{:S(2)}, u32[]{:S(2)}) collective-permute-start(f32[8,2,16,512]{3,2,1,0:T(8,128)S(1)} %get-tuple-element.47), channel_id=1, source_target_pairs={{0,12},{1,13},{2,14},{3,15},{4,8},{5,9},{6,10},{7,11},{8,4},{9,5},... | collective-permute-start | bytes 1572872 | tf_op jit(solution)/shard_map/ppermute | solution.py:695
  103.3 10.7 %collective-permute-start.14 = (f32[8,2,16,128]{3,2,1,0:T(8,128)S(1)}, f32[8,2,16,128]{3,2,1,0:T(8,128)S(1)}, u32[]{:S(2)}, u32[]{:S(2)}) collective-permute-start(f32[8,2,16,128]{3,2,1,0:T(8,128)S(1)} %get-tuple-element.51), channel_id=1, source_target_pairs={{0,15},{1,14},{4,11},{5,10},{16,31},{17,30},{20,27},{21,26},{32,47... | collective-permute-start | bytes 393224 | tf_op jit(solution)/shard_map/ppermute | solution.py:695
  114.0 3.5 %copy-start.6 = (f32[96,16,128]{2,1,0:T(8,128)}, f32[96,16,128]{2,1,0:T(8,128)S(1)}, u32[]{:S(2)}) copy-start(f32[96,16,128]{2,1,0:T(8,128)S(1)} %collective-permute-done.12.refs_3_.h_j0) | copy-start | bytes 2359300
  114.1 3.4 %copy-start.4 = (f32[112,16,128]{2,1,0:T(8,128)}, f32[112,16,128]{2,1,0:T(8,128)S(1)}, u32[]{:S(2)}) copy-start(f32[112,16,128]{2,1,0:T(8,128)S(1)} %collective-permute-done.13.refs_4_.h_i2) | copy-start | bytes 2752516
  117.5 0.9 copy-start.18
  118.4 30.6 %all-to-all-start.1 = ((f32[8,128,512]{2,1,0:T(8,128)}), f32[8,128,512]{2,1,0:T(8,128)S(1)}, u32[]{:S(2)}, u32[]{:S(2)}) async-start(f32[8,128,512]{2,1,0:T(8,128)} %get-tuple-element.52), calls=%async_computation.1 | async-start | bytes 4194304 | tf_op jit(solution)/shard_map/all_to_all | solution.py:686
  122.9 17.9 %collective-permute-start.15 = (f32[8,48,512]{2,1,0:T(8,128)}, f32[8,48,512]{2,1,0:T(8,128)S(1)}, u32[]{:S(2)}, u32[]{:S(2)}) collective-permute-start(f32[8,48,512]{2,1,0:T(8,128)} %copy-done.18), channel_id=1, source_target_pairs={{16,0},{32,16},{48,32},{64,48},{80,64},{96,80},{112,96},{17,1},{33... | collective-permute-start | bytes 2359304 | tf_op jit(solution)/shard_map/ppermute | solution.py:690
  128.9 1.2 copy-start.5
  130.1 1.1 copy-start.7
  131.2 1.6 copy-start.9
  132.8 1.6 copy-start.10
  150.2 23.6 %collective-permute-start.16 = (f32[8,80,512]{2,1,0:T(8,128)}, f32[8,80,512]{2,1,0:T(8,128)}, u32[]{:S(2)}, u32[]{:S(2)}) collective-permute-start(f32[8,80,512]{2,1,0:T(8,128)} %slice.6), channel_id=1, source_target_pairs={{16,0},{32,16},{48,32},{64,48},{80,64},{96,80},{112,96},{17,1},{33... | collective-permute-start | bytes 3932168 | tf_op jit(solution)/shard_map/ppermute | solution.py:690
  154.4 19.4 %all-to-all-start.2 = ((f32[8,56,512]{2,1,0:T(8,128)}), f32[8,56,512]{2,1,0:T(8,128)S(1)}, u32[]{:S(2)}, u32[]{:S(2)}) async-start(f32[8,56,512]{2,1,0:T(8,128)} %join_blocks.1), calls=%async_computation.2 | async-start | bytes 1835008 | tf_op jit(solution)/shard_map/all_to_all | solution.py:686
  173.8 8.1 %collective-permute-start.17 = (f32[8,512]{1,0:T(8,128)S(1)}, f32[8,512]{1,0:T(8,128)S(1)}, u32[]{:S(2)}, u32[]{:S(2)}) collective-permute-start(f32[8,512]{1,0:T(8,128)S(1)} %slice_reduce_fusion), channel_id=1, source_target_pairs={{0,12},{1,13},{2,14},{3,15},{4,8},{5,9},{6,10},{7,11},{8,4},{9,5},... | collective-permute-start | bytes 49160 | tf_op jit(solution)/shard_map/ppermute | solution.py:812
  177.5 1.6 copy-start.3

commit v2 on v1

--- a/solution.py
+++ b/solution.py
@@ -43,20 +43,21 @@
 class Place:
     def __init__(self):
         row = lax.axis_index("row")
-        y = row // 4
-        z = row % 4
-        self.upper = y // 2
+        y = row >> 2
+        z = row & 3
+        self.upper = y >> 1
         self.gi2 = jnp.where((y == 1) | (y == 2), 1, 0)
-        self.gj0 = z // 2
+        self.gj0 = z >> 1
         self.gj1 = jnp.where((z == 1) | (z == 2), 1, 0)
-        gray = z ^ (z // 2)
-        self.slot = jnp.where(self.upper == 1, 4 * (3 - y) + 3 - gray, 4 * y + gray)
 
 
 def unit_at(p, i1):
-    h = i1 // 4
-    odd = p % 2
-    return ((p // 2) * 4 + jnp.where(odd == 1, 3 - h, h)) * 4 + i1 % 4
+    odd = p & 1
+    return ((p >> 1) << 4) + (((i1 >> 2) ^ (3 * odd)) << 2) + (i1 & 3)
+
+
+def wide(unit):
+    return unit + ((unit >> 2) << 2)
 
 
 def iotas():
@@ -68,13 +69,13 @@
 class Tables:
     def __init__(self, place):
         lane, sub = iotas()
-        low1 = lane // 32
+        low1 = lane >> 5
         self.j1 = (low1 + 4 * place.gj1).astype(F32)
-        self.j2 = ((lane // 4) % 8).astype(F32)
-        self.j3 = (lane % 4).astype(F32)
-        low2 = sub // 4
+        self.j2 = ((lane >> 2) & 7).astype(F32)
+        self.j3 = (lane & 3).astype(F32)
+        low2 = sub >> 2
         self.i2 = (low2 + 4 * place.gi2).astype(F32)
-        self.i3 = (sub % 4).astype(F32)
+        self.i3 = (sub & 3).astype(F32)
         self.c1p = jnp.where(low1 > 0, jnp.sqrt(self.j1), 0.0)
         self.c1m = jnp.where(low1 < 3, jnp.sqrt(self.j1 + 1.0), 0.0)
         self.c2p = jnp.sqrt(self.j2)
@@ -121,7 +122,7 @@
     return jnp.where(place.upper == 1, 7 - p, p)
 
 
-def unit_neighbours(place, roots, p, i1):
+def unit_neighbours(place, roots, p, i1, at=unit_at):
     up = place.upper == 1
     i0 = level_of(place, p)
     below = jnp.where(up, p + 1, p - 1)
@@ -130,31 +131,24 @@
     root_above = jnp.where((above >= 0) & (above <= 3), roots[0, i0 + 1], 0.0)
     return (
         i0,
-        (unit_at(jnp.clip(below, 0, 3), i1), root_below),
-        (unit_at(jnp.clip(above, 0, 3), i1), root_above),
-        (unit_at(p, jnp.maximum(i1 - 1, 0)), roots[0, i1]),
-        (unit_at(p, jnp.minimum(i1 + 1, 7)), jnp.where(i1 < 7, roots[0, i1 + 1], 0.0)),
+        (at(jnp.clip(below, 0, 3), i1), root_below),
+        (at(jnp.clip(above, 0, 3), i1), root_above),
+        (at(p, jnp.maximum(i1 - 1, 0)), roots[0, i1]),
+        (at(p, jnp.minimum(i1 + 1, 7)), jnp.where(i1 < 7, roots[0, i1 + 1], 0.0)),
     )
 
 
 def local_kernel(scale, n, *refs):
-    z, base = refs[:2]
-    if n:
-        state, *received = refs[2:6]
-        *scalars, out, next_state = refs[6:15] if n == 1 else (*refs[6:14], refs[16])
-        copy_state(n - 1, state, received, next_state, lambda r: r)
-    else:
-        *scalars, out = refs[2:]
+    z, base, *scalars, out = refs[:10]
     writes = []
     if n == 2:
-        z_out, state_out = refs[14:16]
-        sems = refs[17]
-        writes = [
-            pltpu.make_async_copy(z, z_out, sems.at[0]),
-            pltpu.make_async_copy(next_state, state_out, sems.at[1]),
-        ]
+        z_out, sems = refs[10:]
+        writes = [pltpu.make_async_copy(z, z_out, sems.at[0])]
     start_all(writes)
     amp, det, anh, dec, dep, kerr, roots = scalars
+    def at(p, i1):
+        return unit_at(p, i1) if n else wide(unit_at(p, i1))
+
     place = Place()
     tb = Tables(place)
     detuning = [det[0, q] for q in range(4)]
@@ -178,11 +172,12 @@
     r2p, r3p = u[2] * tb.r2p, u[3] * tb.r3p
     d2p, d3p = decay[2] * tb.r2p, decay[3] * tb.r3p
 
-    def step(n, carry):
-        p = n // 8
-        i1 = n % 8
+    def step(unit, carry):
+        p = unit >> 3
+        i1 = unit & 7
         here = unit_at(p, i1)
-        i0, below, above, less, more = unit_neighbours(place, roots, p, i1)
+        mine = at(p, i1)
+        i0, below, above, less, more = unit_neighbours(place, roots, p, i1, at)
         i0f = i0.astype(F32)
         i1f = i1.astype(F32)
         rows = [i0f, i1f, tb.i2, tb.i3]
@@ -197,7 +192,7 @@
             sand = []
             values = []
             for c in range(2):
-                m = tile(z, here, c, t)
+                m = tile(z, mine, c, t)
                 values.append(m)
                 turned2 = pltpu.roll(m, 4, 1)
                 turned3 = pltpu.roll(m, 1, 1)
@@ -206,9 +201,9 @@
                 k = (u[0] * below[1]) * row0 + (u[0] * above[1]) * tile(z, above[0], c, t)
                 k = k + (u[1] * less[1]) * row1 + (u[1] * more[1]) * tile(z, more[0], c, t)
                 if t > 0:
-                    k = k - (u[0] * root_left) * tile(z, here, c, t - 1)
+                    k = k - (u[0] * root_left) * tile(z, mine, c, t - 1)
                 if t < TILES - 1:
-                    k = k - (u[0] * root_right) * tile(z, here, c, t + 1)
+                    k = k - (u[0] * root_right) * tile(z, mine, c, t + 1)
                 k = k + r2p * pltpu.roll(m, 4, 0) + r2m * pltpu.roll(m, ROWS - 4, 0)
                 k = k + r3p * pltpu.roll(m, 1, 0) + r3m * pltpu.roll(m, ROWS - 1, 0)
                 k = k - c1p * pltpu.roll(m, 32, 1) - c1m * pltpu.roll(m, LANES - 32, 1)
@@ -233,10 +228,10 @@
             )
             x, y = values
             lanes = slice(t * LANES, (t + 1) * LANES)
-            out[here, 0, :, lanes] = tile(base, here, 0, t) + scale * (
+            out[here, 0, :, lanes] = tile(base, wide(here), 0, t) + scale * (
                 damping * x - phase * y - comm[1] + sand[0]
             )
-            out[here, 1, :, lanes] = tile(base, here, 1, t) + scale * (
+            out[here, 1, :, lanes] = tile(base, wide(here), 1, t) + scale * (
                 damping * y + phase * x + comm[0] + sand[1]
             )
         return carry
@@ -245,46 +240,6 @@
     wait_all(writes)
 
 
-PARTS = ((0, 1, 2), (3, 4, 5), (6, 7))
-ROUTES = ((0, 1, 2), (2, 0, 1), (1, 2, 0))
-EDGE = 64
-
-
-def sent_slots(bit):
-    return [r for r in range(8) if r >> bit & 1]
-
-
-def merged_state(n, part, r):
-    bit = ROUTES[n].index(part) if n >= 0 else 0
-    if n < 0 or not r >> bit & 1:
-        return None
-    return bit, EDGE + sent_slots(bit).index(r) * len(PARTS[part]) * TILES
-
-
-def state_entry(part, r):
-    return (r * 8 + PARTS[part][0]) * TILES
-
-
-def copy_state(n, state, received, out, slots):
-    for r in range(8):
-        for part in range(3):
-            size = len(PARTS[part]) * TILES
-            found = merged_state(n, part, r)
-            source, first = (state, state_entry(part, r)) if found is None else (received[found[0]], found[1])
-            out[pl.ds(state_entry(part, slots(r)), size)] = source[first : first + size]
-
-
-def load_riders(n, state, received, carriers):
-    for bit in range(3):
-        part = ROUTES[n][bit]
-        size = len(PARTS[part]) * TILES
-        for at, r in enumerate(sent_slots(bit)):
-            found = merged_state(n - 1, part, r)
-            source, first = (state, state_entry(part, r)) if found is None else (received[found[0]], found[1])
-            start = EDGE + at * size
-            carriers[bit][start : start + size] = source[first : first + size]
-
-
 def start_all(copies):
     for copy in copies:
         copy.start()
@@ -298,7 +253,7 @@
 def put_slabs(place, tb, p, pair, both, s_i0, s_j1, s_j0, s_i2, s_c):
     lane, _ = iotas()
     half = lax.broadcasted_iota(jnp.int32, (8, LANES), 0) < 4
-    block = lane // 32
+    block = lane >> 5
     gj0 = place.gj0 == 1
     gi2 = place.gi2 == 1
     for par in range(2):
@@ -313,7 +268,7 @@
             s_j0[2 * n + c] = jnp.where(gj0, tiles[0], tiles[TILES - 1])
             packed = None
             for t in range(TILES):
-                turned = pltpu.roll(tiles[t], (32 * (t - tb.edge1)) % LANES, 1)
+                turned = pltpu.roll(tiles[t], (32 * (t - tb.edge1)) & (LANES - 1), 1)
                 packed = turned if packed is None else jnp.where(block == t, turned, packed)
             s_j1[2 * n + c] = packed
     for c in range(2):
@@ -325,15 +280,14 @@
             s_i2[entry, (t % 2) * 8 : (t % 2) * 8 + 8] = jnp.where(half, first, second)
 
 
-def slab_kernel(z, state, s_i0, s_j1, s_j0, s_i2, s_c):
+def slab_kernel(z, s_i0, s_j1, s_j0, s_i2, s_c):
     place = Place()
     tb = Tables(place)
-    load_riders(0, state, None, (s_j1, s_j0, s_i2))
     for p in range(4):
 
         def step(pair, carry, p=p):
             both = [
-                [[tile(z, unit_at(p, 2 * pair + par), c, t) for t in range(TILES)] for c in range(2)]
+                [[tile(z, wide(unit_at(p, 2 * pair + par)), c, t) for t in range(TILES)] for c in range(2)]
                 for par in range(2)
             ]
             put_slabs(place, tb, p, pair, both, s_i0, s_j1, s_j0, s_i2, s_c)
@@ -344,18 +298,17 @@
 
 def i2_halo(place, h_i2, p, pair, par, c, t):
     small = h_i2[((p * 4 + pair) * 2 + c) * 2 + t // 2, (t % 2) * 8 : (t % 2) * 8 + 8]
-    small = pltpu.roll(small, 4 * ((par + 1 + place.gi2) % 2), 0)
+    small = pltpu.roll(small, 4 * ((par + 1 + place.gi2) & 1), 0)
     return jnp.concatenate([small, small], axis=0)
 
 
-def edge_kernel(scale, sent, *refs):
-    last = sent is None
+def edge_kernel(scale, last, *refs):
     part, h_i0, h_j1, h_j0, h_i2, h_c = refs[:6]
     if last:
         amp, dec, roots, out_all, out_rest, block, sems = refs[6:]
+        later = 16 * MOST
     else:
-        state, amp, dec, roots, out, *slabs = refs[6:]
-        load_riders(sent, state, (h_j1, h_j0, h_i2), slabs[1:4])
+        amp, dec, roots, out, *slabs = refs[6:]
     place = Place()
     tb = Tables(place)
     up = place.upper == 1
@@ -386,7 +339,7 @@
         for t in range(TILES):
             j0 = 4 * place.gj0 + t
             lanes = slice(t * LANES, (t + 1) * LANES)
-            turn = (32 * (tb.edge1 - t)) % LANES
+            turn = (32 * (tb.edge1 - t)) & (LANES - 1)
             comm = []
             sand = []
             for c in range(2):
@@ -432,36 +385,34 @@
                     for t in range(TILES):
                         lanes = slice(t * LANES, (t + 1) * LANES)
                         at = (2 * a + c) * ROWS
-                        block[here // 4, at : at + ROWS, lanes] = new[c][t]
-                        if 2 * a + c >= MOST:
-                            at -= MOST * ROWS
-                            out_rest[here // 4, at : at + ROWS, lanes] = new[c][t]
+                        block[here >> 2, at : at + ROWS, lanes] = new[c][t]
             return carry
 
         if last:
             lax.fori_loop(0, 2, last_step, 0)
             slots = pl.ds(2 * p, 2)
+            rows = pl.ds(later, 128 - later)
             copies.append(pltpu.make_async_copy(block.at[slots], out_all.at[slots], sems.at[p]))
-            copies[-1].start()
+            copies.append(pltpu.make_async_copy(block.at[slots, rows], out_rest.at[slots], sems.at[4 + p]))
+            start_all(copies[-2:])
         else:
             lax.fori_loop(0, 4, step, 0)
     wait_all(copies)
 
 
-def gradient_kernel(z_in, h_i0, state_in, h_j1, h_j0, h_i2, roots, grad, z, state, rho, sems):
-    reads = [pltpu.make_async_copy(state_in, state, sems.at[0]), pltpu.make_async_copy(z_in, z, sems.at[1])]
+def gradient_kernel(z_in, rho_in, h_i0, h_j1, h_j0, h_i2, roots, grad, z, rho, sems):
+    reads = [pltpu.make_async_copy(rho_in.at[:, pl.ds(4, 4)], rho, sems.at[0]), pltpu.make_async_copy(z_in, z, sems.at[1])]
     start_all(reads)
     place = Place()
     tb = Tables(place)
     gj0f = place.gj0.astype(F32)
     wait_all(reads)
-    copy_state(2, state, (h_j1, h_j0, h_i2), rho, lambda r: r ^ place.slot)
     k1_mask = -2.0 * tb.at1
     k2_mask = 2.0 * tb.at2
 
     def half_step(n, par, acc):
-        p = n // 4
-        pair = n % 4
+        p = n >> 2
+        pair = n & 3
         i1 = 2 * pair + par
         unit = p * 8 + i1
         here = unit_at(p, i1)
@@ -469,7 +420,7 @@
         outer = jnp.where(p == 3, 2.0, 0.0)
         for t in range(TILES):
             j0 = 4 * place.gj0 + t
-            turn = (32 * (tb.edge1 - t)) % LANES
+            turn = (32 * (tb.edge1 - t)) & (LANES - 1)
             for c in range(2):
                 m = tile(z, here, c, t)
                 k0 = below[1] * tile(z, below[0], c, t) + above[1] * tile(z, above[0], c, t)
@@ -489,7 +440,7 @@
                 k2 = k2 + k2_mask * i2_halo(place, h_i2, p, pair, par, c, t)
                 k3 = tb.r3p * pltpu.roll(m, 1, 0) + tb.r3m * pltpu.roll(m, ROWS - 1, 0)
                 k3 = k3 - tb.c3p * pltpu.roll(m, 1, 1) - tb.c3m * pltpu.roll(m, LANES - 1, 1)
-                other = rho[(2 * here + 1 - c) * TILES + t]
+                other = rho[here >> 2, here & 3, 1 - c, :, t * LANES : (t + 1) * LANES]
                 if c == 1:
                     other = -other
                 acc = [acc[q] + k * other for q, k in enumerate((k0, k1, k2, k3))]
@@ -515,38 +466,28 @@
     return pl.ds(32 * a, 32)
 
 
-def pack_kernel(x, out, plain, block, sems):
-    upper = lax.axis_index("row") // 8
-    reads = [
-        pltpu.make_async_copy(x.at[:, slice_rows(a)], plain.at[:, slice_rows(a)], sems.at[a]) for a in range(4)
-    ]
-    writes = [pltpu.make_async_copy(block.at[:, a], out.at[:, a], sems.at[4 + a]) for a in range(4)]
+def pack_kernel(adjoint, state, out, plain, block, sems):
+    upper = lax.axis_index("row") >> 3
+    reads = []
+    for m, x in enumerate((adjoint, state)):
+        for a in range(4):
+            rows = slice_rows(a)
+            reads.append(pltpu.make_async_copy(x.at[:, rows], plain.at[m, :, rows], sems.at[4 * m + a]))
+    writes = [pltpu.make_async_copy(block.at[:, at], out.at[:, at], sems.at[8 + at]) for at in range(8)]
     start_all(reads)
-    for a in range(4):
-        reads[a].wait()
+    for at in range(8):
+        m, a = at // 4, at % 4
+        reads[at].wait()
         for gi2 in range(2):
             for g in range(4):
                 k = 4 * gi2 + jnp.where(upper == 1, 3 - g, g)
                 for c in range(2):
                     for t in range(TILES):
-                        block[k, a, c, :, t * LANES : (t + 1) * LANES] = plain[
-                            c, 32 * a + 16 * gi2 : 32 * a + 16 * gi2 + 16, chunk_lanes(g, t)
+                        block[k, at, c, :, t * LANES : (t + 1) * LANES] = plain[
+                            m, c, 32 * a + 16 * gi2 : 32 * a + 16 * gi2 + 16, chunk_lanes(g, t)
                         ]
-        writes[a].start()
+        writes[at].start()
     wait_all(writes)
-
-
-def deal_kernel(x, state):
-    place = Place()
-    for gi2 in range(2):
-        for g in range(4):
-            k = 4 * gi2 + jnp.where(place.upper == 1, 3 - g, g)
-            r = k ^ place.slot
-            for a in range(4):
-                rows = slice(a * 32 + gi2 * 16, a * 32 + gi2 * 16 + 16)
-                for c in range(2):
-                    for t in range(TILES):
-                        state[(r * 8 + a * 2 + c) * TILES + t] = x[c, rows, chunk_lanes(g, t)]
 
 
 def join_kernel(blocks, grad, out, sems):
@@ -573,7 +514,7 @@
 
 
 def start_kernel(blocks, start, held, plain, sems):
-    upper = lax.axis_index("row") // 8
+    upper = lax.axis_index("row") >> 3
     reads = [
         pltpu.make_async_copy(blocks.at[:, pl.ds(32 * a, 32)], held.at[:, pl.ds(32 * a, 32)], sems.at[a])
         for a in range(4)
@@ -592,7 +533,7 @@
 
 
 def finish_kernel(most, rest, base, defect, held_most, held_rest, held_base, plain, sems):
-    upper = lax.axis_index("row") // 8
+    upper = lax.axis_index("row") >> 3
     rows = 16 * (8 - MOST)
     reads = [
         pltpu.make_async_copy(rest.at[:, pl.ds(0, rows)], held_rest, sems.at[0]),
@@ -629,8 +570,7 @@
 PARAMS = pltpu.CompilerParams(vmem_limit_bytes=16 * 1024 * 1024)
 MOST = 5
 UNIT_SHAPE = (UNITS, 2, ROWS, WIDTH)
-PACKED_SHAPE = (8, 4, 2, ROWS, WIDTH)
-STATE_SHAPE = (64 * TILES, ROWS, LANES)
+PACKED_SHAPE = (8, 8, 2, ROWS, WIDTH)
 PLAIN_SHAPE = (2, 128, ORDER)
 BLOCKS_SHAPE = (8, 128, WIDTH)
 MOST_SHAPE = (8, 16 * MOST, WIDTH)
@@ -638,13 +578,7 @@
 JOINED_SHAPE = (8, 16 * (8 - MOST) + 8, WIDTH)
 
 
-def slab_shapes(n):
-    riders = [4 * len(PARTS[ROUTES[n][bit]]) * TILES for bit in range(3)]
-    return (
-        [(8, 2, ROWS, WIDTH)]
-        + [(EDGE + extra, ROWS, LANES) for extra in riders]
-        + [(8, 2, ROWS, LANES)]
-    )
+SLAB_SHAPES = [(8, 2, ROWS, WIDTH)] + [(64, ROWS, LANES)] * 3 + [(8, 2, ROWS, LANES)]
 
 
 def shape(dims):
@@ -682,6 +616,19 @@
     return pltpu.HBM(dims, F32)
 
 
+def pack(adjoint, state):
+    (packed,) = call(
+        pack_kernel,
+        [hbm(PACKED_SHAPE)],
+        [in_hbm(adjoint), in_hbm(state)],
+        specs=[ANY, ANY],
+        out_specs=[ANY],
+        scratch=[room((2, *PLAIN_SHAPE)), room(PACKED_SHAPE), copies(16)],
+        name="pack_blocks",
+    )
+    return packed
+
+
 def regroup(x):
     return lax.all_to_all(x, "row", 0, 0, axis_index_groups=GROUPS, tiled=True)
 
@@ -690,8 +637,7 @@
     return lax.ppermute(x, "seg", [(i + 1, i) for i in range(7)])
 
 
-def exchange(slabs):
-    perms = (PERM_I0, PERM_J1, PERM_J0, PERM_I2, PERM_CORNER)
+def exchange(slabs, perms):
     return [lax.ppermute(s, "row", perm) for s, perm in zip(slabs, perms)]
 
 
@@ -711,58 +657,43 @@
     full = (amp, detuning[None], anharmonicity[None], dec, dephasing[None], cross_kerr[None], roots)
     few = (amp, dec, roots)
     terminal = terminal_adjoint[0]
-    (packed,) = call(
-        pack_kernel,
-        [hbm(PACKED_SHAPE)],
-        [in_hbm(terminal)],
-        specs=[ANY],
-        out_specs=[ANY],
-        scratch=[room(PLAIN_SHAPE), room(PACKED_SHAPE), copies(8)],
-        name="pack_blocks",
-    )
-    base = regroup(packed).reshape(UNIT_SHAPE)
-    (state,) = call(deal_kernel, [STATE_SHAPE], [midpoint_state[0, 0]], name="deal_state")
-    slabs = call(
-        slab_kernel, slab_shapes(0), [base, state], name="slabs"
-    )
+    both = regroup(pack(terminal, midpoint_state[0, 0]))
+    base = both.reshape(2 * UNITS, 2, ROWS, WIDTH)
+    slabs = call(slab_kernel, SLAB_SHAPES, [base], name="slabs")
     current = base
     for n in range(3):
         scale = STEP if n == 2 else 0.5 * STEP
-        before = halos[1:4] if n else []
-        halos = exchange(slabs)
-        results = call(
+        halos = exchange(slabs, (PERM_I0, PERM_J1, PERM_J0, PERM_I2, PERM_CORNER))
+        part, *middle = call(
             lambda *refs, n=n, scale=scale: local_kernel(scale, n, *refs),
-            [UNIT_SHAPE] + [[], [STATE_SHAPE], [hbm(UNIT_SHAPE), hbm(STATE_SHAPE)]][n],
-            [current, base] + ([state, *before] if n else []),
+            [UNIT_SHAPE] + [hbm(UNIT_SHAPE)] * (n == 2),
+            [current, base],
             full,
             flops=30 << 20,
             size=6 << 20,
-            out_specs=[VMEM] + [[], [VMEM], [ANY, ANY]][n],
-            scratch=[room(STATE_SHAPE), copies(2)] if n == 2 else [],
+            out_specs=[VMEM] + [ANY] * (n == 2),
+            scratch=[copies(1)] if n == 2 else [],
             name="local_terms",
         )
-        part = results[0]
-        if n:
-            *middle, state = results[1:]
         if n < 2:
             current, *slabs = call(
-                lambda *refs, n=n, scale=scale: edge_kernel(scale, n + 1, *refs),
-                [UNIT_SHAPE, *slab_shapes(n + 1)],
-                [part, *halos, state],
+                lambda *refs, scale=scale: edge_kernel(scale, False, *refs),
+                [UNIT_SHAPE, *SLAB_SHAPES],
+                [part, *halos],
                 few,
                 flops=5 << 20,
                 size=8 << 20,
                 name="edge_terms",
             )
     final, rest = call(
-        lambda *refs: edge_kernel(STEP, None, *refs),
-        [hbm(BLOCKS_SHAPE), REST_SHAPE],
+        lambda *refs: edge_kernel(STEP, True, *refs),
+        [hbm(BLOCKS_SHAPE), hbm(REST_SHAPE)],
         [part, *halos],
         few,
         flops=5 << 20,
         size=6 << 20,
-        out_specs=[ANY, VMEM],
-        scratch=[room(BLOCKS_SHAPE), copies(4)],
+        out_specs=[ANY, ANY],
+        scratch=[room(BLOCKS_SHAPE), copies(8)],
         name="edge_terms",
     )
     here = regroup(final)
@@ -770,14 +701,15 @@
     (grad,) = call(
         gradient_kernel,
         [(8, WIDTH)],
-        [*middle, halos[0], state, *halos[1:4]],
+        [*middle, both, *halos[:4]],
         (roots,),
         flops=30 << 20,
         size=6 << 20,
-        specs=[ANY, VMEM, ANY, VMEM, VMEM, VMEM],
-        scratch=[room(UNIT_SHAPE), room(STATE_SHAPE), room(STATE_SHAPE), copies(2)],
+        specs=[ANY] * 2 + [VMEM] * 4,
+        scratch=[room(UNIT_SHAPE), room((8, 4, 2, ROWS, WIDTH)), copies(2)],
         name="gradient",
     )
+    grad = grad + lax.ppermute(grad, "row", PERM_I0)
     (joined,) = call(
         join_kernel,
         [hbm(JOINED_SHAPE)],
@@ -802,15 +734,14 @@
     (defect,) = call(
         finish_kernel,
         [hbm(PLAIN_SHAPE)],
-        [most_next, rest_here, terminal],
+        [most_next, rest_here, in_hbm(terminal)],
         specs=[ANY] * 3,
         out_specs=[ANY],
         scratch=[room(MOST_SHAPE), room(REST_SHAPE), room(PLAIN_SHAPE), room(PLAIN_SHAPE), copies(10)],
         name="defect_rows",
     )
-    grad = jnp.sum(rest_here[:, 16 * (8 - MOST) :], axis=0)
-    grad = grad + lax.ppermute(grad, "row", PERM_I0)
-    totals = jnp.sum(grad.reshape(8, 4, LANES), axis=(0, 2)) / ORDER
+    sums = rest_here[:, 16 * (8 - MOST) :].reshape(8, 8, 4, LANES)
+    totals = jnp.sum(sums, axis=(0, 1, 3)) / ORDER
     return start[None], defect[None], totals[None, None]
 
 

time: 183 us -> 176 us (0.962)
  blocking collectives: 0 us -> 55 us
  waiting for transfers between devices: 54.7 us -> 15.3 us
  starting transfers between devices: 59.5 us -> 46.1 us
  local copies, waits for them, and re-layouts: 13.7 us -> 7.11 us
  Pallas kernels: 53 us -> 50.6 us
    all_to_all x0 -> x1, blocking collectives: none -> 55 us  [regroup(): return lax.all_to_all(x, 'row', 0, 0, axis_index_groups=GROUPS, tiled=True)]
    all_to_all x3 -> x2, waiting for transfers between devices: 43.8 us -> 13.2 us  [regroup(): return lax.all_to_all(x, 'row', 0, 0, axis_index_groups=GROUPS, tiled=True)]
    ppermute x15, waiting for transfers between devices: 11 us -> 0.04 us  [exchange(): return [lax.ppermute(s, 'row', perm) for s, perm in zip(slabs, perms)]]
    all_to_all x3 -> x2, starting transfers between devices: 16 us -> 8 us  [regroup(): return lax.all_to_all(x, 'row', 0, 0, axis_index_groups=GROUPS, tiled=True)]
    unnamed x38 -> x28, local copies, waits for them, and re-layouts: 12.5 us -> 5.9 us
    ppermute x15, starting transfers between devices: 29.8 us -> 23.3 us  [exchange(): return [lax.ppermute(s, 'row', perm) for s, perm in zip(slabs, perms)]]
    ppermute x2, starting transfers between devices: 10.1 us -> 12.6 us  [earlier(): return lax.ppermute(x, 'seg', [(i + 1, i) for i in range(7)])]
    pallas_call x13 -> x12, Pallas kernels: 53 us -> 50.6 us  [call(): pl.pallas_call(kernel, out_shape=out_shape, in_specs=(specs or [VMEM] * l...]
  transfers between devices with their start and end apart: 21 -> 20, of which waited for: 12 -> 2; matrix products, arithmetic and copies ran while one was open for 0% -> 0% of each run, Pallas kernels for 20% -> 17%
where the time goes in v2:
time: 176 us
  blocking collectives  55 us (31%)
  Pallas kernels  50.6 us (29%)
  starting transfers between devices  46.1 us (26%)
  waiting for transfers between devices  15.3 us (9%)
  local copies, waits for them, and re-layouts  7.11 us (4%)
    all_to_all x1, blocking collectives, regroup(): return lax.all_to_all(x, 'row', 0, 0, axis_index_groups=GROUPS, tiled=True)  55 us
    pallas_call x12, Pallas kernels, call(): pl.pallas_call(kernel, out_shape=out_shape, in_specs=(specs or [VMEM] * l...  50.6 us
    ppermute x15, starting transfers between devices, exchange(): return [lax.ppermute(s, 'row', perm) for s, perm in zip(slabs, perms)]  23.3 us
    all_to_all x2, waiting for transfers between devices, regroup(): return lax.all_to_all(x, 'row', 0, 0, axis_index_groups=GROUPS, tiled=True)  13.2 us
    ppermute x2, starting transfers between devices, earlier(): return lax.ppermute(x, 'seg', [(i + 1, i) for i in range(7)])  12.6 us
    all_to_all x2, starting transfers between devices, regroup(): return lax.all_to_all(x, 'row', 0, 0, axis_index_groups=GROUPS, tiled=True)  8 us
    unnamed x28, local copies, waits for them, and re-layouts  5.9 us
  transfers between devices with their start and end apart: 20, of which 2 were waited for; matrix products, arithmetic and copies ran while one was open for 0% of the time, Pallas kernels for 17%

profile of v2, /device:TPU:1, one launch (start us, length us, event | category | flops | bytes accessed | tf_op | source)
XLA Modules:
  0.0 175.8 jit_solution(7425858503469216295)
XLA Ops:
  0.6 3.5 %pack_blocks.1 = f32[8,8,2,16,512]{4,3,2,1,0:T(8,128)} custom-call(f32[2,128,2048]{2,1,0:T(8,128)} %bitcast.44, f32[2,128,2048]{2,1,0:T(8,128)} %bitcast.48), custom_call_target="tpu_custom_call" | custom-call | bytes 4194304 | tf_op jit(solution)/shard_map/pack_blocks/pallas_call | solution.py:598
  4.2 55.0 %all_to_all.15.rho_in = f32[8,8,2,16,512]{4,3,2,1,0:T(8,128)S(1)} all-to-all(f32[8,8,2,16,512]{4,3,2,1,0:T(8,128)} %pack_blocks.1), channel_id=1, replica_groups={{0,1,3,2,4,5,7,6},{14,15,13,12,10,11,9,8},{16,17,19,18,20,21,23,22},{30..., dimensions={0} | all-to-all | bytes 8388608 | tf_op jit(solution)/shard_map/all_to_all | solution.py:633
  59.2 0.0 copy-start.10
  59.2 0.0 copy-start.11
  59.2 0.0 copy-start.12
  59.2 0.0 copy-start.13
  59.2 1.6 slabs.1
  60.9 2.3 %collective-permute-start = (f32[8,2,16,512]{3,2,1,0:T(8,128)S(1)}, f32[8,2,16,512]{3,2,1,0:T(8,128)S(1)}, u32[]{:S(2)}, u32[]{:S(2)}) collective-permute-start(f32[8,2,16,512]{3,2,1,0:T(8,128)S(1)} %get-tuple-element.29), channel_id=1, source_target_pairs={{0,12},{1,13},{2,14},{3,15},{4,8},{5,9},{6,10},{7,11},{8,4},{9,5},... | collective-permute-start | bytes 1572872 | tf_op jit(solution)/shard_map/ppermute | solution.py:641
  63.2 2.2 %collective-permute-start.2 = (f32[64,16,128]{2,1,0:T(8,128)S(1)}, f32[64,16,128]{2,1,0:T(8,128)S(1)}, u32[]{:S(2)}, u32[]{:S(2)}) collective-permute-start(f32[64,16,128]{2,1,0:T(8,128)S(1)} %get-tuple-element.31), channel_id=1, source_target_pairs={{0,3},{1,2},{2,1},{3,0},{4,7},{5,6},{6,5},{7,4},{8,11},{9,10},{10,... | collective-permute-start | bytes 1572872 | tf_op jit(solution)/shard_map/ppermute | solution.py:641
  65.4 0.5 collective-permute-start.3
  65.8 2.9 %collective-permute-start.4 = (f32[8,2,16,128]{3,2,1,0:T(8,128)S(1)}, f32[8,2,16,128]{3,2,1,0:T(8,128)S(1)}, u32[]{:S(2)}, u32[]{:S(2)}) collective-permute-start(f32[8,2,16,128]{3,2,1,0:T(8,128)S(1)} %get-tuple-element.33), channel_id=1, source_target_pairs={{0,15},{1,14},{4,11},{5,10},{16,31},{17,30},{20,27},{21,26},{32,47... | collective-permute-start | bytes 393224 | tf_op jit(solution)/shard_map/ppermute | solution.py:641
  68.8 7.6 %local_terms.3.refs_0_ = f32[32,2,16,512]{3,2,1,0:T(8,128)S(1)} custom-call(f32[64,2,16,512]{3,2,1,0:T(8,128)S(1)} %bitcast.16, f32[64,2,16,512]{3,2,1,0:T(8,128)S(1)} %bitcast.17, f32[1,4]{1,0:T(1,128)S(1)} %bitcast.20, f32[1,4]{1,0:T(1,128)S(1)} %bitcast.32, f32[1,4]{1,0:T(1,128)S(1)} %bitcast.35, f32[1,4]{1,0:T(1,128)S(1)} %bitcast.26, ...), custom_call_target="tpu_custom_call" | custom-call | flops 31457280 | bytes 6291456 | tf_op jit(solution)/shard_map/local_terms/pallas_call | solution.py:598
  76.4 0.0 collective-permute-done.4.refs_5_
  76.4 0.0 collective-permute-done.refs_1_
  76.4 0.0 collective-permute-done.2.refs_3_
  76.4 4.2 %edge_terms.3 = (f32[32,2,16,512]{3,2,1,0:T(8,128)S(1)}, f32[8,2,16,512]{3,2,1,0:T(8,128)S(1)}, f32[64,16,128]{2,1,0:T(8,128)S(1)}, f32[64,16,128]{2,1,0:T(8,128...) custom-call(f32[32,2,16,512]{3,2,1,0:T(8,128)S(1)} %local_terms.3.refs_0_, ...), custom_call_target="tpu_custom_call" | custom-call | flops 5242880 | bytes 8388608 | tf_op jit(solution)/shard_map/edge_terms/pallas_call | solution.py:598
  80.6 0.1 collective-permute-start.5
  80.7 0.2 collective-permute-start.6
  81.0 4.5 %collective-permute-start.7 = (f32[64,16,128]{2,1,0:T(8,128)S(1)}, f32[64,16,128]{2,1,0:T(8,128)S(1)}, u32[]{:S(2)}, u32[]{:S(2)}) collective-permute-start(f32[64,16,128]{2,1,0:T(8,128)S(1)} %get-tuple-element.37), channel_id=1, source_target_pairs={{0,3},{1,2},{2,1},{3,0},{4,7},{5,6},{6,5},{7,4},{8,11},{9,10},{10,... | collective-permute-start | bytes 1572872 | tf_op jit(solution)/shard_map/ppermute | solution.py:641
  85.5 0.4 collective-permute-start.8
  85.9 2.5 %collective-permute-start.9 = (f32[8,2,16,128]{3,2,1,0:T(8,128)S(1)}, f32[8,2,16,128]{3,2,1,0:T(8,128)S(1)}, u32[]{:S(2)}, u32[]{:S(2)}) collective-permute-start(f32[8,2,16,128]{3,2,1,0:T(8,128)S(1)} %get-tuple-element.39), channel_id=1, source_target_pairs={{0,15},{1,14},{4,11},{5,10},{16,31},{17,30},{20,27},{21,26},{32,47... | collective-permute-start | bytes 393224 | tf_op jit(solution)/shard_map/ppermute | solution.py:641
  88.4 7.2 %local_terms.4.refs_0_ = f32[32,2,16,512]{3,2,1,0:T(8,128)S(1)} custom-call(f32[32,2,16,512]{3,2,1,0:T(8,128)S(1)} %get-tuple-element.34.refs_0_, f32[64,2,16,512]{3,2,1,0:T(8,128)S(1)} %bitcast.18, f32[1,4]{1,0:T(1,128)S(1)} %bitcast.22, f32[1,4]{1,0:T(1,128)S(1)} %bitcast.33, f32[1,4]{1,0:T(1,128)S(1)} %bitcast.36, f32[1,4]{1,0:T(1,128)S(1)} %bitcast.28, ...), custom_call_target="tpu_custom_call" | custom-call | flops 31457280 | bytes 6291456 | tf_op jit(solution)/shard_map/local_terms/pallas_call | solution.py:598
  95.6 4.2 %edge_terms.4 = (f32[32,2,16,512]{3,2,1,0:T(8,128)S(1)}, f32[8,2,16,512]{3,2,1,0:T(8,128)S(1)}, f32[64,16,128]{2,1,0:T(8,128)S(1)}, f32[64,16,128]{2,1,0:T(8,128...) custom-call(f32[32,2,16,512]{3,2,1,0:T(8,128)S(1)} %local_terms.4.refs_0_, ...), custom_call_target="tpu_custom_call" | custom-call | flops 5242880 | bytes 8388608 | tf_op jit(solution)/shard_map/edge_terms/pallas_call | solution.py:598
  99.8 0.4 collective-permute-start.10
  100.2 0.6 collective-permute-start.11
  100.8 2.3 %collective-permute-start.12 = (f32[64,16,128]{2,1,0:T(8,128)S(1)}, f32[64,16,128]{2,1,0:T(8,128)S(1)}, u32[]{:S(2)}, u32[]{:S(2)}) collective-permute-start(f32[64,16,128]{2,1,0:T(8,128)S(1)} %get-tuple-element.44), channel_id=1, source_target_pairs={{0,3},{1,2},{2,1},{3,0},{4,7},{5,6},{6,5},{7,4},{8,11},{9,10},{10,... | collective-permute-start | bytes 1572872 | tf_op jit(solution)/shard_map/ppermute | solution.py:641
  103.1 0.5 collective-permute-start.13
  103.7 3.9 %collective-permute-start.14 = (f32[8,2,16,128]{3,2,1,0:T(8,128)S(1)}, f32[8,2,16,128]{3,2,1,0:T(8,128)S(1)}, u32[]{:S(2)}, u32[]{:S(2)}) collective-permute-start(f32[8,2,16,128]{3,2,1,0:T(8,128)S(1)} %get-tuple-element.46), channel_id=1, source_target_pairs={{0,15},{1,14},{4,11},{5,10},{16,31},{17,30},{20,27},{21,26},{32,47... | collective-permute-start | bytes 393224 | tf_op jit(solution)/shard_map/ppermute | solution.py:641
  107.6 7.2 %local_terms.5 = (f32[32,2,16,512]{3,2,1,0:T(8,128)S(1)}, f32[32,2,16,512]{3,2,1,0:T(8,128)}) custom-call(f32[32,2,16,512]{3,2,1,0:T(8,128)S(1)} %get-tuple-element.40.refs_0_, f32[64,2,16,512]{3,2,1,0:T(8,128)S(1)} %bitcast.19, f32[1,4]{1,0:T(1,128)S(1)} %bitcast.24, f32[1,4]{1,0:T(1,128)S(1)} %bitcast.34, f32[1,4]{1,0:T(1,128)S(1)} %bitcast.37, ...), custom_call_target="tpu_custom_call" | custom-call | flops 31457280 | bytes 6291456 | tf_op jit(solution)/shard_map/local_terms/pallas_call | solution.py:598
  114.9 3.4 %edge_terms.5 = (f32[8,128,512]{2,1,0:T(8,128)}, f32[8,48,512]{2,1,0:T(8,128)}) custom-call(f32[32,2,16,512]{3,2,1,0:T(8,128)S(1)} %get-tuple-element.41.refs_0_, f32[8,2,16,512]{3,2,1,0:T(8,128)S(1)} %collective-permute-done.10.refs_1_.h_i0, f32[64,16,128]{2,1,0:T(8,128)S(1)} %collective-permute-done.11.refs_2_.h_j1, ...), custom_call_target="tpu_custom_call" | custom-call | flops 5242880 | bytes 6291456 | tf_op jit(solution)/shard_map/edge_terms/pallas_call | solution.py:598
  118.4 3.6 %all-to-all-start.1 = ((f32[8,128,512]{2,1,0:T(8,128)}), f32[8,128,512]{2,1,0:T(8,128)S(1)}, u32[]{:S(2)}, u32[]{:S(2)}) async-start(f32[8,128,512]{2,1,0:T(8,128)} %get-tuple-element.47), calls=%async_computation.1 | async-start | bytes 4194304 | tf_op jit(solution)/shard_map/all_to_all | solution.py:633
  122.0 7.5 %collective-permute-start.15 = (f32[8,48,512]{2,1,0:T(8,128)}, f32[8,48,512]{2,1,0:T(8,128)S(1)}, u32[]{:S(2)}, u32[]{:S(2)}) collective-permute-start(f32[8,48,512]{2,1,0:T(8,128)} %get-tuple-element.48), channel_id=1, source_target_pairs={{16,0},{32,16},{48,32},{64,48},{80,64},{96,80},{112,96},{17,1},{33... | collective-permute-start | bytes 2359304 | tf_op jit(solution)/shard_map/ppermute | solution.py:637
  129.5 2.2 %copy-done.1 = f32[8,8,2,16,512]{4,3,2,1,0:T(8,128)S(1)} copy-done((f32[8,8,2,16,512]{4,3,2,1,0:T(8,128)S(1)}, f32[8,8,2,16,512]{4,3,2,1,0:T(8,128)}, u32[]{:S(2)}) %copy-start.1) | copy-done | bytes 4194328
  131.7 1.0 copy-done.3
  132.7 1.0 copy-done.5
  133.7 1.6 copy-done.6
  135.3 6.1 %gradient.1 = f32[8,512]{1,0:T(8,128)S(1)} custom-call(f32[32,2,16,512]{3,2,1,0:T(8,128)S(1)} %copy-done.6, f32[8,8,2,16,512]{4,3,2,1,0:T(8,128)S(1)} %copy-done.1, f32[8,2,16,512]{3,2,1,0:T(8,128)S(1)} %collective-permute-done.10.refs_1_.h_i0, f32[64,16,128]{2,1,0:T(8,128)S(1)} %collective-permute-done.11.refs_2_.h_j1, f32[64,16,128]{2,1,0:T(8,128)S(1)} %copy-done.3, ...), custom_call_target="tpu_custom_call" | custom-call | flops 31457280 | bytes 6291456 | tf_op jit(solution)/shard_map/gradient/pallas_call | solution.py:598
  141.4 2.2 %collective-permute-start.16 = (f32[8,512]{1,0:T(8,128)S(1)}, f32[8,512]{1,0:T(8,128)S(1)}, u32[]{:S(2)}, u32[]{:S(2)}) collective-permute-start(f32[8,512]{1,0:T(8,128)S(1)} %gradient.1), channel_id=1, source_target_pairs={{0,12},{1,13},{2,14},{3,15},{4,8},{5,9},{6,10},{7,11},{8,4},{9,5},... | collective-permute-start | bytes 49160 | tf_op jit(solution)/shard_map/ppermute | solution.py:712
  143.6 2.0 %collective-permute-done.16 = f32[8,512]{1,0:T(8,128)S(1)} collective-permute-done((f32[8,512]{1,0:T(8,128)S(1)}, f32[8,512]{1,0:T(8,128)S(1)}, u32[]{:S(2)}, u32[]{:S(2)}) %collective-permute-start.16) | collective-permute-done | bytes 16416 | tf_op jit(solution)/shard_map/ppermute | solution.py:712
  145.6 1.0 join_blocks.1
  146.7 1.2 slice.6
  147.9 5.1 %collective-permute-start.17 = (f32[8,80,512]{2,1,0:T(8,128)}, f32[8,80,512]{2,1,0:T(8,128)}, u32[]{:S(2)}, u32[]{:S(2)}) collective-permute-start(f32[8,80,512]{2,1,0:T(8,128)} %slice.6), channel_id=1, source_target_pairs={{16,0},{32,16},{48,32},{64,48},{80,64},{96,80},{112,96},{17,1},{33... | collective-permute-start | bytes 3932168 | tf_op jit(solution)/shard_map/ppermute | solution.py:637
  153.0 4.4 %all-to-all-start.2 = ((f32[8,56,512]{2,1,0:T(8,128)}), f32[8,56,512]{2,1,0:T(8,128)S(1)}, u32[]{:S(2)}, u32[]{:S(2)}) async-start(f32[8,56,512]{2,1,0:T(8,128)} %join_blocks.1), calls=%async_computation.2 | async-start | bytes 1835008 | tf_op jit(solution)/shard_map/all_to_all | solution.py:633
  157.4 1.6 start_rows.1
  159.0 13.2 %all-to-all-done.2.rest = f32[8,56,512]{2,1,0:T(8,128)S(1)} async-done(((f32[8,56,512]{2,1,0:T(8,128)}), f32[8,56,512]{2,1,0:T(8,128)S(1)}, u32[]{:S(2)}, u32[]{:S(2)}) %all-to-all-start.2) | async-done | bytes 917536 | tf_op jit(solution)/shard_map/all_to_all | solution.py:633
  172.2 2.9 %defect_rows.1 = f32[2,128,2048]{2,1,0:T(8,128)} custom-call(f32[8,80,512]{2,1,0:T(8,128)} %collective-permute-done.17.most, f32[8,56,512]{2,1,0:T(8,128)S(1)} %all-to-all-done.2.rest, f32[2,128,2048]{2,1,0:T(8,128)} %bitcast.45), custom_call_target="tpu_custom_call" | custom-call | bytes 4194304 | tf_op jit(solution)/shard_map/defect_rows/pallas_call | solution.py:598
  175.2 0.1 bitcast_reduce_fusion
  175.3 0.5 multiply_bitcast_fusion
  (38 shorter events, 0.1 us)
Async XLA Ops:
  59.2 48.4 %copy-start = (f32[8,8,2,16,512]{4,3,2,1,0:T(8,128)}, f32[8,8,2,16,512]{4,3,2,1,0:T(8,128)S(1)}, u32[]{:S(2)}) copy-start(f32[8,8,2,16,512]{4,3,2,1,0:T(8,128)S(1)} %all_to_all.15.rho_in) | copy-start | bytes 12582916
  59.2 9.6 %copy-start.7 = (f32[1,16]{1,0:T(1,128)S(1)}, f32[1,16]{1,0:T(1,128)}, u32[]{:S(2)}) copy-start(f32[1,16]{1,0:T(1,128)} %constant.11.refs_8_.roots) | copy-start | bytes 196
  59.2 9.6 %copy-start.8 = (f32[1,1,4]{2,1,0:T(1,128)S(1)}, f32[1,1,4]{2,1,0:T(1,128)}, u32[]{:S(2)}) copy-start(f32[1,1,4]{2,1,0:T(1,128)} %param.11) | copy-start | bytes 52
  59.2 9.6 %copy-start.9 = (f32[4]{0:T(128)S(1)}, f32[4]{0:T(128)}, u32[]{:S(2)}) copy-start(f32[4]{0:T(128)} %param.14) | copy-start | bytes 52
  59.2 9.6 %copy-start.10 = (f32[4]{0:T(128)S(1)}, f32[4]{0:T(128)}, u32[]{:S(2)}) copy-start(f32[4]{0:T(128)} %param.12) | copy-start | bytes 52
  59.2 9.6 %copy-start.11 = (f32[4]{0:T(128)S(1)}, f32[4]{0:T(128)}, u32[]{:S(2)}) copy-start(f32[4]{0:T(128)} %param.13) | copy-start | bytes 52
  59.2 9.6 %copy-start.12 = (f32[4]{0:T(128)S(1)}, f32[4]{0:T(128)}, u32[]{:S(2)}) copy-start(f32[4]{0:T(128)} %param.15) | copy-start | bytes 52
  59.2 9.6 %copy-start.13 = (f32[6]{0:T(128)S(1)}, f32[6]{0:T(128)}, u32[]{:S(2)}) copy-start(f32[6]{0:T(128)} %param.16) | copy-start | bytes 76
  60.9 15.5 %collective-permute-start = (f32[8,2,16,512]{3,2,1,0:T(8,128)S(1)}, f32[8,2,16,512]{3,2,1,0:T(8,128)S(1)}, u32[]{:S(2)}, u32[]{:S(2)}) collective-permute-start(f32[8,2,16,512]{3,2,1,0:T(8,128)S(1)} %get-tuple-element.29), channel_id=1, source_target_pairs={{0,12},{1,13},{2,14},{3,15},{4,8},{5,9},{6,10},{7,11},{8,4},{9,5},... | collective-permute-start | bytes 1572872 | tf_op jit(solution)/shard_map/ppermute | solution.py:641
  63.2 13.2 %collective-permute-start.1 = (f32[64,16,128]{2,1,0:T(8,128)S(1)}, f32[64,16,128]{2,1,0:T(8,128)S(1)}, u32[]{:S(2)}, u32[]{:S(2)}) collective-permute-start(f32[64,16,128]{2,1,0:T(8,128)S(1)} %get-tuple-element.30), channel_id=1, source_target_pairs={{0,1},{1,0},{2,3},{3,2},{4,5},{5,4},{6,7},{7,6},{8,9},{9,8},{10,11... | collective-permute-start | bytes 1572872 | tf_op jit(solution)/shard_map/ppermute | solution.py:641
  63.2 13.2 %collective-permute-start.2 = (f32[64,16,128]{2,1,0:T(8,128)S(1)}, f32[64,16,128]{2,1,0:T(8,128)S(1)}, u32[]{:S(2)}, u32[]{:S(2)}) collective-permute-start(f32[64,16,128]{2,1,0:T(8,128)S(1)} %get-tuple-element.31), channel_id=1, source_target_pairs={{0,3},{1,2},{2,1},{3,0},{4,7},{5,6},{6,5},{7,4},{8,11},{9,10},{10,... | collective-permute-start | bytes 1572872 | tf_op jit(solution)/shard_map/ppermute | solution.py:641
  65.4 11.1 %collective-permute-start.3 = (f32[64,16,128]{2,1,0:T(8,128)S(1)}, f32[64,16,128]{2,1,0:T(8,128)S(1)}, u32[]{:S(2)}, u32[]{:S(2)}) collective-permute-start(f32[64,16,128]{2,1,0:T(8,128)S(1)} %get-tuple-element.32), channel_id=1, source_target_pairs={{0,4},{1,5},{2,6},{3,7},{4,0},{5,1},{6,2},{7,3},{8,12},{9,13},{10,... | collective-permute-start | bytes 1572872 | tf_op jit(solution)/shard_map/ppermute | solution.py:641
  65.8 10.5 %collective-permute-start.4 = (f32[8,2,16,128]{3,2,1,0:T(8,128)S(1)}, f32[8,2,16,128]{3,2,1,0:T(8,128)S(1)}, u32[]{:S(2)}, u32[]{:S(2)}) collective-permute-start(f32[8,2,16,128]{3,2,1,0:T(8,128)S(1)} %get-tuple-element.33), channel_id=1, source_target_pairs={{0,15},{1,14},{4,11},{5,10},{16,31},{17,30},{20,27},{21,26},{32,47... | collective-permute-start | bytes 393224 | tf_op jit(solution)/shard_map/ppermute | solution.py:641
  80.6 14.9 %collective-permute-start.5 = (f32[8,2,16,512]{3,2,1,0:T(8,128)S(1)}, f32[8,2,16,512]{3,2,1,0:T(8,128)S(1)}, u32[]{:S(2)}, u32[]{:S(2)}) collective-permute-start(f32[8,2,16,512]{3,2,1,0:T(8,128)S(1)} %get-tuple-element.35), channel_id=1, source_target_pairs={{0,12},{1,13},{2,14},{3,15},{4,8},{5,9},{6,10},{7,11},{8,4},{9,5},... | collective-permute-start | bytes 1572872 | tf_op jit(solution)/shard_map/ppermute | solution.py:641
  80.7 14.8 %collective-permute-start.6 = (f32[64,16,128]{2,1,0:T(8,128)S(1)}, f32[64,16,128]{2,1,0:T(8,128)S(1)}, u32[]{:S(2)}, u32[]{:S(2)}) collective-permute-start(f32[64,16,128]{2,1,0:T(8,128)S(1)} %get-tuple-element.36), channel_id=1, source_target_pairs={{0,1},{1,0},{2,3},{3,2},{4,5},{5,4},{6,7},{7,6},{8,9},{9,8},{10,11... | collective-permute-start | bytes 1572872 | tf_op jit(solution)/shard_map/ppermute | solution.py:641
  81.0 14.6 %collective-permute-start.7 = (f32[64,16,128]{2,1,0:T(8,128)S(1)}, f32[64,16,128]{2,1,0:T(8,128)S(1)}, u32[]{:S(2)}, u32[]{:S(2)}) collective-permute-start(f32[64,16,128]{2,1,0:T(8,128)S(1)} %get-tuple-element.37), channel_id=1, source_target_pairs={{0,3},{1,2},{2,1},{3,0},{4,7},{5,6},{6,5},{7,4},{8,11},{9,10},{10,... | collective-permute-start | bytes 1572872 | tf_op jit(solution)/shard_map/ppermute | solution.py:641
  85.5 10.1 %collective-permute-start.8 = (f32[64,16,128]{2,1,0:T(8,128)S(1)}, f32[64,16,128]{2,1,0:T(8,128)S(1)}, u32[]{:S(2)}, u32[]{:S(2)}) collective-permute-start(f32[64,16,128]{2,1,0:T(8,128)S(1)} %get-tuple-element.38), channel_id=1, source_target_pairs={{0,4},{1,5},{2,6},{3,7},{4,0},{5,1},{6,2},{7,3},{8,12},{9,13},{10,... | collective-permute-start | bytes 1572872 | tf_op jit(solution)/shard_map/ppermute | solution.py:641
  85.9 9.7 %collective-permute-start.9 = (f32[8,2,16,128]{3,2,1,0:T(8,128)S(1)}, f32[8,2,16,128]{3,2,1,0:T(8,128)S(1)}, u32[]{:S(2)}, u32[]{:S(2)}) collective-permute-start(f32[8,2,16,128]{3,2,1,0:T(8,128)S(1)} %get-tuple-element.39), channel_id=1, source_target_pairs={{0,15},{1,14},{4,11},{5,10},{16,31},{17,30},{20,27},{21,26},{32,47... | collective-permute-start | bytes 393224 | tf_op jit(solution)/shard_map/ppermute | solution.py:641
  99.8 15.0 %collective-permute-start.10 = (f32[8,2,16,512]{3,2,1,0:T(8,128)S(1)}, f32[8,2,16,512]{3,2,1,0:T(8,128)S(1)}, u32[]{:S(2)}, u32[]{:S(2)}) collective-permute-start(f32[8,2,16,512]{3,2,1,0:T(8,128)S(1)} %get-tuple-element.42), channel_id=1, source_target_pairs={{0,12},{1,13},{2,14},{3,15},{4,8},{5,9},{6,10},{7,11},{8,4},{9,5},... | collective-permute-start | bytes 1572872 | tf_op jit(solution)/shard_map/ppermute | solution.py:641
  100.2 14.7 %collective-permute-start.11 = (f32[64,16,128]{2,1,0:T(8,128)S(1)}, f32[64,16,128]{2,1,0:T(8,128)S(1)}, u32[]{:S(2)}, u32[]{:S(2)}) collective-permute-start(f32[64,16,128]{2,1,0:T(8,128)S(1)} %get-tuple-element.43), channel_id=1, source_target_pairs={{0,1},{1,0},{2,3},{3,2},{4,5},{5,4},{6,7},{7,6},{8,9},{9,8},{10,11... | collective-permute-start | bytes 1572872 | tf_op jit(solution)/shard_map/ppermute | solution.py:641
  100.8 14.0 %collective-permute-start.12 = (f32[64,16,128]{2,1,0:T(8,128)S(1)}, f32[64,16,128]{2,1,0:T(8,128)S(1)}, u32[]{:S(2)}, u32[]{:S(2)}) collective-permute-start(f32[64,16,128]{2,1,0:T(8,128)S(1)} %get-tuple-element.44), channel_id=1, source_target_pairs={{0,3},{1,2},{2,1},{3,0},{4,7},{5,6},{6,5},{7,4},{8,11},{9,10},{10,... | collective-permute-start | bytes 1572872 | tf_op jit(solution)/shard_map/ppermute | solution.py:641
  103.1 11.8 %collective-permute-start.13 = (f32[64,16,128]{2,1,0:T(8,128)S(1)}, f32[64,16,128]{2,1,0:T(8,128)S(1)}, u32[]{:S(2)}, u32[]{:S(2)}) collective-permute-start(f32[64,16,128]{2,1,0:T(8,128)S(1)} %get-tuple-element.45), channel_id=1, source_target_pairs={{0,4},{1,5},{2,6},{3,7},{4,0},{5,1},{6,2},{7,3},{8,12},{9,13},{10,... | collective-permute-start | bytes 1572872 | tf_op jit(solution)/shard_map/ppermute | solution.py:641
  103.7 11.2 %collective-permute-start.14 = (f32[8,2,16,128]{3,2,1,0:T(8,128)S(1)}, f32[8,2,16,128]{3,2,1,0:T(8,128)S(1)}, u32[]{:S(2)}, u32[]{:S(2)}) collective-permute-start(f32[8,2,16,128]{3,2,1,0:T(8,128)S(1)} %get-tuple-element.46), channel_id=1, source_target_pairs={{0,15},{1,14},{4,11},{5,10},{16,31},{17,30},{20,27},{21,26},{32,47... | collective-permute-start | bytes 393224 | tf_op jit(solution)/shard_map/ppermute | solution.py:641
  114.9 3.5 %copy-start.2 = (f32[64,16,128]{2,1,0:T(8,128)}, f32[64,16,128]{2,1,0:T(8,128)S(1)}, u32[]{:S(2)}) copy-start(f32[64,16,128]{2,1,0:T(8,128)S(1)} %collective-permute-done.12.refs_3_.h_j0) | copy-start | bytes 1572868
  114.9 3.5 %copy-start.4 = (f32[64,16,128]{2,1,0:T(8,128)}, f32[64,16,128]{2,1,0:T(8,128)S(1)}, u32[]{:S(2)}) copy-start(f32[64,16,128]{2,1,0:T(8,128)S(1)} %collective-permute-done.13.refs_4_.h_i2) | copy-start | bytes 1572868
  118.4 28.3 %all-to-all-start.1 = ((f32[8,128,512]{2,1,0:T(8,128)}), f32[8,128,512]{2,1,0:T(8,128)S(1)}, u32[]{:S(2)}, u32[]{:S(2)}) async-start(f32[8,128,512]{2,1,0:T(8,128)} %get-tuple-element.47), calls=%async_computation.1 | async-start | bytes 4194304 | tf_op jit(solution)/shard_map/all_to_all | solution.py:633
  122.0 23.6 %collective-permute-start.15 = (f32[8,48,512]{2,1,0:T(8,128)}, f32[8,48,512]{2,1,0:T(8,128)S(1)}, u32[]{:S(2)}, u32[]{:S(2)}) collective-permute-start(f32[8,48,512]{2,1,0:T(8,128)} %get-tuple-element.48), channel_id=1, source_target_pairs={{16,0},{32,16},{48,32},{64,48},{80,64},{96,80},{112,96},{17,1},{33... | collective-permute-start | bytes 2359304 | tf_op jit(solution)/shard_map/ppermute | solution.py:637
  129.5 2.2 %copy-start.1 = (f32[8,8,2,16,512]{4,3,2,1,0:T(8,128)S(1)}, f32[8,8,2,16,512]{4,3,2,1,0:T(8,128)}, u32[]{:S(2)}) copy-start(f32[8,8,2,16,512]{4,3,2,1,0:T(8,128)} %copy-done) | copy-start | bytes 12582916
  131.7 1.0 copy-start.3
  132.7 1.0 copy-start.5
  133.7 1.6 copy-start.6
  141.4 4.2 %collective-permute-start.16 = (f32[8,512]{1,0:T(8,128)S(1)}, f32[8,512]{1,0:T(8,128)S(1)}, u32[]{:S(2)}, u32[]{:S(2)}) collective-permute-start(f32[8,512]{1,0:T(8,128)S(1)} %gradient.1), channel_id=1, source_target_pairs={{0,12},{1,13},{2,14},{3,15},{4,8},{5,9},{6,10},{7,11},{8,4},{9,5},... | collective-permute-start | bytes 49160 | tf_op jit(solution)/shard_map/ppermute | solution.py:712
  147.9 24.3 %collective-permute-start.17 = (f32[8,80,512]{2,1,0:T(8,128)}, f32[8,80,512]{2,1,0:T(8,128)}, u32[]{:S(2)}, u32[]{:S(2)}) collective-permute-start(f32[8,80,512]{2,1,0:T(8,128)} %slice.6), channel_id=1, source_target_pairs={{16,0},{32,16},{48,32},{64,48},{80,64},{96,80},{112,96},{17,1},{33... | collective-permute-start | bytes 3932168 | tf_op jit(solution)/shard_map/ppermute | solution.py:637
  153.0 19.2 %all-to-all-start.2 = ((f32[8,56,512]{2,1,0:T(8,128)}), f32[8,56,512]{2,1,0:T(8,128)S(1)}, u32[]{:S(2)}, u32[]{:S(2)}) async-start(f32[8,56,512]{2,1,0:T(8,128)} %join_blocks.1), calls=%async_computation.2 | async-start | bytes 1835008 | tf_op jit(solution)/shard_map/all_to_all | solution.py:633

commit v3 on v2

--- a/solution.py
+++ b/solution.py
@@ -236,7 +236,7 @@
             )
         return carry
 
-    lax.fori_loop(0, UNITS, step, 0)
+    lax.fori_loop(0, UNITS, step, 0, unroll=4)
     wait_all(writes)
 
 
@@ -252,7 +252,7 @@
 
 def put_slabs(place, tb, p, pair, both, s_i0, s_j1, s_j0, s_i2, s_c):
     lane, _ = iotas()
-    half = lax.broadcasted_iota(jnp.int32, (8, LANES), 0) < 4
+    half = (lax.broadcasted_iota(jnp.int32, (8, LANES), 0) >> 2) == 1 - place.gi2
     block = lane >> 5
     gj0 = place.gj0 == 1
     gi2 = place.gi2 == 1
@@ -266,18 +266,18 @@
                     s_i0[i1, c, :, t * LANES : (t + 1) * LANES] = tiles[t]
                 s_c[i1, c] = tiles[TILES - 1]
             s_j0[2 * n + c] = jnp.where(gj0, tiles[0], tiles[TILES - 1])
-            packed = None
-            for t in range(TILES):
-                turned = pltpu.roll(tiles[t], (32 * (t - tb.edge1)) & (LANES - 1), 1)
-                packed = turned if packed is None else jnp.where(block == t, turned, packed)
+            packed = tiles[0]
+            for t in range(1, TILES):
+                turned = pltpu.roll(tiles[t], 32 * t, 1)
+                packed = jnp.where(block == ((tb.edge1 + t) & 3), turned, packed)
             s_j1[2 * n + c] = packed
     for c in range(2):
         for t in range(TILES):
             even, odd = both[0][c][t], both[1][c][t]
-            first = jnp.where(gi2, even[0:8], pltpu.roll(even[8:16], 4, 0))
-            second = jnp.where(gi2, pltpu.roll(odd[0:8], 4, 0), odd[8:16])
+            stays = jnp.where(gi2, even[0:8], odd[8:16])
+            moves = pltpu.roll(jnp.where(gi2, odd[0:8], even[8:16]), 4, 0)
             entry = ((p * 4 + pair) * 2 + c) * 2 + t // 2
-            s_i2[entry, (t % 2) * 8 : (t % 2) * 8 + 8] = jnp.where(half, first, second)
+            s_i2[entry, (t % 2) * 8 : (t % 2) * 8 + 8] = jnp.where(half, stays, moves)
 
 
 def slab_kernel(z, s_i0, s_j1, s_j0, s_i2, s_c):
@@ -293,13 +293,13 @@
             put_slabs(place, tb, p, pair, both, s_i0, s_j1, s_j0, s_i2, s_c)
             return carry
 
-        lax.fori_loop(0, 4, step, 0)
+        lax.fori_loop(0, 4, step, 0, unroll=True)
 
 
 def i2_halo(place, h_i2, p, pair, par, c, t):
     small = h_i2[((p * 4 + pair) * 2 + c) * 2 + t // 2, (t % 2) * 8 : (t % 2) * 8 + 8]
-    small = pltpu.roll(small, 4 * ((par + 1 + place.gi2) & 1), 0)
-    return jnp.concatenate([small, small], axis=0)
+    turned = pltpu.roll(small, 4, 0)
+    return jnp.where(place.gi2 == par, turned, small)
 
 
 def edge_kernel(scale, last, *refs):
@@ -320,11 +320,11 @@
     decay = [scale * dec[0, q] for q in range(4)]
     u = [scale * amp[0, q] for q in range(4)]
     s1_base = (decay[1] * 2.0 * gj1f) * tb.at1
-    s2_base = (decay[2] * 2.0 * gi2f) * tb.at2 * tb.c2p
+    s2_base = ((decay[2] * 2.0 * gi2f) * tb.at2 * tb.c2p)[0:8]
     k1_mask = (-2.0 * u[1]) * tb.at1
     k2_mask = (2.0 * u[2]) * tb.at2
 
-    def one(p, pair, par):
+    def one(p, pair, par, kept):
         i0 = jnp.where(up, 7 - p, p)
         below = jnp.where(up, p + 1, p - 1)
         below_in = (below >= 0) & (below <= 3)
@@ -339,13 +339,21 @@
         for t in range(TILES):
             j0 = 4 * place.gj0 + t
             lanes = slice(t * LANES, (t + 1) * LANES)
-            turn = (32 * (tb.edge1 - t)) & (LANES - 1)
+            turn = (32 * (2 * tb.edge1 - 3 - t)) & (LANES - 1)
             comm = []
             sand = []
             for c in range(2):
                 across = i2_halo(place, h_i2, p, pair, par, c, t)
-                k = k2_mask * across + k1_mask * pltpu.roll(h_j1[2 * n + c], turn, 1)
-                s = s2_base * pltpu.roll(across, 4, 1) + s1_less * pltpu.roll(h_j1[2 * n_less + c], turn, 1)
+                own = pltpu.roll(h_j1[2 * n + c], turn, 1)
+                if par == 0:
+                    lower = pltpu.roll(h_j1[2 * n_less + c], turn, 1)
+                else:
+                    lower = kept[c, t]
+                kept[c, t] = own
+                k = k2_mask * jnp.concatenate([across, across], axis=0) + k1_mask * own
+                first = s2_base * pltpu.roll(across, 4, 1)
+                s = s1_less * lower
+                s = jnp.concatenate([s[0:8] + first, s[8:16]], axis=0)
                 if p == 3:
                     k = k + (2.0 * u[0]) * h_i0[i1, c, :, lanes]
                     if t > 0:
@@ -369,8 +377,9 @@
 
         def step(pair, carry, p=p):
             both = []
+            kept = {}
             for par in range(2):
-                here, new = one(p, pair, par)
+                here, new = one(p, pair, par, kept)
                 for c in range(2):
                     for t in range(TILES):
                         out[here, c, :, t * LANES : (t + 1) * LANES] = new[c][t]
@@ -379,8 +388,9 @@
             return carry
 
         def last_step(h, carry, p=p):
+            kept = {}
             for a in range(4):
-                here, new = one(p, 2 * h + a // 2, a % 2)
+                here, new = one(p, 2 * h + a // 2, a % 2, kept)
                 for c in range(2):
                     for t in range(TILES):
                         lanes = slice(t * LANES, (t + 1) * LANES)
@@ -389,19 +399,28 @@
             return carry
 
         if last:
-            lax.fori_loop(0, 2, last_step, 0)
+            lax.fori_loop(0, 2, last_step, 0, unroll=True)
             slots = pl.ds(2 * p, 2)
             rows = pl.ds(later, 128 - later)
             copies.append(pltpu.make_async_copy(block.at[slots], out_all.at[slots], sems.at[p]))
             copies.append(pltpu.make_async_copy(block.at[slots, rows], out_rest.at[slots], sems.at[4 + p]))
             start_all(copies[-2:])
         else:
-            lax.fori_loop(0, 4, step, 0)
+            lax.fori_loop(0, 4, step, 0, unroll=True)
     wait_all(copies)
 
 
-def gradient_kernel(z_in, rho_in, h_i0, h_j1, h_j0, h_i2, roots, grad, z, rho, sems):
-    reads = [pltpu.make_async_copy(rho_in.at[:, pl.ds(4, 4)], rho, sems.at[0]), pltpu.make_async_copy(z_in, z, sems.at[1])]
+def gradient_kernel(z_in, rho_in, i0_in, j1_in, j0_in, i2_in, roots, grad, z, rho, h_i0, h_j1, h_j0, h_i2, sems):
+    reads = []
+    for source, target in (
+        (z_in, z),
+        (rho_in.at[:, pl.ds(4, 4)], rho),
+        (i0_in, h_i0),
+        (j1_in, h_j1),
+        (j0_in, h_j0),
+        (i2_in, h_i2),
+    ):
+        reads.append(pltpu.make_async_copy(source, target, sems.at[len(reads)]))
     start_all(reads)
     place = Place()
     tb = Tables(place)
@@ -420,7 +439,7 @@
         outer = jnp.where(p == 3, 2.0, 0.0)
         for t in range(TILES):
             j0 = 4 * place.gj0 + t
-            turn = (32 * (tb.edge1 - t)) & (LANES - 1)
+            turn = (32 * (2 * tb.edge1 - 3 - t)) & (LANES - 1)
             for c in range(2):
                 m = tile(z, here, c, t)
                 k0 = below[1] * tile(z, below[0], c, t) + above[1] * tile(z, above[0], c, t)
@@ -437,7 +456,8 @@
                 k1 = k1 + k1_mask * pltpu.roll(h_j1[2 * unit + c], turn, 1)
                 k2 = tb.r2p * pltpu.roll(m, 4, 0) + tb.r2m * pltpu.roll(m, ROWS - 4, 0)
                 k2 = k2 - tb.c2p * pltpu.roll(m, 4, 1) - tb.c2m * pltpu.roll(m, LANES - 4, 1)
-                k2 = k2 + k2_mask * i2_halo(place, h_i2, p, pair, par, c, t)
+                across = i2_halo(place, h_i2, p, pair, par, c, t)
+                k2 = k2 + k2_mask * jnp.concatenate([across, across], axis=0)
                 k3 = tb.r3p * pltpu.roll(m, 1, 0) + tb.r3m * pltpu.roll(m, ROWS - 1, 0)
                 k3 = k3 - tb.c3p * pltpu.roll(m, 1, 1) - tb.c3m * pltpu.roll(m, LANES - 1, 1)
                 other = rho[here >> 2, here & 3, 1 - c, :, t * LANES : (t + 1) * LANES]
@@ -452,7 +472,8 @@
             acc = half_step(n, par, acc)
         return tuple(acc)
 
-    total = lax.fori_loop(0, UNITS // 2, step, tuple(jnp.zeros((ROWS, LANES), F32) for _ in range(4)))
+    start = tuple(jnp.zeros((ROWS, LANES), F32) for _ in range(4))
+    total = lax.fori_loop(0, UNITS // 2, step, start, unroll=2)
     for q in range(4):
         grad[:, q * LANES : (q + 1) * LANES] = total[q][0:8] + total[q][8:16]
 
@@ -532,28 +553,47 @@
     wait_all(writes)
 
 
-def finish_kernel(most, rest, base, defect, held_most, held_rest, held_base, plain, sems):
+def early_kernel(most, base, defect, held, held_base, plain, sems):
+    upper = lax.axis_index("row") >> 3
+    reads = []
+    writes = []
+    for a in range(EARLY):
+        rows = pl.ds(32 * a, 32)
+        reads.append(pltpu.make_async_copy(most.at[:, rows], held.at[:, rows], sems.at[3 * a]))
+        reads.append(pltpu.make_async_copy(base.at[:, rows], held_base.at[:, rows], sems.at[3 * a + 1]))
+        writes.append(pltpu.make_async_copy(plain.at[:, rows], defect.at[:, rows], sems.at[3 * a + 2]))
+    start_all(reads)
+    for a in range(EARLY):
+        wait_all(reads[2 * a : 2 * a + 2])
+        for c in range(2):
+            index = 2 * a + c
+            undeal(upper, index, held, 16 * index, plain, held_base)
+        writes[a].start()
+    wait_all(writes)
+
+
+def late_kernel(partial, most, rest, base, defect, total, held_most, held_rest, held_base, plain, sems):
+    del partial
     upper = lax.axis_index("row") >> 3
     rows = 16 * (8 - MOST)
+    first = 32 * EARLY
     reads = [
-        pltpu.make_async_copy(rest.at[:, pl.ds(0, rows)], held_rest, sems.at[0]),
-        pltpu.make_async_copy(most, held_most, sems.at[1]),
+        pltpu.make_async_copy(rest, held_rest, sems.at[0]),
+        pltpu.make_async_copy(
+            base.at[:, pl.ds(first, 128 - first)], held_base.at[:, pl.ds(first, 128 - first)], sems.at[1]
+        ),
+        pltpu.make_async_copy(
+            most.at[:, pl.ds(first, 16 * MOST - first)], held_most.at[:, pl.ds(first, 16 * MOST - first)], sems.at[2]
+        ),
     ]
-    order = (3, 2, 1, 0)
-    for a in order:
-        reads.append(
-            pltpu.make_async_copy(base.at[:, slice_rows(a)], held_base.at[:, slice_rows(a)], sems.at[2 + a])
-        )
+    order = range(3, EARLY - 1, -1)
     writes = [
-        pltpu.make_async_copy(plain.at[:, slice_rows(a)], defect.at[:, slice_rows(a)], sems.at[6 + a])
+        pltpu.make_async_copy(plain.at[:, slice_rows(a)], defect.at[:, slice_rows(a)], sems.at[3 + a])
         for a in order
     ]
     start_all(reads)
-    reads[0].wait()
+    wait_all(reads)
     for at, a in enumerate(order):
-        if at == 1:
-            reads[1].wait()
-        reads[2 + at].wait()
         for c in range(2):
             index = 2 * a + c
             if index < MOST:
@@ -561,7 +601,20 @@
             else:
                 undeal(upper, index, held_rest, 16 * (index - MOST), plain, held_base)
         writes[at].start()
+    lane = lax.broadcasted_iota(jnp.int32, (1, 1, 4), 2)
+    sums = jnp.zeros((1, 1, 4), F32)
+    for q in range(4):
+        part = held_rest[0, rows : rows + 8, q * LANES : (q + 1) * LANES]
+        for k in range(1, 8):
+            part = part + held_rest[k, rows : rows + 8, q * LANES : (q + 1) * LANES]
+        sums = jnp.where(lane == q, jnp.sum(part) / ORDER, sums)
+    total[...] = sums
     wait_all(writes)
+
+
+def most_kernel(blocks, out):
+    for k in range(8):
+        out[k] = blocks[k, 0 : 16 * MOST]
 
 
 VMEM = pl.BlockSpec(memory_space=pltpu.VMEM)
@@ -569,6 +622,7 @@
 ANY = pl.BlockSpec(memory_space=pl.ANY)
 PARAMS = pltpu.CompilerParams(vmem_limit_bytes=16 * 1024 * 1024)
 MOST = 5
+EARLY = MOST // 2
 UNIT_SHAPE = (UNITS, 2, ROWS, WIDTH)
 PACKED_SHAPE = (8, 8, 2, ROWS, WIDTH)
 PLAIN_SHAPE = (2, 128, ORDER)
@@ -701,12 +755,12 @@
     (grad,) = call(
         gradient_kernel,
         [(8, WIDTH)],
-        [*middle, both, *halos[:4]],
+        [in_hbm(x) for x in (*middle, both, *halos[:4])],
         (roots,),
         flops=30 << 20,
         size=6 << 20,
-        specs=[ANY] * 2 + [VMEM] * 4,
-        scratch=[room(UNIT_SHAPE), room((8, 4, 2, ROWS, WIDTH)), copies(2)],
+        specs=[ANY] * 6,
+        scratch=[room(UNIT_SHAPE), room((8, 4, 2, ROWS, WIDTH)), *map(room, SLAB_SHAPES[:4]), copies(6)],
         name="gradient",
     )
     grad = grad + lax.ppermute(grad, "row", PERM_I0)
@@ -720,7 +774,8 @@
     )
     here, joined = lax.optimization_barrier((here, joined))
     rest_here = regroup(joined)
-    most_next = earlier(here[:, : 16 * MOST])
+    (most,) = call(most_kernel, [MOST_SHAPE], [here], name="most_blocks")
+    most_next = earlier(most)
     (start,) = call(
         start_kernel,
         [hbm(PLAIN_SHAPE)],
@@ -730,19 +785,28 @@
         scratch=[room(BLOCKS_SHAPE), room(PLAIN_SHAPE), copies(8)],
         name="start_rows",
     )
-    start, rest_here, most_next = lax.optimization_barrier((start, rest_here, most_next))
+    terminal = in_hbm(terminal)
     (defect,) = call(
-        finish_kernel,
+        early_kernel,
         [hbm(PLAIN_SHAPE)],
-        [most_next, rest_here, in_hbm(terminal)],
-        specs=[ANY] * 3,
+        [most_next, terminal],
+        specs=[ANY, ANY],
         out_specs=[ANY],
-        scratch=[room(MOST_SHAPE), room(REST_SHAPE), room(PLAIN_SHAPE), room(PLAIN_SHAPE), copies(10)],
-        name="defect_rows",
+        scratch=[room(MOST_SHAPE), room(PLAIN_SHAPE), room(PLAIN_SHAPE), copies(3 * EARLY)],
+        name="defect_early",
     )
-    sums = rest_here[:, 16 * (8 - MOST) :].reshape(8, 8, 4, LANES)
-    totals = jnp.sum(sums, axis=(0, 1, 3)) / ORDER
-    return start[None], defect[None], totals[None, None]
+    start, defect, rest_here = lax.optimization_barrier((start, defect, rest_here))
+    defect, totals = call(
+        late_kernel,
+        [hbm(PLAIN_SHAPE), (1, 1, 4)],
+        [defect, most_next, rest_here, terminal],
+        specs=[ANY] * 4,
+        out_specs=[ANY, VMEM],
+        scratch=[room(MOST_SHAPE), room(JOINED_SHAPE), room(PLAIN_SHAPE), room(PLAIN_SHAPE), copies(7)],
+        name="defect_late",
+        input_output_aliases={0: 0},
+    )
+    return start[None], defect[None], totals
 
 
 def solution(mesh):

time: 176 us -> 170 us (0.966)
  local copies, waits for them, and re-layouts: 7.11 us -> 0.06 us
  starting transfers between devices: 46.1 us -> 51.3 us
  Pallas kernels: 50.6 us -> 46.1 us
    all_to_all x2, waiting for transfers between devices: 13.2 us -> 0.05 us  [regroup(): return lax.all_to_all(x, 'row', 0, 0, axis_index_groups=GROUPS, tiled=True)]
    ppermute x2, waiting for transfers between devices: 0.01 us -> 11.1 us  [earlier(): return lax.ppermute(x, 'seg', [(i + 1, i) for i in range(7)])]
    unnamed x28 -> x26, local copies, waits for them, and re-layouts: 5.9 us -> 0.06 us
    pallas_call x12 -> x14, Pallas kernels: 50.6 us -> 46.1 us  [call(): pl.pallas_call(kernel, out_shape=out_shape, in_specs=(specs or [VMEM] * l...]
    ppermute x15, waiting for transfers between devices: 0.04 us -> 3.2 us  [exchange(): return [lax.ppermute(s, 'row', perm) for s, perm in zip(slabs, perms)]]
    ppermute x2, starting transfers between devices: 12.6 us -> 15.8 us  [earlier(): return lax.ppermute(x, 'seg', [(i + 1, i) for i in range(7)])]
  transfers between devices with their start and end apart: 20 -> 20, of which waited for: 2 -> 6; matrix products, arithmetic and copies ran while one was open for 0% -> 0% of each run, Pallas kernels for 17% -> 17%
where the time goes in v3:
time: 170 us; the launch traced here: 169 us
  blocking collectives  55 us (32%)
  starting transfers between devices  51.3 us (30%)
  Pallas kernels  46.1 us (27%)
  waiting for transfers between devices  15.8 us (9%)
    all_to_all x1, blocking collectives, regroup(): return lax.all_to_all(x, 'row', 0, 0, axis_index_groups=GROUPS, tiled=True)  55 us
    pallas_call x14, Pallas kernels, call(): pl.pallas_call(kernel, out_shape=out_shape, in_specs=(specs or [VMEM] * l...  46.1 us
    ppermute x15, starting transfers between devices, exchange(): return [lax.ppermute(s, 'row', perm) for s, perm in zip(slabs, perms)]  23.9 us
    ppermute x2, starting transfers between devices, earlier(): return lax.ppermute(x, 'seg', [(i + 1, i) for i in range(7)])  15.8 us
    ppermute x2, waiting for transfers between devices, earlier(): return lax.ppermute(x, 'seg', [(i + 1, i) for i in range(7)])  11.1 us
    all_to_all x2, starting transfers between devices, regroup(): return lax.all_to_all(x, 'row', 0, 0, axis_index_groups=GROUPS, tiled=True)  8.06 us
    ppermute x1, starting transfers between devices, body(): grad = grad + lax.ppermute(grad, 'row', PERM_I0)  3.63 us
  transfers between devices with their start and end apart: 20, of which 6 were waited for; matrix products, arithmetic and copies ran while one was open for 0% of the time, Pallas kernels for 17%

profile of v3, /device:TPU:1, one launch (start us, length us, event | category | flops | bytes accessed | tf_op | source)
XLA Modules:
  0.0 169.4 jit_solution(16218314345202832226)
XLA Ops:
  0.6 3.5 %pack_blocks.1 = f32[8,8,2,16,512]{4,3,2,1,0:T(8,128)} custom-call(f32[2,128,2048]{2,1,0:T(8,128)} %bitcast.40, f32[2,128,2048]{2,1,0:T(8,128)} %bitcast.45), custom_call_target="tpu_custom_call" | custom-call | bytes 4194304 | tf_op jit(solution)/shard_map/pack_blocks/pallas_call | solution.py:652
  4.2 55.0 %all_to_all.15.rho_in = f32[8,8,2,16,512]{4,3,2,1,0:T(8,128)S(1)} all-to-all(f32[8,8,2,16,512]{4,3,2,1,0:T(8,128)} %pack_blocks.1), channel_id=1, replica_groups={{0,1,3,2,4,5,7,6},{14,15,13,12,10,11,9,8},{16,17,19,18,20,21,23,22},{30..., dimensions={0} | all-to-all | bytes 8388608 | tf_op jit(solution)/shard_map/all_to_all | solution.py:687
  59.2 0.0 copy-start.8
  59.2 0.0 copy-start.9
  59.2 0.0 copy-start.10
  59.2 0.0 copy-start.11
  59.2 0.5 slabs.1
  59.7 2.3 %collective-permute-start = (f32[8,2,16,512]{3,2,1,0:T(8,128)S(1)}, f32[8,2,16,512]{3,2,1,0:T(8,128)S(1)}, u32[]{:S(2)}, u32[]{:S(2)}) collective-permute-start(f32[8,2,16,512]{3,2,1,0:T(8,128)S(1)} %get-tuple-element.31), channel_id=1, source_target_pairs={{0,12},{1,13},{2,14},{3,15},{4,8},{5,9},{6,10},{7,11},{8,4},{9,5},... | collective-permute-start | bytes 1572872 | tf_op jit(solution)/shard_map/ppermute | solution.py:695
  62.0 0.0 collective-permute-start.1
  62.0 2.2 %collective-permute-start.2 = (f32[64,16,128]{2,1,0:T(8,128)S(1)}, f32[64,16,128]{2,1,0:T(8,128)S(1)}, u32[]{:S(2)}, u32[]{:S(2)}) collective-permute-start(f32[64,16,128]{2,1,0:T(8,128)S(1)} %get-tuple-element.33), channel_id=1, source_target_pairs={{0,3},{1,2},{2,1},{3,0},{4,7},{5,6},{6,5},{7,4},{8,11},{9,10},{10,... | collective-permute-start | bytes 1572872 | tf_op jit(solution)/shard_map/ppermute | solution.py:695
  64.2 0.5 collective-permute-start.3
  64.7 2.9 %collective-permute-start.4 = (f32[8,2,16,128]{3,2,1,0:T(8,128)S(1)}, f32[8,2,16,128]{3,2,1,0:T(8,128)S(1)}, u32[]{:S(2)}, u32[]{:S(2)}) collective-permute-start(f32[8,2,16,128]{3,2,1,0:T(8,128)S(1)} %get-tuple-element.35), channel_id=1, source_target_pairs={{0,15},{1,14},{4,11},{5,10},{16,31},{17,30},{20,27},{21,26},{32,47... | collective-permute-start | bytes 393224 | tf_op jit(solution)/shard_map/ppermute | solution.py:695
  67.6 5.6 %local_terms.3.refs_0_ = f32[32,2,16,512]{3,2,1,0:T(8,128)S(1)} custom-call(f32[64,2,16,512]{3,2,1,0:T(8,128)S(1)} %bitcast.12, f32[64,2,16,512]{3,2,1,0:T(8,128)S(1)} %bitcast.13, f32[1,4]{1,0:T(1,128)S(1)} %bitcast.16, f32[1,4]{1,0:T(1,128)S(1)} %bitcast.28, f32[1,4]{1,0:T(1,128)S(1)} %bitcast.31, f32[1,4]{1,0:T(1,128)S(1)} %bitcast.22, ...), custom_call_target="tpu_custom_call" | custom-call | flops 31457280 | bytes 6291456 | tf_op jit(solution)/shard_map/local_terms/pallas_call | solution.py:652
  73.2 1.3 collective-permute-done.4.refs_5_
  74.5 0.0 collective-permute-done.refs_1_
  74.5 0.0 collective-permute-done.1.refs_2_
  74.5 0.0 collective-permute-done.2.refs_3_
  74.5 0.3 collective-permute-done.3.refs_4_
  74.8 2.9 %edge_terms.3 = (f32[32,2,16,512]{3,2,1,0:T(8,128)S(1)}, f32[8,2,16,512]{3,2,1,0:T(8,128)S(1)}, f32[64,16,128]{2,1,0:T(8,128)S(1)}, f32[64,16,128]{2,1,0:T(8,128...) custom-call(f32[32,2,16,512]{3,2,1,0:T(8,128)S(1)} %local_terms.3.refs_0_, ...), custom_call_target="tpu_custom_call" | custom-call | flops 5242880 | bytes 8388608 | tf_op jit(solution)/shard_map/edge_terms/pallas_call | solution.py:652
  77.7 0.5 collective-permute-start.5
  78.2 4.9 %collective-permute-start.7 = (f32[64,16,128]{2,1,0:T(8,128)S(1)}, f32[64,16,128]{2,1,0:T(8,128)S(1)}, u32[]{:S(2)}, u32[]{:S(2)}) collective-permute-start(f32[64,16,128]{2,1,0:T(8,128)S(1)} %get-tuple-element.39), channel_id=1, source_target_pairs={{0,3},{1,2},{2,1},{3,0},{4,7},{5,6},{6,5},{7,4},{8,11},{9,10},{10,... | collective-permute-start | bytes 1572872 | tf_op jit(solution)/shard_map/ppermute | solution.py:695
  83.0 0.4 collective-permute-start.8
  83.4 2.5 %collective-permute-start.9 = (f32[8,2,16,128]{3,2,1,0:T(8,128)S(1)}, f32[8,2,16,128]{3,2,1,0:T(8,128)S(1)}, u32[]{:S(2)}, u32[]{:S(2)}) collective-permute-start(f32[8,2,16,128]{3,2,1,0:T(8,128)S(1)} %get-tuple-element.41), channel_id=1, source_target_pairs={{0,15},{1,14},{4,11},{5,10},{16,31},{17,30},{20,27},{21,26},{32,47... | collective-permute-start | bytes 393224 | tf_op jit(solution)/shard_map/ppermute | solution.py:695
  85.9 5.6 %local_terms.4.refs_0_ = f32[32,2,16,512]{3,2,1,0:T(8,128)S(1)} custom-call(f32[32,2,16,512]{3,2,1,0:T(8,128)S(1)} %get-tuple-element.36.refs_0_, f32[64,2,16,512]{3,2,1,0:T(8,128)S(1)} %bitcast.14, f32[1,4]{1,0:T(1,128)S(1)} %bitcast.18, f32[1,4]{1,0:T(1,128)S(1)} %bitcast.29, f32[1,4]{1,0:T(1,128)S(1)} %bitcast.32, f32[1,4]{1,0:T(1,128)S(1)} %bitcast.24, ...), custom_call_target="tpu_custom_call" | custom-call | flops 31457280 | bytes 6291456 | tf_op jit(solution)/shard_map/local_terms/pallas_call | solution.py:652
  91.5 0.7 collective-permute-done.7.refs_3_
  92.2 0.9 collective-permute-done.8.refs_4_
  93.1 2.9 %edge_terms.4 = (f32[32,2,16,512]{3,2,1,0:T(8,128)S(1)}, f32[8,2,16,512]{3,2,1,0:T(8,128)S(1)}, f32[64,16,128]{2,1,0:T(8,128)S(1)}, f32[64,16,128]{2,1,0:T(8,128...) custom-call(f32[32,2,16,512]{3,2,1,0:T(8,128)S(1)} %local_terms.4.refs_0_, ...), custom_call_target="tpu_custom_call" | custom-call | flops 5242880 | bytes 8388608 | tf_op jit(solution)/shard_map/edge_terms/pallas_call | solution.py:652
  96.0 0.4 collective-permute-start.10
  96.4 0.6 collective-permute-start.11
  97.1 2.3 %collective-permute-start.12 = (f32[64,16,128]{2,1,0:T(8,128)S(1)}, f32[64,16,128]{2,1,0:T(8,128)S(1)}, u32[]{:S(2)}, u32[]{:S(2)}) collective-permute-start(f32[64,16,128]{2,1,0:T(8,128)S(1)} %get-tuple-element.46), channel_id=1, source_target_pairs={{0,3},{1,2},{2,1},{3,0},{4,7},{5,6},{6,5},{7,4},{8,11},{9,10},{10,... | collective-permute-start | bytes 1572872 | tf_op jit(solution)/shard_map/ppermute | solution.py:695
  99.4 0.5 collective-permute-start.13
  99.9 4.0 %collective-permute-start.14 = (f32[8,2,16,128]{3,2,1,0:T(8,128)S(1)}, f32[8,2,16,128]{3,2,1,0:T(8,128)S(1)}, u32[]{:S(2)}, u32[]{:S(2)}) collective-permute-start(f32[8,2,16,128]{3,2,1,0:T(8,128)S(1)} %get-tuple-element.48), channel_id=1, source_target_pairs={{0,15},{1,14},{4,11},{5,10},{16,31},{17,30},{20,27},{21,26},{32,47... | collective-permute-start | bytes 393224 | tf_op jit(solution)/shard_map/ppermute | solution.py:695
  103.9 5.6 %local_terms.5 = (f32[32,2,16,512]{3,2,1,0:T(8,128)S(1)}, f32[32,2,16,512]{3,2,1,0:T(8,128)}) custom-call(f32[32,2,16,512]{3,2,1,0:T(8,128)S(1)} %get-tuple-element.42.refs_0_, f32[64,2,16,512]{3,2,1,0:T(8,128)S(1)} %bitcast.15, f32[1,4]{1,0:T(1,128)S(1)} %bitcast.20, f32[1,4]{1,0:T(1,128)S(1)} %bitcast.30, f32[1,4]{1,0:T(1,128)S(1)} %bitcast.33, ...), custom_call_target="tpu_custom_call" | custom-call | flops 31457280 | bytes 6291456 | tf_op jit(solution)/shard_map/local_terms/pallas_call | solution.py:652
  109.6 2.6 %edge_terms.5 = (f32[8,128,512]{2,1,0:T(8,128)}, f32[8,48,512]{2,1,0:T(8,128)}) custom-call(f32[32,2,16,512]{3,2,1,0:T(8,128)S(1)} %get-tuple-element.43.refs_0_, f32[8,2,16,512]{3,2,1,0:T(8,128)S(1)} %collective-permute-done.10.refs_1_.i0_in, f32[64,16,128]{2,1,0:T(8,128)S(1)} %collective-permute-done.11.refs_2_.j1_in, ...), custom_call_target="tpu_custom_call" | custom-call | flops 5242880 | bytes 6291456 | tf_op jit(solution)/shard_map/edge_terms/pallas_call | solution.py:652
  112.3 3.7 %all-to-all-start.1 = ((f32[8,128,512]{2,1,0:T(8,128)}), f32[8,128,512]{2,1,0:T(8,128)S(1)}, u32[]{:S(2)}, u32[]{:S(2)}) async-start(f32[8,128,512]{2,1,0:T(8,128)} %get-tuple-element.49), calls=%async_computation.1 | async-start | bytes 4194304 | tf_op jit(solution)/shard_map/all_to_all | solution.py:687
  116.0 7.6 %collective-permute-start.15 = (f32[8,48,512]{2,1,0:T(8,128)S(1)}, f32[8,48,512]{2,1,0:T(8,128)S(1)}, u32[]{:S(2)}, u32[]{:S(2)}) collective-permute-start(f32[8,48,512]{2,1,0:T(8,128)S(1)} %copy-done.12), channel_id=1, source_target_pairs={{16,0},{32,16},{48,32},{64,48},{80,64},{96,80},{112,96},{17,1},{33... | collective-permute-start | bytes 2359304 | tf_op jit(solution)/shard_map/ppermute | solution.py:691
  123.6 7.9 %gradient.1 = f32[8,512]{1,0:T(8,128)S(1)} custom-call(f32[32,2,16,512]{3,2,1,0:T(8,128)} %get-tuple-element.51.z_in, f32[8,8,2,16,512]{4,3,2,1,0:T(8,128)} %copy-done, f32[8,2,16,512]{3,2,1,0:T(8,128)} %copy-done.1, f32[64,16,128]{2,1,0:T(8,128)} %copy-done.2, f32[64,16,128]{2,1,0:T(8,128)} %copy-done.3, f32[64,16,128]{2,1,0:T(8,128)} %copy-done.4, ...), custom_call_target="tpu_custom_call" | custom-call | flops 31457280 | bytes 6291456 | tf_op jit(solution)/shard_map/gradient/pallas_call | solution.py:652
  131.6 3.6 %collective-permute-start.16 = (f32[8,512]{1,0:T(8,128)S(1)}, f32[8,512]{1,0:T(8,128)S(1)}, u32[]{:S(2)}, u32[]{:S(2)}) collective-permute-start(f32[8,512]{1,0:T(8,128)S(1)} %gradient.1), channel_id=1, source_target_pairs={{0,12},{1,13},{2,14},{3,15},{4,8},{5,9},{6,10},{7,11},{8,4},{9,5},... | collective-permute-start | bytes 49160 | tf_op jit(solution)/shard_map/ppermute | solution.py:766
  135.2 1.4 collective-permute-done.16
  136.6 1.0 join_blocks.1
  137.6 1.1 most_blocks.1
  138.8 8.2 %collective-permute-start.17 = (f32[8,80,512]{2,1,0:T(8,128)}, f32[8,80,512]{2,1,0:T(8,128)S(1)}, u32[]{:S(2)}, u32[]{:S(2)}) collective-permute-start(f32[8,80,512]{2,1,0:T(8,128)} %most_blocks.1), channel_id=1, source_target_pairs={{16,0},{32,16},{48,32},{64,48},{80,64},{96,80},{112,96},{17,1},{33... | collective-permute-start | bytes 3932168 | tf_op jit(solution)/shard_map/ppermute | solution.py:691
  147.0 4.3 %all-to-all-start.2 = ((f32[8,56,512]{2,1,0:T(8,128)}), f32[8,56,512]{2,1,0:T(8,128)}, u32[]{:S(2)}, u32[]{:S(2)}) async-start(f32[8,56,512]{2,1,0:T(8,128)} %join_blocks.1), calls=%async_computation.2 | async-start | bytes 1835008 | tf_op jit(solution)/shard_map/all_to_all | solution.py:687
  151.3 1.6 start_rows.1
  152.8 11.1 %collective-permute-done.17.most = f32[8,80,512]{2,1,0:T(8,128)S(1)} collective-permute-done((f32[8,80,512]{2,1,0:T(8,128)}, f32[8,80,512]{2,1,0:T(8,128)S(1)}, u32[]{:S(2)}, u32[]{:S(2)}) %collective-permute-start.17) | collective-permute-done | bytes 1310752 | tf_op jit(solution)/shard_map/ppermute | solution.py:691
  163.9 2.1 %defect_early.1.partial = f32[2,128,2048]{2,1,0:T(8,128)} custom-call(f32[8,80,512]{2,1,0:T(8,128)S(1)} %collective-permute-done.17.most, f32[2,128,2048]{2,1,0:T(8,128)} %bitcast.41), custom_call_target="tpu_custom_call" | custom-call | bytes 4194304 | tf_op jit(solution)/shard_map/defect_early/pallas_call | solution.py:652
  166.1 0.0 all-to-all-done.2.rest
  166.1 3.1 %defect_late.1 = (f32[2,128,2048]{2,1,0:T(8,128)}, f32[1,1,4]{2,1,0:T(1,128)}) custom-call(f32[2,128,2048]{2,1,0:T(8,128)} %defect_early.1.partial, f32[8,80,512]{2,1,0:T(8,128)S(1)} %collective-permute-done.17.most, f32[8,56,512]{2,1,0:T(8,128)} %all-to-all-done.2.rest, f32[2,128,2048]{2,1,0:T(8,128)} %bitcast.42), custom_call_target="tpu_custom_call", output_to_operand_aliasing={{0}: (0, {})} | custom-call | bytes 4194304 | tf_op jit(solution)/shard_map/defect_late/pallas_call | solution.py:652
  (34 shorter events, 0.1 us)
Async XLA Ops:
  59.1 44.7 %copy-start = (f32[8,8,2,16,512]{4,3,2,1,0:T(8,128)}, f32[8,8,2,16,512]{4,3,2,1,0:T(8,128)S(1)}, u32[]{:S(2)}) copy-start(f32[8,8,2,16,512]{4,3,2,1,0:T(8,128)S(1)} %all_to_all.15.rho_in) | copy-start | bytes 12582916
  59.1 8.4 %copy-start.5 = (f32[1,16]{1,0:T(1,128)S(1)}, f32[1,16]{1,0:T(1,128)}, u32[]{:S(2)}) copy-start(f32[1,16]{1,0:T(1,128)} %constant.6.refs_8_.roots) | copy-start | bytes 196
  59.1 8.4 %copy-start.6 = (f32[1,1,4]{2,1,0:T(1,128)S(1)}, f32[1,1,4]{2,1,0:T(1,128)}, u32[]{:S(2)}) copy-start(f32[1,1,4]{2,1,0:T(1,128)} %param.11) | copy-start | bytes 52
  59.1 8.4 %copy-start.7 = (f32[4]{0:T(128)S(1)}, f32[4]{0:T(128)}, u32[]{:S(2)}) copy-start(f32[4]{0:T(128)} %param.14) | copy-start | bytes 52
  59.2 8.4 %copy-start.8 = (f32[4]{0:T(128)S(1)}, f32[4]{0:T(128)}, u32[]{:S(2)}) copy-start(f32[4]{0:T(128)} %param.12) | copy-start | bytes 52
  59.2 8.4 %copy-start.9 = (f32[4]{0:T(128)S(1)}, f32[4]{0:T(128)}, u32[]{:S(2)}) copy-start(f32[4]{0:T(128)} %param.13) | copy-start | bytes 52
  59.2 8.4 %copy-start.10 = (f32[4]{0:T(128)S(1)}, f32[4]{0:T(128)}, u32[]{:S(2)}) copy-start(f32[4]{0:T(128)} %param.15) | copy-start | bytes 52
  59.2 8.4 %copy-start.11 = (f32[6]{0:T(128)S(1)}, f32[6]{0:T(128)}, u32[]{:S(2)}) copy-start(f32[6]{0:T(128)} %param.16) | copy-start | bytes 76
  59.7 14.8 %collective-permute-start = (f32[8,2,16,512]{3,2,1,0:T(8,128)S(1)}, f32[8,2,16,512]{3,2,1,0:T(8,128)S(1)}, u32[]{:S(2)}, u32[]{:S(2)}) collective-permute-start(f32[8,2,16,512]{3,2,1,0:T(8,128)S(1)} %get-tuple-element.31), channel_id=1, source_target_pairs={{0,12},{1,13},{2,14},{3,15},{4,8},{5,9},{6,10},{7,11},{8,4},{9,5},... | collective-permute-start | bytes 1572872 | tf_op jit(solution)/shard_map/ppermute | solution.py:695
  62.0 12.5 %collective-permute-start.1 = (f32[64,16,128]{2,1,0:T(8,128)S(1)}, f32[64,16,128]{2,1,0:T(8,128)S(1)}, u32[]{:S(2)}, u32[]{:S(2)}) collective-permute-start(f32[64,16,128]{2,1,0:T(8,128)S(1)} %get-tuple-element.32), channel_id=1, source_target_pairs={{0,1},{1,0},{2,3},{3,2},{4,5},{5,4},{6,7},{7,6},{8,9},{9,8},{10,11... | collective-permute-start | bytes 1572872 | tf_op jit(solution)/shard_map/ppermute | solution.py:695
  62.0 12.5 %collective-permute-start.2 = (f32[64,16,128]{2,1,0:T(8,128)S(1)}, f32[64,16,128]{2,1,0:T(8,128)S(1)}, u32[]{:S(2)}, u32[]{:S(2)}) collective-permute-start(f32[64,16,128]{2,1,0:T(8,128)S(1)} %get-tuple-element.33), channel_id=1, source_target_pairs={{0,3},{1,2},{2,1},{3,0},{4,7},{5,6},{6,5},{7,4},{8,11},{9,10},{10,... | collective-permute-start | bytes 1572872 | tf_op jit(solution)/shard_map/ppermute | solution.py:695
  64.2 10.6 %collective-permute-start.3 = (f32[64,16,128]{2,1,0:T(8,128)S(1)}, f32[64,16,128]{2,1,0:T(8,128)S(1)}, u32[]{:S(2)}, u32[]{:S(2)}) collective-permute-start(f32[64,16,128]{2,1,0:T(8,128)S(1)} %get-tuple-element.34), channel_id=1, source_target_pairs={{0,4},{1,5},{2,6},{3,7},{4,0},{5,1},{6,2},{7,3},{8,12},{9,13},{10,... | collective-permute-start | bytes 1572872 | tf_op jit(solution)/shard_map/ppermute | solution.py:695
  64.7 9.8 %collective-permute-start.4 = (f32[8,2,16,128]{3,2,1,0:T(8,128)S(1)}, f32[8,2,16,128]{3,2,1,0:T(8,128)S(1)}, u32[]{:S(2)}, u32[]{:S(2)}) collective-permute-start(f32[8,2,16,128]{3,2,1,0:T(8,128)S(1)} %get-tuple-element.35), channel_id=1, source_target_pairs={{0,15},{1,14},{4,11},{5,10},{16,31},{17,30},{20,27},{21,26},{32,47... | collective-permute-start | bytes 393224 | tf_op jit(solution)/shard_map/ppermute | solution.py:695
  77.7 13.8 %collective-permute-start.5 = (f32[8,2,16,512]{3,2,1,0:T(8,128)S(1)}, f32[8,2,16,512]{3,2,1,0:T(8,128)S(1)}, u32[]{:S(2)}, u32[]{:S(2)}) collective-permute-start(f32[8,2,16,512]{3,2,1,0:T(8,128)S(1)} %get-tuple-element.37), channel_id=1, source_target_pairs={{0,12},{1,13},{2,14},{3,15},{4,8},{5,9},{6,10},{7,11},{8,4},{9,5},... | collective-permute-start | bytes 1572872 | tf_op jit(solution)/shard_map/ppermute | solution.py:695
  78.2 13.3 %collective-permute-start.6 = (f32[64,16,128]{2,1,0:T(8,128)S(1)}, f32[64,16,128]{2,1,0:T(8,128)S(1)}, u32[]{:S(2)}, u32[]{:S(2)}) collective-permute-start(f32[64,16,128]{2,1,0:T(8,128)S(1)} %get-tuple-element.38), channel_id=1, source_target_pairs={{0,1},{1,0},{2,3},{3,2},{4,5},{5,4},{6,7},{7,6},{8,9},{9,8},{10,11... | collective-permute-start | bytes 1572872 | tf_op jit(solution)/shard_map/ppermute | solution.py:695
  78.2 14.1 %collective-permute-start.7 = (f32[64,16,128]{2,1,0:T(8,128)S(1)}, f32[64,16,128]{2,1,0:T(8,128)S(1)}, u32[]{:S(2)}, u32[]{:S(2)}) collective-permute-start(f32[64,16,128]{2,1,0:T(8,128)S(1)} %get-tuple-element.39), channel_id=1, source_target_pairs={{0,3},{1,2},{2,1},{3,0},{4,7},{5,6},{6,5},{7,4},{8,11},{9,10},{10,... | collective-permute-start | bytes 1572872 | tf_op jit(solution)/shard_map/ppermute | solution.py:695
  83.0 10.1 %collective-permute-start.8 = (f32[64,16,128]{2,1,0:T(8,128)S(1)}, f32[64,16,128]{2,1,0:T(8,128)S(1)}, u32[]{:S(2)}, u32[]{:S(2)}) collective-permute-start(f32[64,16,128]{2,1,0:T(8,128)S(1)} %get-tuple-element.40), channel_id=1, source_target_pairs={{0,4},{1,5},{2,6},{3,7},{4,0},{5,1},{6,2},{7,3},{8,12},{9,13},{10,... | collective-permute-start | bytes 1572872 | tf_op jit(solution)/shard_map/ppermute | solution.py:695
  83.4 8.1 %collective-permute-start.9 = (f32[8,2,16,128]{3,2,1,0:T(8,128)S(1)}, f32[8,2,16,128]{3,2,1,0:T(8,128)S(1)}, u32[]{:S(2)}, u32[]{:S(2)}) collective-permute-start(f32[8,2,16,128]{3,2,1,0:T(8,128)S(1)} %get-tuple-element.41), channel_id=1, source_target_pairs={{0,15},{1,14},{4,11},{5,10},{16,31},{17,30},{20,27},{21,26},{32,47... | collective-permute-start | bytes 393224 | tf_op jit(solution)/shard_map/ppermute | solution.py:695
  96.0 13.4 %collective-permute-start.10 = (f32[8,2,16,512]{3,2,1,0:T(8,128)S(1)}, f32[8,2,16,512]{3,2,1,0:T(8,128)S(1)}, u32[]{:S(2)}, u32[]{:S(2)}) collective-permute-start(f32[8,2,16,512]{3,2,1,0:T(8,128)S(1)} %get-tuple-element.44), channel_id=1, source_target_pairs={{0,12},{1,13},{2,14},{3,15},{4,8},{5,9},{6,10},{7,11},{8,4},{9,5},... | collective-permute-start | bytes 1572872 | tf_op jit(solution)/shard_map/ppermute | solution.py:695
  96.4 13.1 %collective-permute-start.11 = (f32[64,16,128]{2,1,0:T(8,128)S(1)}, f32[64,16,128]{2,1,0:T(8,128)S(1)}, u32[]{:S(2)}, u32[]{:S(2)}) collective-permute-start(f32[64,16,128]{2,1,0:T(8,128)S(1)} %get-tuple-element.45), channel_id=1, source_target_pairs={{0,1},{1,0},{2,3},{3,2},{4,5},{5,4},{6,7},{7,6},{8,9},{9,8},{10,11... | collective-permute-start | bytes 1572872 | tf_op jit(solution)/shard_map/ppermute | solution.py:695
  97.1 12.5 %collective-permute-start.12 = (f32[64,16,128]{2,1,0:T(8,128)S(1)}, f32[64,16,128]{2,1,0:T(8,128)S(1)}, u32[]{:S(2)}, u32[]{:S(2)}) collective-permute-start(f32[64,16,128]{2,1,0:T(8,128)S(1)} %get-tuple-element.46), channel_id=1, source_target_pairs={{0,3},{1,2},{2,1},{3,0},{4,7},{5,6},{6,5},{7,4},{8,11},{9,10},{10,... | collective-permute-start | bytes 1572872 | tf_op jit(solution)/shard_map/ppermute | solution.py:695
  99.4 10.2 %collective-permute-start.13 = (f32[64,16,128]{2,1,0:T(8,128)S(1)}, f32[64,16,128]{2,1,0:T(8,128)S(1)}, u32[]{:S(2)}, u32[]{:S(2)}) collective-permute-start(f32[64,16,128]{2,1,0:T(8,128)S(1)} %get-tuple-element.47), channel_id=1, source_target_pairs={{0,4},{1,5},{2,6},{3,7},{4,0},{5,1},{6,2},{7,3},{8,12},{9,13},{10,... | collective-permute-start | bytes 1572872 | tf_op jit(solution)/shard_map/ppermute | solution.py:695
  99.9 9.6 %collective-permute-start.14 = (f32[8,2,16,128]{3,2,1,0:T(8,128)S(1)}, f32[8,2,16,128]{3,2,1,0:T(8,128)S(1)}, u32[]{:S(2)}, u32[]{:S(2)}) collective-permute-start(f32[8,2,16,128]{3,2,1,0:T(8,128)S(1)} %get-tuple-element.48), channel_id=1, source_target_pairs={{0,15},{1,14},{4,11},{5,10},{16,31},{17,30},{20,27},{21,26},{32,47... | collective-permute-start | bytes 393224 | tf_op jit(solution)/shard_map/ppermute | solution.py:695
  109.5 2.7 %copy-start.1 = (f32[8,2,16,512]{3,2,1,0:T(8,128)}, f32[8,2,16,512]{3,2,1,0:T(8,128)S(1)}, u32[]{:S(2)}) copy-start(f32[8,2,16,512]{3,2,1,0:T(8,128)S(1)} %collective-permute-done.10.refs_1_.i0_in) | copy-start | bytes 1572868
  109.5 2.7 %copy-start.2 = (f32[64,16,128]{2,1,0:T(8,128)}, f32[64,16,128]{2,1,0:T(8,128)S(1)}, u32[]{:S(2)}) copy-start(f32[64,16,128]{2,1,0:T(8,128)S(1)} %collective-permute-done.11.refs_2_.j1_in) | copy-start | bytes 1572868
  109.5 2.7 %copy-start.3 = (f32[64,16,128]{2,1,0:T(8,128)}, f32[64,16,128]{2,1,0:T(8,128)S(1)}, u32[]{:S(2)}) copy-start(f32[64,16,128]{2,1,0:T(8,128)S(1)} %collective-permute-done.12.refs_3_.j0_in) | copy-start | bytes 1572868
  109.6 2.7 %copy-start.4 = (f32[64,16,128]{2,1,0:T(8,128)}, f32[64,16,128]{2,1,0:T(8,128)S(1)}, u32[]{:S(2)}) copy-start(f32[64,16,128]{2,1,0:T(8,128)S(1)} %collective-permute-done.13.refs_4_.i2_in) | copy-start | bytes 1572868
  112.2 3.8 %copy-start.12 = (f32[8,48,512]{2,1,0:T(8,128)S(1)}, f32[8,48,512]{2,1,0:T(8,128)}, u32[]{:S(2)}) copy-start(f32[8,48,512]{2,1,0:T(8,128)} %get-tuple-element.50) | copy-start | bytes 2359300
  112.3 25.4 %all-to-all-start.1 = ((f32[8,128,512]{2,1,0:T(8,128)}), f32[8,128,512]{2,1,0:T(8,128)S(1)}, u32[]{:S(2)}, u32[]{:S(2)}) async-start(f32[8,128,512]{2,1,0:T(8,128)} %get-tuple-element.49), calls=%async_computation.1 | async-start | bytes 4194304 | tf_op jit(solution)/shard_map/all_to_all | solution.py:687
  116.0 20.6 %collective-permute-start.15 = (f32[8,48,512]{2,1,0:T(8,128)S(1)}, f32[8,48,512]{2,1,0:T(8,128)S(1)}, u32[]{:S(2)}, u32[]{:S(2)}) collective-permute-start(f32[8,48,512]{2,1,0:T(8,128)S(1)} %copy-done.12), channel_id=1, source_target_pairs={{16,0},{32,16},{48,32},{64,48},{80,64},{96,80},{112,96},{17,1},{33... | collective-permute-start | bytes 2359304 | tf_op jit(solution)/shard_map/ppermute | solution.py:691
  131.6 5.1 %collective-permute-start.16 = (f32[8,512]{1,0:T(8,128)S(1)}, f32[8,512]{1,0:T(8,128)S(1)}, u32[]{:S(2)}, u32[]{:S(2)}) collective-permute-start(f32[8,512]{1,0:T(8,128)S(1)} %gradient.1), channel_id=1, source_target_pairs={{0,12},{1,13},{2,14},{3,15},{4,8},{5,9},{6,10},{7,11},{8,4},{9,5},... | collective-permute-start | bytes 49160 | tf_op jit(solution)/shard_map/ppermute | solution.py:766
  138.8 25.2 %collective-permute-start.17 = (f32[8,80,512]{2,1,0:T(8,128)}, f32[8,80,512]{2,1,0:T(8,128)S(1)}, u32[]{:S(2)}, u32[]{:S(2)}) collective-permute-start(f32[8,80,512]{2,1,0:T(8,128)} %most_blocks.1), channel_id=1, source_target_pairs={{16,0},{32,16},{48,32},{64,48},{80,64},{96,80},{112,96},{17,1},{33... | collective-permute-start | bytes 3932168 | tf_op jit(solution)/shard_map/ppermute | solution.py:691
  147.0 19.2 %all-to-all-start.2 = ((f32[8,56,512]{2,1,0:T(8,128)}), f32[8,56,512]{2,1,0:T(8,128)}, u32[]{:S(2)}, u32[]{:S(2)}) async-start(f32[8,56,512]{2,1,0:T(8,128)} %join_blocks.1), calls=%async_computation.2 | async-start | bytes 1835008 | tf_op jit(solution)/shard_map/all_to_all | solution.py:687

commit v4 on v3

--- a/solution.py
+++ b/solution.py
@@ -692,7 +692,10 @@
 
 
 def exchange(slabs, perms):
-    return [lax.ppermute(s, "row", perm) for s, perm in zip(slabs, perms)]
+    arrived = [None] * len(perms)
+    for at in (1, 2, 3, 0, 4):
+        arrived[at] = lax.ppermute(slabs[at], "row", perms[at])
+    return arrived
 
 
 def body(

time: 170 us -> 170 us (level)
  no operation moved by 1% of the time
where the time goes in v4:
time: 170 us; the launch traced here: 169 us
  blocking collectives  55 us (32%)
  starting transfers between devices  51.3 us (30%)
  Pallas kernels  46.1 us (27%)
  waiting for transfers between devices  15.8 us (9%)
    all_to_all x1, blocking collectives, regroup(): return lax.all_to_all(x, 'row', 0, 0, axis_index_groups=GROUPS, tiled=True)  55 us
    pallas_call x14, Pallas kernels, call(): pl.pallas_call(kernel, out_shape=out_shape, in_specs=(specs or [VMEM] * l...  46.1 us
    ppermute x15, starting transfers between devices, exchange(): arrived[at] = lax.ppermute(slabs[at], 'row', perms[at])  23.9 us
    ppermute x2, starting transfers between devices, earlier(): return lax.ppermute(x, 'seg', [(i + 1, i) for i in range(7)])  15.8 us
    ppermute x2, waiting for transfers between devices, earlier(): return lax.ppermute(x, 'seg', [(i + 1, i) for i in range(7)])  11.1 us
    all_to_all x2, starting transfers between devices, regroup(): return lax.all_to_all(x, 'row', 0, 0, axis_index_groups=GROUPS, tiled=True)  8.06 us
    ppermute x1, starting transfers between devices, body(): grad = grad + lax.ppermute(grad, 'row', PERM_I0)  3.63 us
  transfers between devices with their start and end apart: 20, of which 6 were waited for; matrix products, arithmetic and copies ran while one was open for 0% of the time, Pallas kernels for 17%

profile of v4, /device:TPU:1, one launch (start us, length us, event | category | flops | bytes accessed | tf_op | source)
XLA Modules:
  0.0 169.4 jit_solution(16218314345202832226)
XLA Ops:
  0.6 3.5 %pack_blocks.1 = f32[8,8,2,16,512]{4,3,2,1,0:T(8,128)} custom-call(f32[2,128,2048]{2,1,0:T(8,128)} %bitcast.40, f32[2,128,2048]{2,1,0:T(8,128)} %bitcast.45), custom_call_target="tpu_custom_call" | custom-call | bytes 4194304 | tf_op jit(solution)/shard_map/pack_blocks/pallas_call | solution.py:652
  4.2 55.0 %all_to_all.15.rho_in = f32[8,8,2,16,512]{4,3,2,1,0:T(8,128)S(1)} all-to-all(f32[8,8,2,16,512]{4,3,2,1,0:T(8,128)} %pack_blocks.1), channel_id=1, replica_groups={{0,1,3,2,4,5,7,6},{14,15,13,12,10,11,9,8},{16,17,19,18,20,21,23,22},{30..., dimensions={0} | all-to-all | bytes 8388608 | tf_op jit(solution)/shard_map/all_to_all | solution.py:687
  59.2 0.0 copy-start.8
  59.2 0.0 copy-start.9
  59.2 0.0 copy-start.10
  59.2 0.0 copy-start.11
  59.2 0.5 slabs.1
  59.7 2.3 %collective-permute-start = (f32[8,2,16,512]{3,2,1,0:T(8,128)S(1)}, f32[8,2,16,512]{3,2,1,0:T(8,128)S(1)}, u32[]{:S(2)}, u32[]{:S(2)}) collective-permute-start(f32[8,2,16,512]{3,2,1,0:T(8,128)S(1)} %get-tuple-element.31), channel_id=1, source_target_pairs={{0,12},{1,13},{2,14},{3,15},{4,8},{5,9},{6,10},{7,11},{8,4},{9,5},... | collective-permute-start | bytes 1572872 | tf_op jit(solution)/shard_map/ppermute | solution.py:697
  62.0 0.0 collective-permute-start.1
  62.0 2.2 %collective-permute-start.2 = (f32[64,16,128]{2,1,0:T(8,128)S(1)}, f32[64,16,128]{2,1,0:T(8,128)S(1)}, u32[]{:S(2)}, u32[]{:S(2)}) collective-permute-start(f32[64,16,128]{2,1,0:T(8,128)S(1)} %get-tuple-element.33), channel_id=1, source_target_pairs={{0,3},{1,2},{2,1},{3,0},{4,7},{5,6},{6,5},{7,4},{8,11},{9,10},{10,... | collective-permute-start | bytes 1572872 | tf_op jit(solution)/shard_map/ppermute | solution.py:697
  64.2 0.5 collective-permute-start.3
  64.7 2.9 %collective-permute-start.4 = (f32[8,2,16,128]{3,2,1,0:T(8,128)S(1)}, f32[8,2,16,128]{3,2,1,0:T(8,128)S(1)}, u32[]{:S(2)}, u32[]{:S(2)}) collective-permute-start(f32[8,2,16,128]{3,2,1,0:T(8,128)S(1)} %get-tuple-element.35), channel_id=1, source_target_pairs={{0,15},{1,14},{4,11},{5,10},{16,31},{17,30},{20,27},{21,26},{32,47... | collective-permute-start | bytes 393224 | tf_op jit(solution)/shard_map/ppermute | solution.py:697
  67.6 5.6 %local_terms.3.refs_0_ = f32[32,2,16,512]{3,2,1,0:T(8,128)S(1)} custom-call(f32[64,2,16,512]{3,2,1,0:T(8,128)S(1)} %bitcast.12, f32[64,2,16,512]{3,2,1,0:T(8,128)S(1)} %bitcast.13, f32[1,4]{1,0:T(1,128)S(1)} %bitcast.16, f32[1,4]{1,0:T(1,128)S(1)} %bitcast.28, f32[1,4]{1,0:T(1,128)S(1)} %bitcast.31, f32[1,4]{1,0:T(1,128)S(1)} %bitcast.22, ...), custom_call_target="tpu_custom_call" | custom-call | flops 31457280 | bytes 6291456 | tf_op jit(solution)/shard_map/local_terms/pallas_call | solution.py:652
  73.2 1.3 collective-permute-done.4.refs_5_
  74.5 0.0 collective-permute-done.refs_1_
  74.5 0.0 collective-permute-done.1.refs_2_
  74.5 0.0 collective-permute-done.2.refs_3_
  74.5 0.3 collective-permute-done.3.refs_4_
  74.8 2.9 %edge_terms.3 = (f32[32,2,16,512]{3,2,1,0:T(8,128)S(1)}, f32[8,2,16,512]{3,2,1,0:T(8,128)S(1)}, f32[64,16,128]{2,1,0:T(8,128)S(1)}, f32[64,16,128]{2,1,0:T(8,128...) custom-call(f32[32,2,16,512]{3,2,1,0:T(8,128)S(1)} %local_terms.3.refs_0_, ...), custom_call_target="tpu_custom_call" | custom-call | flops 5242880 | bytes 8388608 | tf_op jit(solution)/shard_map/edge_terms/pallas_call | solution.py:652
  77.7 0.5 collective-permute-start.5
  78.2 4.9 %collective-permute-start.7 = (f32[64,16,128]{2,1,0:T(8,128)S(1)}, f32[64,16,128]{2,1,0:T(8,128)S(1)}, u32[]{:S(2)}, u32[]{:S(2)}) collective-permute-start(f32[64,16,128]{2,1,0:T(8,128)S(1)} %get-tuple-element.39), channel_id=1, source_target_pairs={{0,3},{1,2},{2,1},{3,0},{4,7},{5,6},{6,5},{7,4},{8,11},{9,10},{10,... | collective-permute-start | bytes 1572872 | tf_op jit(solution)/shard_map/ppermute | solution.py:697
  83.0 0.4 collective-permute-start.8
  83.4 2.5 %collective-permute-start.9 = (f32[8,2,16,128]{3,2,1,0:T(8,128)S(1)}, f32[8,2,16,128]{3,2,1,0:T(8,128)S(1)}, u32[]{:S(2)}, u32[]{:S(2)}) collective-permute-start(f32[8,2,16,128]{3,2,1,0:T(8,128)S(1)} %get-tuple-element.41), channel_id=1, source_target_pairs={{0,15},{1,14},{4,11},{5,10},{16,31},{17,30},{20,27},{21,26},{32,47... | collective-permute-start | bytes 393224 | tf_op jit(solution)/shard_map/ppermute | solution.py:697
  85.9 5.6 %local_terms.4.refs_0_ = f32[32,2,16,512]{3,2,1,0:T(8,128)S(1)} custom-call(f32[32,2,16,512]{3,2,1,0:T(8,128)S(1)} %get-tuple-element.36.refs_0_, f32[64,2,16,512]{3,2,1,0:T(8,128)S(1)} %bitcast.14, f32[1,4]{1,0:T(1,128)S(1)} %bitcast.18, f32[1,4]{1,0:T(1,128)S(1)} %bitcast.29, f32[1,4]{1,0:T(1,128)S(1)} %bitcast.32, f32[1,4]{1,0:T(1,128)S(1)} %bitcast.24, ...), custom_call_target="tpu_custom_call" | custom-call | flops 31457280 | bytes 6291456 | tf_op jit(solution)/shard_map/local_terms/pallas_call | solution.py:652
  91.5 0.7 collective-permute-done.7.refs_3_
  92.2 0.9 collective-permute-done.8.refs_4_
  93.1 2.9 %edge_terms.4 = (f32[32,2,16,512]{3,2,1,0:T(8,128)S(1)}, f32[8,2,16,512]{3,2,1,0:T(8,128)S(1)}, f32[64,16,128]{2,1,0:T(8,128)S(1)}, f32[64,16,128]{2,1,0:T(8,128...) custom-call(f32[32,2,16,512]{3,2,1,0:T(8,128)S(1)} %local_terms.4.refs_0_, ...), custom_call_target="tpu_custom_call" | custom-call | flops 5242880 | bytes 8388608 | tf_op jit(solution)/shard_map/edge_terms/pallas_call | solution.py:652
  96.0 0.4 collective-permute-start.10
  96.4 0.6 collective-permute-start.11
  97.1 2.3 %collective-permute-start.12 = (f32[64,16,128]{2,1,0:T(8,128)S(1)}, f32[64,16,128]{2,1,0:T(8,128)S(1)}, u32[]{:S(2)}, u32[]{:S(2)}) collective-permute-start(f32[64,16,128]{2,1,0:T(8,128)S(1)} %get-tuple-element.46), channel_id=1, source_target_pairs={{0,3},{1,2},{2,1},{3,0},{4,7},{5,6},{6,5},{7,4},{8,11},{9,10},{10,... | collective-permute-start | bytes 1572872 | tf_op jit(solution)/shard_map/ppermute | solution.py:697
  99.4 0.5 collective-permute-start.13
  99.9 4.0 %collective-permute-start.14 = (f32[8,2,16,128]{3,2,1,0:T(8,128)S(1)}, f32[8,2,16,128]{3,2,1,0:T(8,128)S(1)}, u32[]{:S(2)}, u32[]{:S(2)}) collective-permute-start(f32[8,2,16,128]{3,2,1,0:T(8,128)S(1)} %get-tuple-element.48), channel_id=1, source_target_pairs={{0,15},{1,14},{4,11},{5,10},{16,31},{17,30},{20,27},{21,26},{32,47... | collective-permute-start | bytes 393224 | tf_op jit(solution)/shard_map/ppermute | solution.py:697
  103.9 5.6 %local_terms.5 = (f32[32,2,16,512]{3,2,1,0:T(8,128)S(1)}, f32[32,2,16,512]{3,2,1,0:T(8,128)}) custom-call(f32[32,2,16,512]{3,2,1,0:T(8,128)S(1)} %get-tuple-element.42.refs_0_, f32[64,2,16,512]{3,2,1,0:T(8,128)S(1)} %bitcast.15, f32[1,4]{1,0:T(1,128)S(1)} %bitcast.20, f32[1,4]{1,0:T(1,128)S(1)} %bitcast.30, f32[1,4]{1,0:T(1,128)S(1)} %bitcast.33, ...), custom_call_target="tpu_custom_call" | custom-call | flops 31457280 | bytes 6291456 | tf_op jit(solution)/shard_map/local_terms/pallas_call | solution.py:652
  109.6 2.6 %edge_terms.5 = (f32[8,128,512]{2,1,0:T(8,128)}, f32[8,48,512]{2,1,0:T(8,128)}) custom-call(f32[32,2,16,512]{3,2,1,0:T(8,128)S(1)} %get-tuple-element.43.refs_0_, f32[8,2,16,512]{3,2,1,0:T(8,128)S(1)} %collective-permute-done.10.refs_1_.i0_in, f32[64,16,128]{2,1,0:T(8,128)S(1)} %collective-permute-done.11.refs_2_.j1_in, ...), custom_call_target="tpu_custom_call" | custom-call | flops 5242880 | bytes 6291456 | tf_op jit(solution)/shard_map/edge_terms/pallas_call | solution.py:652
  112.3 3.7 %all-to-all-start.1 = ((f32[8,128,512]{2,1,0:T(8,128)}), f32[8,128,512]{2,1,0:T(8,128)S(1)}, u32[]{:S(2)}, u32[]{:S(2)}) async-start(f32[8,128,512]{2,1,0:T(8,128)} %get-tuple-element.49), calls=%async_computation.1 | async-start | bytes 4194304 | tf_op jit(solution)/shard_map/all_to_all | solution.py:687
  116.0 7.6 %collective-permute-start.15 = (f32[8,48,512]{2,1,0:T(8,128)S(1)}, f32[8,48,512]{2,1,0:T(8,128)S(1)}, u32[]{:S(2)}, u32[]{:S(2)}) collective-permute-start(f32[8,48,512]{2,1,0:T(8,128)S(1)} %copy-done.12), channel_id=1, source_target_pairs={{16,0},{32,16},{48,32},{64,48},{80,64},{96,80},{112,96},{17,1},{33... | collective-permute-start | bytes 2359304 | tf_op jit(solution)/shard_map/ppermute | solution.py:691
  123.6 7.9 %gradient.1 = f32[8,512]{1,0:T(8,128)S(1)} custom-call(f32[32,2,16,512]{3,2,1,0:T(8,128)} %get-tuple-element.51.z_in, f32[8,8,2,16,512]{4,3,2,1,0:T(8,128)} %copy-done, f32[8,2,16,512]{3,2,1,0:T(8,128)} %copy-done.1, f32[64,16,128]{2,1,0:T(8,128)} %copy-done.2, f32[64,16,128]{2,1,0:T(8,128)} %copy-done.3, f32[64,16,128]{2,1,0:T(8,128)} %copy-done.4, ...), custom_call_target="tpu_custom_call" | custom-call | flops 31457280 | bytes 6291456 | tf_op jit(solution)/shard_map/gradient/pallas_call | solution.py:652
  131.6 3.6 %collective-permute-start.16 = (f32[8,512]{1,0:T(8,128)S(1)}, f32[8,512]{1,0:T(8,128)S(1)}, u32[]{:S(2)}, u32[]{:S(2)}) collective-permute-start(f32[8,512]{1,0:T(8,128)S(1)} %gradient.1), channel_id=1, source_target_pairs={{0,12},{1,13},{2,14},{3,15},{4,8},{5,9},{6,10},{7,11},{8,4},{9,5},... | collective-permute-start | bytes 49160 | tf_op jit(solution)/shard_map/ppermute | solution.py:769
  135.2 1.4 collective-permute-done.16
  136.6 1.0 join_blocks.1
  137.6 1.1 most_blocks.1
  138.8 8.2 %collective-permute-start.17 = (f32[8,80,512]{2,1,0:T(8,128)}, f32[8,80,512]{2,1,0:T(8,128)S(1)}, u32[]{:S(2)}, u32[]{:S(2)}) collective-permute-start(f32[8,80,512]{2,1,0:T(8,128)} %most_blocks.1), channel_id=1, source_target_pairs={{16,0},{32,16},{48,32},{64,48},{80,64},{96,80},{112,96},{17,1},{33... | collective-permute-start | bytes 3932168 | tf_op jit(solution)/shard_map/ppermute | solution.py:691
  147.0 4.3 %all-to-all-start.2 = ((f32[8,56,512]{2,1,0:T(8,128)}), f32[8,56,512]{2,1,0:T(8,128)}, u32[]{:S(2)}, u32[]{:S(2)}) async-start(f32[8,56,512]{2,1,0:T(8,128)} %join_blocks.1), calls=%async_computation.2 | async-start | bytes 1835008 | tf_op jit(solution)/shard_map/all_to_all | solution.py:687
  151.3 1.6 start_rows.1
  152.8 11.1 %collective-permute-done.17.most = f32[8,80,512]{2,1,0:T(8,128)S(1)} collective-permute-done((f32[8,80,512]{2,1,0:T(8,128)}, f32[8,80,512]{2,1,0:T(8,128)S(1)}, u32[]{:S(2)}, u32[]{:S(2)}) %collective-permute-start.17) | collective-permute-done | bytes 1310752 | tf_op jit(solution)/shard_map/ppermute | solution.py:691
  163.9 2.1 %defect_early.1.partial = f32[2,128,2048]{2,1,0:T(8,128)} custom-call(f32[8,80,512]{2,1,0:T(8,128)S(1)} %collective-permute-done.17.most, f32[2,128,2048]{2,1,0:T(8,128)} %bitcast.41), custom_call_target="tpu_custom_call" | custom-call | bytes 4194304 | tf_op jit(solution)/shard_map/defect_early/pallas_call | solution.py:652
  166.1 0.0 all-to-all-done.2.rest
  166.1 3.1 %defect_late.1 = (f32[2,128,2048]{2,1,0:T(8,128)}, f32[1,1,4]{2,1,0:T(1,128)}) custom-call(f32[2,128,2048]{2,1,0:T(8,128)} %defect_early.1.partial, f32[8,80,512]{2,1,0:T(8,128)S(1)} %collective-permute-done.17.most, f32[8,56,512]{2,1,0:T(8,128)} %all-to-all-done.2.rest, f32[2,128,2048]{2,1,0:T(8,128)} %bitcast.42), custom_call_target="tpu_custom_call", output_to_operand_aliasing={{0}: (0, {})} | custom-call | bytes 4194304 | tf_op jit(solution)/shard_map/defect_late/pallas_call | solution.py:652
  (34 shorter events, 0.1 us)
Async XLA Ops:
  59.1 44.7 %copy-start = (f32[8,8,2,16,512]{4,3,2,1,0:T(8,128)}, f32[8,8,2,16,512]{4,3,2,1,0:T(8,128)S(1)}, u32[]{:S(2)}) copy-start(f32[8,8,2,16,512]{4,3,2,1,0:T(8,128)S(1)} %all_to_all.15.rho_in) | copy-start | bytes 12582916
  59.1 8.4 %copy-start.5 = (f32[1,16]{1,0:T(1,128)S(1)}, f32[1,16]{1,0:T(1,128)}, u32[]{:S(2)}) copy-start(f32[1,16]{1,0:T(1,128)} %constant.6.refs_8_.roots) | copy-start | bytes 196
  59.1 8.4 %copy-start.6 = (f32[1,1,4]{2,1,0:T(1,128)S(1)}, f32[1,1,4]{2,1,0:T(1,128)}, u32[]{:S(2)}) copy-start(f32[1,1,4]{2,1,0:T(1,128)} %param.11) | copy-start | bytes 52
  59.1 8.4 %copy-start.7 = (f32[4]{0:T(128)S(1)}, f32[4]{0:T(128)}, u32[]{:S(2)}) copy-start(f32[4]{0:T(128)} %param.14) | copy-start | bytes 52
  59.2 8.4 %copy-start.8 = (f32[4]{0:T(128)S(1)}, f32[4]{0:T(128)}, u32[]{:S(2)}) copy-start(f32[4]{0:T(128)} %param.12) | copy-start | bytes 52
  59.2 8.4 %copy-start.9 = (f32[4]{0:T(128)S(1)}, f32[4]{0:T(128)}, u32[]{:S(2)}) copy-start(f32[4]{0:T(128)} %param.13) | copy-start | bytes 52
  59.2 8.4 %copy-start.10 = (f32[4]{0:T(128)S(1)}, f32[4]{0:T(128)}, u32[]{:S(2)}) copy-start(f32[4]{0:T(128)} %param.15) | copy-start | bytes 52
  59.2 8.4 %copy-start.11 = (f32[6]{0:T(128)S(1)}, f32[6]{0:T(128)}, u32[]{:S(2)}) copy-start(f32[6]{0:T(128)} %param.16) | copy-start | bytes 76
  59.7 14.8 %collective-permute-start = (f32[8,2,16,512]{3,2,1,0:T(8,128)S(1)}, f32[8,2,16,512]{3,2,1,0:T(8,128)S(1)}, u32[]{:S(2)}, u32[]{:S(2)}) collective-permute-start(f32[8,2,16,512]{3,2,1,0:T(8,128)S(1)} %get-tuple-element.31), channel_id=1, source_target_pairs={{0,12},{1,13},{2,14},{3,15},{4,8},{5,9},{6,10},{7,11},{8,4},{9,5},... | collective-permute-start | bytes 1572872 | tf_op jit(solution)/shard_map/ppermute | solution.py:697
  62.0 12.5 %collective-permute-start.1 = (f32[64,16,128]{2,1,0:T(8,128)S(1)}, f32[64,16,128]{2,1,0:T(8,128)S(1)}, u32[]{:S(2)}, u32[]{:S(2)}) collective-permute-start(f32[64,16,128]{2,1,0:T(8,128)S(1)} %get-tuple-element.32), channel_id=1, source_target_pairs={{0,1},{1,0},{2,3},{3,2},{4,5},{5,4},{6,7},{7,6},{8,9},{9,8},{10,11... | collective-permute-start | bytes 1572872 | tf_op jit(solution)/shard_map/ppermute | solution.py:697
  62.0 12.5 %collective-permute-start.2 = (f32[64,16,128]{2,1,0:T(8,128)S(1)}, f32[64,16,128]{2,1,0:T(8,128)S(1)}, u32[]{:S(2)}, u32[]{:S(2)}) collective-permute-start(f32[64,16,128]{2,1,0:T(8,128)S(1)} %get-tuple-element.33), channel_id=1, source_target_pairs={{0,3},{1,2},{2,1},{3,0},{4,7},{5,6},{6,5},{7,4},{8,11},{9,10},{10,... | collective-permute-start | bytes 1572872 | tf_op jit(solution)/shard_map/ppermute | solution.py:697
  64.2 10.6 %collective-permute-start.3 = (f32[64,16,128]{2,1,0:T(8,128)S(1)}, f32[64,16,128]{2,1,0:T(8,128)S(1)}, u32[]{:S(2)}, u32[]{:S(2)}) collective-permute-start(f32[64,16,128]{2,1,0:T(8,128)S(1)} %get-tuple-element.34), channel_id=1, source_target_pairs={{0,4},{1,5},{2,6},{3,7},{4,0},{5,1},{6,2},{7,3},{8,12},{9,13},{10,... | collective-permute-start | bytes 1572872 | tf_op jit(solution)/shard_map/ppermute | solution.py:697
  64.7 9.8 %collective-permute-start.4 = (f32[8,2,16,128]{3,2,1,0:T(8,128)S(1)}, f32[8,2,16,128]{3,2,1,0:T(8,128)S(1)}, u32[]{:S(2)}, u32[]{:S(2)}) collective-permute-start(f32[8,2,16,128]{3,2,1,0:T(8,128)S(1)} %get-tuple-element.35), channel_id=1, source_target_pairs={{0,15},{1,14},{4,11},{5,10},{16,31},{17,30},{20,27},{21,26},{32,47... | collective-permute-start | bytes 393224 | tf_op jit(solution)/shard_map/ppermute | solution.py:697
  77.7 13.8 %collective-permute-start.5 = (f32[8,2,16,512]{3,2,1,0:T(8,128)S(1)}, f32[8,2,16,512]{3,2,1,0:T(8,128)S(1)}, u32[]{:S(2)}, u32[]{:S(2)}) collective-permute-start(f32[8,2,16,512]{3,2,1,0:T(8,128)S(1)} %get-tuple-element.37), channel_id=1, source_target_pairs={{0,12},{1,13},{2,14},{3,15},{4,8},{5,9},{6,10},{7,11},{8,4},{9,5},... | collective-permute-start | bytes 1572872 | tf_op jit(solution)/shard_map/ppermute | solution.py:697
  78.2 13.3 %collective-permute-start.6 = (f32[64,16,128]{2,1,0:T(8,128)S(1)}, f32[64,16,128]{2,1,0:T(8,128)S(1)}, u32[]{:S(2)}, u32[]{:S(2)}) collective-permute-start(f32[64,16,128]{2,1,0:T(8,128)S(1)} %get-tuple-element.38), channel_id=1, source_target_pairs={{0,1},{1,0},{2,3},{3,2},{4,5},{5,4},{6,7},{7,6},{8,9},{9,8},{10,11... | collective-permute-start | bytes 1572872 | tf_op jit(solution)/shard_map/ppermute | solution.py:697
  78.2 14.1 %collective-permute-start.7 = (f32[64,16,128]{2,1,0:T(8,128)S(1)}, f32[64,16,128]{2,1,0:T(8,128)S(1)}, u32[]{:S(2)}, u32[]{:S(2)}) collective-permute-start(f32[64,16,128]{2,1,0:T(8,128)S(1)} %get-tuple-element.39), channel_id=1, source_target_pairs={{0,3},{1,2},{2,1},{3,0},{4,7},{5,6},{6,5},{7,4},{8,11},{9,10},{10,... | collective-permute-start | bytes 1572872 | tf_op jit(solution)/shard_map/ppermute | solution.py:697
  83.0 10.1 %collective-permute-start.8 = (f32[64,16,128]{2,1,0:T(8,128)S(1)}, f32[64,16,128]{2,1,0:T(8,128)S(1)}, u32[]{:S(2)}, u32[]{:S(2)}) collective-permute-start(f32[64,16,128]{2,1,0:T(8,128)S(1)} %get-tuple-element.40), channel_id=1, source_target_pairs={{0,4},{1,5},{2,6},{3,7},{4,0},{5,1},{6,2},{7,3},{8,12},{9,13},{10,... | collective-permute-start | bytes 1572872 | tf_op jit(solution)/shard_map/ppermute | solution.py:697
  83.4 8.1 %collective-permute-start.9 = (f32[8,2,16,128]{3,2,1,0:T(8,128)S(1)}, f32[8,2,16,128]{3,2,1,0:T(8,128)S(1)}, u32[]{:S(2)}, u32[]{:S(2)}) collective-permute-start(f32[8,2,16,128]{3,2,1,0:T(8,128)S(1)} %get-tuple-element.41), channel_id=1, source_target_pairs={{0,15},{1,14},{4,11},{5,10},{16,31},{17,30},{20,27},{21,26},{32,47... | collective-permute-start | bytes 393224 | tf_op jit(solution)/shard_map/ppermute | solution.py:697
  96.0 13.4 %collective-permute-start.10 = (f32[8,2,16,512]{3,2,1,0:T(8,128)S(1)}, f32[8,2,16,512]{3,2,1,0:T(8,128)S(1)}, u32[]{:S(2)}, u32[]{:S(2)}) collective-permute-start(f32[8,2,16,512]{3,2,1,0:T(8,128)S(1)} %get-tuple-element.44), channel_id=1, source_target_pairs={{0,12},{1,13},{2,14},{3,15},{4,8},{5,9},{6,10},{7,11},{8,4},{9,5},... | collective-permute-start | bytes 1572872 | tf_op jit(solution)/shard_map/ppermute | solution.py:697
  96.4 13.1 %collective-permute-start.11 = (f32[64,16,128]{2,1,0:T(8,128)S(1)}, f32[64,16,128]{2,1,0:T(8,128)S(1)}, u32[]{:S(2)}, u32[]{:S(2)}) collective-permute-start(f32[64,16,128]{2,1,0:T(8,128)S(1)} %get-tuple-element.45), channel_id=1, source_target_pairs={{0,1},{1,0},{2,3},{3,2},{4,5},{5,4},{6,7},{7,6},{8,9},{9,8},{10,11... | collective-permute-start | bytes 1572872 | tf_op jit(solution)/shard_map/ppermute | solution.py:697
  97.1 12.5 %collective-permute-start.12 = (f32[64,16,128]{2,1,0:T(8,128)S(1)}, f32[64,16,128]{2,1,0:T(8,128)S(1)}, u32[]{:S(2)}, u32[]{:S(2)}) collective-permute-start(f32[64,16,128]{2,1,0:T(8,128)S(1)} %get-tuple-element.46), channel_id=1, source_target_pairs={{0,3},{1,2},{2,1},{3,0},{4,7},{5,6},{6,5},{7,4},{8,11},{9,10},{10,... | collective-permute-start | bytes 1572872 | tf_op jit(solution)/shard_map/ppermute | solution.py:697
  99.4 10.2 %collective-permute-start.13 = (f32[64,16,128]{2,1,0:T(8,128)S(1)}, f32[64,16,128]{2,1,0:T(8,128)S(1)}, u32[]{:S(2)}, u32[]{:S(2)}) collective-permute-start(f32[64,16,128]{2,1,0:T(8,128)S(1)} %get-tuple-element.47), channel_id=1, source_target_pairs={{0,4},{1,5},{2,6},{3,7},{4,0},{5,1},{6,2},{7,3},{8,12},{9,13},{10,... | collective-permute-start | bytes 1572872 | tf_op jit(solution)/shard_map/ppermute | solution.py:697
  99.9 9.6 %collective-permute-start.14 = (f32[8,2,16,128]{3,2,1,0:T(8,128)S(1)}, f32[8,2,16,128]{3,2,1,0:T(8,128)S(1)}, u32[]{:S(2)}, u32[]{:S(2)}) collective-permute-start(f32[8,2,16,128]{3,2,1,0:T(8,128)S(1)} %get-tuple-element.48), channel_id=1, source_target_pairs={{0,15},{1,14},{4,11},{5,10},{16,31},{17,30},{20,27},{21,26},{32,47... | collective-permute-start | bytes 393224 | tf_op jit(solution)/shard_map/ppermute | solution.py:697
  109.5 2.7 %copy-start.1 = (f32[8,2,16,512]{3,2,1,0:T(8,128)}, f32[8,2,16,512]{3,2,1,0:T(8,128)S(1)}, u32[]{:S(2)}) copy-start(f32[8,2,16,512]{3,2,1,0:T(8,128)S(1)} %collective-permute-done.10.refs_1_.i0_in) | copy-start | bytes 1572868
  109.5 2.7 %copy-start.2 = (f32[64,16,128]{2,1,0:T(8,128)}, f32[64,16,128]{2,1,0:T(8,128)S(1)}, u32[]{:S(2)}) copy-start(f32[64,16,128]{2,1,0:T(8,128)S(1)} %collective-permute-done.11.refs_2_.j1_in) | copy-start | bytes 1572868
  109.5 2.7 %copy-start.3 = (f32[64,16,128]{2,1,0:T(8,128)}, f32[64,16,128]{2,1,0:T(8,128)S(1)}, u32[]{:S(2)}) copy-start(f32[64,16,128]{2,1,0:T(8,128)S(1)} %collective-permute-done.12.refs_3_.j0_in) | copy-start | bytes 1572868
  109.6 2.7 %copy-start.4 = (f32[64,16,128]{2,1,0:T(8,128)}, f32[64,16,128]{2,1,0:T(8,128)S(1)}, u32[]{:S(2)}) copy-start(f32[64,16,128]{2,1,0:T(8,128)S(1)} %collective-permute-done.13.refs_4_.i2_in) | copy-start | bytes 1572868
  112.2 3.8 %copy-start.12 = (f32[8,48,512]{2,1,0:T(8,128)S(1)}, f32[8,48,512]{2,1,0:T(8,128)}, u32[]{:S(2)}) copy-start(f32[8,48,512]{2,1,0:T(8,128)} %get-tuple-element.50) | copy-start | bytes 2359300
  112.3 25.4 %all-to-all-start.1 = ((f32[8,128,512]{2,1,0:T(8,128)}), f32[8,128,512]{2,1,0:T(8,128)S(1)}, u32[]{:S(2)}, u32[]{:S(2)}) async-start(f32[8,128,512]{2,1,0:T(8,128)} %get-tuple-element.49), calls=%async_computation.1 | async-start | bytes 4194304 | tf_op jit(solution)/shard_map/all_to_all | solution.py:687
  116.0 20.6 %collective-permute-start.15 = (f32[8,48,512]{2,1,0:T(8,128)S(1)}, f32[8,48,512]{2,1,0:T(8,128)S(1)}, u32[]{:S(2)}, u32[]{:S(2)}) collective-permute-start(f32[8,48,512]{2,1,0:T(8,128)S(1)} %copy-done.12), channel_id=1, source_target_pairs={{16,0},{32,16},{48,32},{64,48},{80,64},{96,80},{112,96},{17,1},{33... | collective-permute-start | bytes 2359304 | tf_op jit(solution)/shard_map/ppermute | solution.py:691
  131.6 5.1 %collective-permute-start.16 = (f32[8,512]{1,0:T(8,128)S(1)}, f32[8,512]{1,0:T(8,128)S(1)}, u32[]{:S(2)}, u32[]{:S(2)}) collective-permute-start(f32[8,512]{1,0:T(8,128)S(1)} %gradient.1), channel_id=1, source_target_pairs={{0,12},{1,13},{2,14},{3,15},{4,8},{5,9},{6,10},{7,11},{8,4},{9,5},... | collective-permute-start | bytes 49160 | tf_op jit(solution)/shard_map/ppermute | solution.py:769
  138.8 25.2 %collective-permute-start.17 = (f32[8,80,512]{2,1,0:T(8,128)}, f32[8,80,512]{2,1,0:T(8,128)S(1)}, u32[]{:S(2)}, u32[]{:S(2)}) collective-permute-start(f32[8,80,512]{2,1,0:T(8,128)} %most_blocks.1), channel_id=1, source_target_pairs={{16,0},{32,16},{48,32},{64,48},{80,64},{96,80},{112,96},{17,1},{33... | collective-permute-start | bytes 3932168 | tf_op jit(solution)/shard_map/ppermute | solution.py:691
  147.0 19.2 %all-to-all-start.2 = ((f32[8,56,512]{2,1,0:T(8,128)}), f32[8,56,512]{2,1,0:T(8,128)}, u32[]{:S(2)}, u32[]{:S(2)}) async-start(f32[8,56,512]{2,1,0:T(8,128)} %join_blocks.1), calls=%async_computation.2 | async-start | bytes 1835008 | tf_op jit(solution)/shard_map/all_to_all | solution.py:687

commit v5 on v3

--- a/solution.py
+++ b/solution.py
@@ -592,8 +592,10 @@
         for a in order
     ]
     start_all(reads)
-    wait_all(reads)
+    wait_all(reads[:2])
     for at, a in enumerate(order):
+        if at == 1:
+            reads[2].wait()
         for c in range(2):
             index = 2 * a + c
             if index < MOST:

time: 170 us -> 170 us (level)
  no operation moved by 1% of the time
where the time goes in v5:
time: 170 us; the launch traced here: 169 us
  blocking collectives  55 us (32%)
  starting transfers between devices  51.3 us (30%)
  Pallas kernels  46.1 us (27%)
  waiting for transfers between devices  15.8 us (9%)
    all_to_all x1, blocking collectives, regroup(): return lax.all_to_all(x, 'row', 0, 0, axis_index_groups=GROUPS, tiled=True)  55 us
    pallas_call x14, Pallas kernels, call(): pl.pallas_call(kernel, out_shape=out_shape, in_specs=(specs or [VMEM] * l...  46.1 us
    ppermute x15, starting transfers between devices, exchange(): return [lax.ppermute(s, 'row', perm) for s, perm in zip(slabs, perms)]  23.9 us
    ppermute x2, starting transfers between devices, earlier(): return lax.ppermute(x, 'seg', [(i + 1, i) for i in range(7)])  15.8 us
    ppermute x2, waiting for transfers between devices, earlier(): return lax.ppermute(x, 'seg', [(i + 1, i) for i in range(7)])  11.1 us
    all_to_all x2, starting transfers between devices, regroup(): return lax.all_to_all(x, 'row', 0, 0, axis_index_groups=GROUPS, tiled=True)  8.06 us
    ppermute x1, starting transfers between devices, body(): grad = grad + lax.ppermute(grad, 'row', PERM_I0)  3.63 us
  transfers between devices with their start and end apart: 20, of which 6 were waited for; matrix products, arithmetic and copies ran while one was open for 0% of the time, Pallas kernels for 17%

profile of v5, /device:TPU:1, one launch (start us, length us, event | category | flops | bytes accessed | tf_op | source)
XLA Modules:
  0.0 169.4 jit_solution(5849597277541482025)
XLA Ops:
  0.6 3.5 %pack_blocks.1 = f32[8,8,2,16,512]{4,3,2,1,0:T(8,128)} custom-call(f32[2,128,2048]{2,1,0:T(8,128)} %bitcast.40, f32[2,128,2048]{2,1,0:T(8,128)} %bitcast.45), custom_call_target="tpu_custom_call" | custom-call | bytes 4194304 | tf_op jit(solution)/shard_map/pack_blocks/pallas_call | solution.py:654
  4.2 55.0 %all_to_all.15.rho_in = f32[8,8,2,16,512]{4,3,2,1,0:T(8,128)S(1)} all-to-all(f32[8,8,2,16,512]{4,3,2,1,0:T(8,128)} %pack_blocks.1), channel_id=1, replica_groups={{0,1,3,2,4,5,7,6},{14,15,13,12,10,11,9,8},{16,17,19,18,20,21,23,22},{30..., dimensions={0} | all-to-all | bytes 8388608 | tf_op jit(solution)/shard_map/all_to_all | solution.py:689
  59.2 0.0 copy-start.8
  59.2 0.0 copy-start.9
  59.2 0.0 copy-start.10
  59.2 0.0 copy-start.11
  59.2 0.5 slabs.1
  59.7 2.3 %collective-permute-start = (f32[8,2,16,512]{3,2,1,0:T(8,128)S(1)}, f32[8,2,16,512]{3,2,1,0:T(8,128)S(1)}, u32[]{:S(2)}, u32[]{:S(2)}) collective-permute-start(f32[8,2,16,512]{3,2,1,0:T(8,128)S(1)} %get-tuple-element.31), channel_id=1, source_target_pairs={{0,12},{1,13},{2,14},{3,15},{4,8},{5,9},{6,10},{7,11},{8,4},{9,5},... | collective-permute-start | bytes 1572872 | tf_op jit(solution)/shard_map/ppermute | solution.py:697
  62.0 0.0 collective-permute-start.1
  62.0 2.2 %collective-permute-start.2 = (f32[64,16,128]{2,1,0:T(8,128)S(1)}, f32[64,16,128]{2,1,0:T(8,128)S(1)}, u32[]{:S(2)}, u32[]{:S(2)}) collective-permute-start(f32[64,16,128]{2,1,0:T(8,128)S(1)} %get-tuple-element.33), channel_id=1, source_target_pairs={{0,3},{1,2},{2,1},{3,0},{4,7},{5,6},{6,5},{7,4},{8,11},{9,10},{10,... | collective-permute-start | bytes 1572872 | tf_op jit(solution)/shard_map/ppermute | solution.py:697
  64.2 0.5 collective-permute-start.3
  64.7 2.9 %collective-permute-start.4 = (f32[8,2,16,128]{3,2,1,0:T(8,128)S(1)}, f32[8,2,16,128]{3,2,1,0:T(8,128)S(1)}, u32[]{:S(2)}, u32[]{:S(2)}) collective-permute-start(f32[8,2,16,128]{3,2,1,0:T(8,128)S(1)} %get-tuple-element.35), channel_id=1, source_target_pairs={{0,15},{1,14},{4,11},{5,10},{16,31},{17,30},{20,27},{21,26},{32,47... | collective-permute-start | bytes 393224 | tf_op jit(solution)/shard_map/ppermute | solution.py:697
  67.6 5.6 %local_terms.3.refs_0_ = f32[32,2,16,512]{3,2,1,0:T(8,128)S(1)} custom-call(f32[64,2,16,512]{3,2,1,0:T(8,128)S(1)} %bitcast.12, f32[64,2,16,512]{3,2,1,0:T(8,128)S(1)} %bitcast.13, f32[1,4]{1,0:T(1,128)S(1)} %bitcast.16, f32[1,4]{1,0:T(1,128)S(1)} %bitcast.28, f32[1,4]{1,0:T(1,128)S(1)} %bitcast.31, f32[1,4]{1,0:T(1,128)S(1)} %bitcast.22, ...), custom_call_target="tpu_custom_call" | custom-call | flops 31457280 | bytes 6291456 | tf_op jit(solution)/shard_map/local_terms/pallas_call | solution.py:654
  73.2 1.3 collective-permute-done.4.refs_5_
  74.5 0.0 collective-permute-done.refs_1_
  74.5 0.0 collective-permute-done.1.refs_2_
  74.5 0.0 collective-permute-done.2.refs_3_
  74.5 0.3 collective-permute-done.3.refs_4_
  74.8 2.9 %edge_terms.3 = (f32[32,2,16,512]{3,2,1,0:T(8,128)S(1)}, f32[8,2,16,512]{3,2,1,0:T(8,128)S(1)}, f32[64,16,128]{2,1,0:T(8,128)S(1)}, f32[64,16,128]{2,1,0:T(8,128...) custom-call(f32[32,2,16,512]{3,2,1,0:T(8,128)S(1)} %local_terms.3.refs_0_, ...), custom_call_target="tpu_custom_call" | custom-call | flops 5242880 | bytes 8388608 | tf_op jit(solution)/shard_map/edge_terms/pallas_call | solution.py:654
  77.7 0.5 collective-permute-start.5
  78.2 4.9 %collective-permute-start.7 = (f32[64,16,128]{2,1,0:T(8,128)S(1)}, f32[64,16,128]{2,1,0:T(8,128)S(1)}, u32[]{:S(2)}, u32[]{:S(2)}) collective-permute-start(f32[64,16,128]{2,1,0:T(8,128)S(1)} %get-tuple-element.39), channel_id=1, source_target_pairs={{0,3},{1,2},{2,1},{3,0},{4,7},{5,6},{6,5},{7,4},{8,11},{9,10},{10,... | collective-permute-start | bytes 1572872 | tf_op jit(solution)/shard_map/ppermute | solution.py:697
  83.0 0.4 collective-permute-start.8
  83.4 2.5 %collective-permute-start.9 = (f32[8,2,16,128]{3,2,1,0:T(8,128)S(1)}, f32[8,2,16,128]{3,2,1,0:T(8,128)S(1)}, u32[]{:S(2)}, u32[]{:S(2)}) collective-permute-start(f32[8,2,16,128]{3,2,1,0:T(8,128)S(1)} %get-tuple-element.41), channel_id=1, source_target_pairs={{0,15},{1,14},{4,11},{5,10},{16,31},{17,30},{20,27},{21,26},{32,47... | collective-permute-start | bytes 393224 | tf_op jit(solution)/shard_map/ppermute | solution.py:697
  85.9 5.6 %local_terms.4.refs_0_ = f32[32,2,16,512]{3,2,1,0:T(8,128)S(1)} custom-call(f32[32,2,16,512]{3,2,1,0:T(8,128)S(1)} %get-tuple-element.36.refs_0_, f32[64,2,16,512]{3,2,1,0:T(8,128)S(1)} %bitcast.14, f32[1,4]{1,0:T(1,128)S(1)} %bitcast.18, f32[1,4]{1,0:T(1,128)S(1)} %bitcast.29, f32[1,4]{1,0:T(1,128)S(1)} %bitcast.32, f32[1,4]{1,0:T(1,128)S(1)} %bitcast.24, ...), custom_call_target="tpu_custom_call" | custom-call | flops 31457280 | bytes 6291456 | tf_op jit(solution)/shard_map/local_terms/pallas_call | solution.py:654
  91.5 0.7 collective-permute-done.7.refs_3_
  92.2 0.9 collective-permute-done.8.refs_4_
  93.1 2.9 %edge_terms.4 = (f32[32,2,16,512]{3,2,1,0:T(8,128)S(1)}, f32[8,2,16,512]{3,2,1,0:T(8,128)S(1)}, f32[64,16,128]{2,1,0:T(8,128)S(1)}, f32[64,16,128]{2,1,0:T(8,128...) custom-call(f32[32,2,16,512]{3,2,1,0:T(8,128)S(1)} %local_terms.4.refs_0_, ...), custom_call_target="tpu_custom_call" | custom-call | flops 5242880 | bytes 8388608 | tf_op jit(solution)/shard_map/edge_terms/pallas_call | solution.py:654
  96.0 0.4 collective-permute-start.10
  96.4 0.6 collective-permute-start.11
  97.1 2.3 %collective-permute-start.12 = (f32[64,16,128]{2,1,0:T(8,128)S(1)}, f32[64,16,128]{2,1,0:T(8,128)S(1)}, u32[]{:S(2)}, u32[]{:S(2)}) collective-permute-start(f32[64,16,128]{2,1,0:T(8,128)S(1)} %get-tuple-element.46), channel_id=1, source_target_pairs={{0,3},{1,2},{2,1},{3,0},{4,7},{5,6},{6,5},{7,4},{8,11},{9,10},{10,... | collective-permute-start | bytes 1572872 | tf_op jit(solution)/shard_map/ppermute | solution.py:697
  99.4 0.5 collective-permute-start.13
  99.9 4.0 %collective-permute-start.14 = (f32[8,2,16,128]{3,2,1,0:T(8,128)S(1)}, f32[8,2,16,128]{3,2,1,0:T(8,128)S(1)}, u32[]{:S(2)}, u32[]{:S(2)}) collective-permute-start(f32[8,2,16,128]{3,2,1,0:T(8,128)S(1)} %get-tuple-element.48), channel_id=1, source_target_pairs={{0,15},{1,14},{4,11},{5,10},{16,31},{17,30},{20,27},{21,26},{32,47... | collective-permute-start | bytes 393224 | tf_op jit(solution)/shard_map/ppermute | solution.py:697
  103.9 5.6 %local_terms.5 = (f32[32,2,16,512]{3,2,1,0:T(8,128)S(1)}, f32[32,2,16,512]{3,2,1,0:T(8,128)}) custom-call(f32[32,2,16,512]{3,2,1,0:T(8,128)S(1)} %get-tuple-element.42.refs_0_, f32[64,2,16,512]{3,2,1,0:T(8,128)S(1)} %bitcast.15, f32[1,4]{1,0:T(1,128)S(1)} %bitcast.20, f32[1,4]{1,0:T(1,128)S(1)} %bitcast.30, f32[1,4]{1,0:T(1,128)S(1)} %bitcast.33, ...), custom_call_target="tpu_custom_call" | custom-call | flops 31457280 | bytes 6291456 | tf_op jit(solution)/shard_map/local_terms/pallas_call | solution.py:654
  109.6 2.6 %edge_terms.5 = (f32[8,128,512]{2,1,0:T(8,128)}, f32[8,48,512]{2,1,0:T(8,128)}) custom-call(f32[32,2,16,512]{3,2,1,0:T(8,128)S(1)} %get-tuple-element.43.refs_0_, f32[8,2,16,512]{3,2,1,0:T(8,128)S(1)} %collective-permute-done.10.refs_1_.i0_in, f32[64,16,128]{2,1,0:T(8,128)S(1)} %collective-permute-done.11.refs_2_.j1_in, ...), custom_call_target="tpu_custom_call" | custom-call | flops 5242880 | bytes 6291456 | tf_op jit(solution)/shard_map/edge_terms/pallas_call | solution.py:654
  112.3 3.7 %all-to-all-start.1 = ((f32[8,128,512]{2,1,0:T(8,128)}), f32[8,128,512]{2,1,0:T(8,128)S(1)}, u32[]{:S(2)}, u32[]{:S(2)}) async-start(f32[8,128,512]{2,1,0:T(8,128)} %get-tuple-element.49), calls=%async_computation.1 | async-start | bytes 4194304 | tf_op jit(solution)/shard_map/all_to_all | solution.py:689
  116.0 7.6 %collective-permute-start.15 = (f32[8,48,512]{2,1,0:T(8,128)S(1)}, f32[8,48,512]{2,1,0:T(8,128)S(1)}, u32[]{:S(2)}, u32[]{:S(2)}) collective-permute-start(f32[8,48,512]{2,1,0:T(8,128)S(1)} %copy-done.12), channel_id=1, source_target_pairs={{16,0},{32,16},{48,32},{64,48},{80,64},{96,80},{112,96},{17,1},{33... | collective-permute-start | bytes 2359304 | tf_op jit(solution)/shard_map/ppermute | solution.py:693
  123.6 7.9 %gradient.1 = f32[8,512]{1,0:T(8,128)S(1)} custom-call(f32[32,2,16,512]{3,2,1,0:T(8,128)} %get-tuple-element.51.z_in, f32[8,8,2,16,512]{4,3,2,1,0:T(8,128)} %copy-done, f32[8,2,16,512]{3,2,1,0:T(8,128)} %copy-done.1, f32[64,16,128]{2,1,0:T(8,128)} %copy-done.2, f32[64,16,128]{2,1,0:T(8,128)} %copy-done.3, f32[64,16,128]{2,1,0:T(8,128)} %copy-done.4, ...), custom_call_target="tpu_custom_call" | custom-call | flops 31457280 | bytes 6291456 | tf_op jit(solution)/shard_map/gradient/pallas_call | solution.py:654
  131.6 3.6 %collective-permute-start.16 = (f32[8,512]{1,0:T(8,128)S(1)}, f32[8,512]{1,0:T(8,128)S(1)}, u32[]{:S(2)}, u32[]{:S(2)}) collective-permute-start(f32[8,512]{1,0:T(8,128)S(1)} %gradient.1), channel_id=1, source_target_pairs={{0,12},{1,13},{2,14},{3,15},{4,8},{5,9},{6,10},{7,11},{8,4},{9,5},... | collective-permute-start | bytes 49160 | tf_op jit(solution)/shard_map/ppermute | solution.py:768
  135.2 1.4 collective-permute-done.16
  136.6 1.0 join_blocks.1
  137.6 1.1 most_blocks.1
  138.8 8.2 %collective-permute-start.17 = (f32[8,80,512]{2,1,0:T(8,128)}, f32[8,80,512]{2,1,0:T(8,128)S(1)}, u32[]{:S(2)}, u32[]{:S(2)}) collective-permute-start(f32[8,80,512]{2,1,0:T(8,128)} %most_blocks.1), channel_id=1, source_target_pairs={{16,0},{32,16},{48,32},{64,48},{80,64},{96,80},{112,96},{17,1},{33... | collective-permute-start | bytes 3932168 | tf_op jit(solution)/shard_map/ppermute | solution.py:693
  147.0 4.3 %all-to-all-start.2 = ((f32[8,56,512]{2,1,0:T(8,128)}), f32[8,56,512]{2,1,0:T(8,128)}, u32[]{:S(2)}, u32[]{:S(2)}) async-start(f32[8,56,512]{2,1,0:T(8,128)} %join_blocks.1), calls=%async_computation.2 | async-start | bytes 1835008 | tf_op jit(solution)/shard_map/all_to_all | solution.py:689
  151.3 1.6 start_rows.1
  152.8 11.1 %collective-permute-done.17.most = f32[8,80,512]{2,1,0:T(8,128)S(1)} collective-permute-done((f32[8,80,512]{2,1,0:T(8,128)}, f32[8,80,512]{2,1,0:T(8,128)S(1)}, u32[]{:S(2)}, u32[]{:S(2)}) %collective-permute-start.17) | collective-permute-done | bytes 1310752 | tf_op jit(solution)/shard_map/ppermute | solution.py:693
  163.9 2.1 %defect_early.1.partial = f32[2,128,2048]{2,1,0:T(8,128)} custom-call(f32[8,80,512]{2,1,0:T(8,128)S(1)} %collective-permute-done.17.most, f32[2,128,2048]{2,1,0:T(8,128)} %bitcast.41), custom_call_target="tpu_custom_call" | custom-call | bytes 4194304 | tf_op jit(solution)/shard_map/defect_early/pallas_call | solution.py:654
  166.1 0.0 all-to-all-done.2.rest
  166.1 3.1 %defect_late.1 = (f32[2,128,2048]{2,1,0:T(8,128)}, f32[1,1,4]{2,1,0:T(1,128)}) custom-call(f32[2,128,2048]{2,1,0:T(8,128)} %defect_early.1.partial, f32[8,80,512]{2,1,0:T(8,128)S(1)} %collective-permute-done.17.most, f32[8,56,512]{2,1,0:T(8,128)} %all-to-all-done.2.rest, f32[2,128,2048]{2,1,0:T(8,128)} %bitcast.42), custom_call_target="tpu_custom_call", output_to_operand_aliasing={{0}: (0, {})} | custom-call | bytes 4194304 | tf_op jit(solution)/shard_map/defect_late/pallas_call | solution.py:654
  (34 shorter events, 0.1 us)
Async XLA Ops:
  59.1 44.7 %copy-start = (f32[8,8,2,16,512]{4,3,2,1,0:T(8,128)}, f32[8,8,2,16,512]{4,3,2,1,0:T(8,128)S(1)}, u32[]{:S(2)}) copy-start(f32[8,8,2,16,512]{4,3,2,1,0:T(8,128)S(1)} %all_to_all.15.rho_in) | copy-start | bytes 12582916
  59.1 8.4 %copy-start.5 = (f32[1,16]{1,0:T(1,128)S(1)}, f32[1,16]{1,0:T(1,128)}, u32[]{:S(2)}) copy-start(f32[1,16]{1,0:T(1,128)} %constant.6.refs_8_.roots) | copy-start | bytes 196
  59.1 8.4 %copy-start.6 = (f32[1,1,4]{2,1,0:T(1,128)S(1)}, f32[1,1,4]{2,1,0:T(1,128)}, u32[]{:S(2)}) copy-start(f32[1,1,4]{2,1,0:T(1,128)} %param.11) | copy-start | bytes 52
  59.1 8.4 %copy-start.7 = (f32[4]{0:T(128)S(1)}, f32[4]{0:T(128)}, u32[]{:S(2)}) copy-start(f32[4]{0:T(128)} %param.14) | copy-start | bytes 52
  59.2 8.4 %copy-start.8 = (f32[4]{0:T(128)S(1)}, f32[4]{0:T(128)}, u32[]{:S(2)}) copy-start(f32[4]{0:T(128)} %param.12) | copy-start | bytes 52
  59.2 8.4 %copy-start.9 = (f32[4]{0:T(128)S(1)}, f32[4]{0:T(128)}, u32[]{:S(2)}) copy-start(f32[4]{0:T(128)} %param.13) | copy-start | bytes 52
  59.2 8.4 %copy-start.10 = (f32[4]{0:T(128)S(1)}, f32[4]{0:T(128)}, u32[]{:S(2)}) copy-start(f32[4]{0:T(128)} %param.15) | copy-start | bytes 52
  59.2 8.4 %copy-start.11 = (f32[6]{0:T(128)S(1)}, f32[6]{0:T(128)}, u32[]{:S(2)}) copy-start(f32[6]{0:T(128)} %param.16) | copy-start | bytes 76
  59.7 14.8 %collective-permute-start = (f32[8,2,16,512]{3,2,1,0:T(8,128)S(1)}, f32[8,2,16,512]{3,2,1,0:T(8,128)S(1)}, u32[]{:S(2)}, u32[]{:S(2)}) collective-permute-start(f32[8,2,16,512]{3,2,1,0:T(8,128)S(1)} %get-tuple-element.31), channel_id=1, source_target_pairs={{0,12},{1,13},{2,14},{3,15},{4,8},{5,9},{6,10},{7,11},{8,4},{9,5},... | collective-permute-start | bytes 1572872 | tf_op jit(solution)/shard_map/ppermute | solution.py:697
  62.0 12.5 %collective-permute-start.1 = (f32[64,16,128]{2,1,0:T(8,128)S(1)}, f32[64,16,128]{2,1,0:T(8,128)S(1)}, u32[]{:S(2)}, u32[]{:S(2)}) collective-permute-start(f32[64,16,128]{2,1,0:T(8,128)S(1)} %get-tuple-element.32), channel_id=1, source_target_pairs={{0,1},{1,0},{2,3},{3,2},{4,5},{5,4},{6,7},{7,6},{8,9},{9,8},{10,11... | collective-permute-start | bytes 1572872 | tf_op jit(solution)/shard_map/ppermute | solution.py:697
  62.0 12.5 %collective-permute-start.2 = (f32[64,16,128]{2,1,0:T(8,128)S(1)}, f32[64,16,128]{2,1,0:T(8,128)S(1)}, u32[]{:S(2)}, u32[]{:S(2)}) collective-permute-start(f32[64,16,128]{2,1,0:T(8,128)S(1)} %get-tuple-element.33), channel_id=1, source_target_pairs={{0,3},{1,2},{2,1},{3,0},{4,7},{5,6},{6,5},{7,4},{8,11},{9,10},{10,... | collective-permute-start | bytes 1572872 | tf_op jit(solution)/shard_map/ppermute | solution.py:697
  64.2 10.6 %collective-permute-start.3 = (f32[64,16,128]{2,1,0:T(8,128)S(1)}, f32[64,16,128]{2,1,0:T(8,128)S(1)}, u32[]{:S(2)}, u32[]{:S(2)}) collective-permute-start(f32[64,16,128]{2,1,0:T(8,128)S(1)} %get-tuple-element.34), channel_id=1, source_target_pairs={{0,4},{1,5},{2,6},{3,7},{4,0},{5,1},{6,2},{7,3},{8,12},{9,13},{10,... | collective-permute-start | bytes 1572872 | tf_op jit(solution)/shard_map/ppermute | solution.py:697
  64.7 9.8 %collective-permute-start.4 = (f32[8,2,16,128]{3,2,1,0:T(8,128)S(1)}, f32[8,2,16,128]{3,2,1,0:T(8,128)S(1)}, u32[]{:S(2)}, u32[]{:S(2)}) collective-permute-start(f32[8,2,16,128]{3,2,1,0:T(8,128)S(1)} %get-tuple-element.35), channel_id=1, source_target_pairs={{0,15},{1,14},{4,11},{5,10},{16,31},{17,30},{20,27},{21,26},{32,47... | collective-permute-start | bytes 393224 | tf_op jit(solution)/shard_map/ppermute | solution.py:697
  77.7 13.8 %collective-permute-start.5 = (f32[8,2,16,512]{3,2,1,0:T(8,128)S(1)}, f32[8,2,16,512]{3,2,1,0:T(8,128)S(1)}, u32[]{:S(2)}, u32[]{:S(2)}) collective-permute-start(f32[8,2,16,512]{3,2,1,0:T(8,128)S(1)} %get-tuple-element.37), channel_id=1, source_target_pairs={{0,12},{1,13},{2,14},{3,15},{4,8},{5,9},{6,10},{7,11},{8,4},{9,5},... | collective-permute-start | bytes 1572872 | tf_op jit(solution)/shard_map/ppermute | solution.py:697
  78.2 13.3 %collective-permute-start.6 = (f32[64,16,128]{2,1,0:T(8,128)S(1)}, f32[64,16,128]{2,1,0:T(8,128)S(1)}, u32[]{:S(2)}, u32[]{:S(2)}) collective-permute-start(f32[64,16,128]{2,1,0:T(8,128)S(1)} %get-tuple-element.38), channel_id=1, source_target_pairs={{0,1},{1,0},{2,3},{3,2},{4,5},{5,4},{6,7},{7,6},{8,9},{9,8},{10,11... | collective-permute-start | bytes 1572872 | tf_op jit(solution)/shard_map/ppermute | solution.py:697
  78.2 14.1 %collective-permute-start.7 = (f32[64,16,128]{2,1,0:T(8,128)S(1)}, f32[64,16,128]{2,1,0:T(8,128)S(1)}, u32[]{:S(2)}, u32[]{:S(2)}) collective-permute-start(f32[64,16,128]{2,1,0:T(8,128)S(1)} %get-tuple-element.39), channel_id=1, source_target_pairs={{0,3},{1,2},{2,1},{3,0},{4,7},{5,6},{6,5},{7,4},{8,11},{9,10},{10,... | collective-permute-start | bytes 1572872 | tf_op jit(solution)/shard_map/ppermute | solution.py:697
  83.0 10.1 %collective-permute-start.8 = (f32[64,16,128]{2,1,0:T(8,128)S(1)}, f32[64,16,128]{2,1,0:T(8,128)S(1)}, u32[]{:S(2)}, u32[]{:S(2)}) collective-permute-start(f32[64,16,128]{2,1,0:T(8,128)S(1)} %get-tuple-element.40), channel_id=1, source_target_pairs={{0,4},{1,5},{2,6},{3,7},{4,0},{5,1},{6,2},{7,3},{8,12},{9,13},{10,... | collective-permute-start | bytes 1572872 | tf_op jit(solution)/shard_map/ppermute | solution.py:697
  83.4 8.1 %collective-permute-start.9 = (f32[8,2,16,128]{3,2,1,0:T(8,128)S(1)}, f32[8,2,16,128]{3,2,1,0:T(8,128)S(1)}, u32[]{:S(2)}, u32[]{:S(2)}) collective-permute-start(f32[8,2,16,128]{3,2,1,0:T(8,128)S(1)} %get-tuple-element.41), channel_id=1, source_target_pairs={{0,15},{1,14},{4,11},{5,10},{16,31},{17,30},{20,27},{21,26},{32,47... | collective-permute-start | bytes 393224 | tf_op jit(solution)/shard_map/ppermute | solution.py:697
  96.0 13.4 %collective-permute-start.10 = (f32[8,2,16,512]{3,2,1,0:T(8,128)S(1)}, f32[8,2,16,512]{3,2,1,0:T(8,128)S(1)}, u32[]{:S(2)}, u32[]{:S(2)}) collective-permute-start(f32[8,2,16,512]{3,2,1,0:T(8,128)S(1)} %get-tuple-element.44), channel_id=1, source_target_pairs={{0,12},{1,13},{2,14},{3,15},{4,8},{5,9},{6,10},{7,11},{8,4},{9,5},... | collective-permute-start | bytes 1572872 | tf_op jit(solution)/shard_map/ppermute | solution.py:697
  96.4 13.1 %collective-permute-start.11 = (f32[64,16,128]{2,1,0:T(8,128)S(1)}, f32[64,16,128]{2,1,0:T(8,128)S(1)}, u32[]{:S(2)}, u32[]{:S(2)}) collective-permute-start(f32[64,16,128]{2,1,0:T(8,128)S(1)} %get-tuple-element.45), channel_id=1, source_target_pairs={{0,1},{1,0},{2,3},{3,2},{4,5},{5,4},{6,7},{7,6},{8,9},{9,8},{10,11... | collective-permute-start | bytes 1572872 | tf_op jit(solution)/shard_map/ppermute | solution.py:697
  97.1 12.5 %collective-permute-start.12 = (f32[64,16,128]{2,1,0:T(8,128)S(1)}, f32[64,16,128]{2,1,0:T(8,128)S(1)}, u32[]{:S(2)}, u32[]{:S(2)}) collective-permute-start(f32[64,16,128]{2,1,0:T(8,128)S(1)} %get-tuple-element.46), channel_id=1, source_target_pairs={{0,3},{1,2},{2,1},{3,0},{4,7},{5,6},{6,5},{7,4},{8,11},{9,10},{10,... | collective-permute-start | bytes 1572872 | tf_op jit(solution)/shard_map/ppermute | solution.py:697
  99.4 10.2 %collective-permute-start.13 = (f32[64,16,128]{2,1,0:T(8,128)S(1)}, f32[64,16,128]{2,1,0:T(8,128)S(1)}, u32[]{:S(2)}, u32[]{:S(2)}) collective-permute-start(f32[64,16,128]{2,1,0:T(8,128)S(1)} %get-tuple-element.47), channel_id=1, source_target_pairs={{0,4},{1,5},{2,6},{3,7},{4,0},{5,1},{6,2},{7,3},{8,12},{9,13},{10,... | collective-permute-start | bytes 1572872 | tf_op jit(solution)/shard_map/ppermute | solution.py:697
  99.9 9.6 %collective-permute-start.14 = (f32[8,2,16,128]{3,2,1,0:T(8,128)S(1)}, f32[8,2,16,128]{3,2,1,0:T(8,128)S(1)}, u32[]{:S(2)}, u32[]{:S(2)}) collective-permute-start(f32[8,2,16,128]{3,2,1,0:T(8,128)S(1)} %get-tuple-element.48), channel_id=1, source_target_pairs={{0,15},{1,14},{4,11},{5,10},{16,31},{17,30},{20,27},{21,26},{32,47... | collective-permute-start | bytes 393224 | tf_op jit(solution)/shard_map/ppermute | solution.py:697
  109.5 2.7 %copy-start.1 = (f32[8,2,16,512]{3,2,1,0:T(8,128)}, f32[8,2,16,512]{3,2,1,0:T(8,128)S(1)}, u32[]{:S(2)}) copy-start(f32[8,2,16,512]{3,2,1,0:T(8,128)S(1)} %collective-permute-done.10.refs_1_.i0_in) | copy-start | bytes 1572868
  109.5 2.7 %copy-start.2 = (f32[64,16,128]{2,1,0:T(8,128)}, f32[64,16,128]{2,1,0:T(8,128)S(1)}, u32[]{:S(2)}) copy-start(f32[64,16,128]{2,1,0:T(8,128)S(1)} %collective-permute-done.11.refs_2_.j1_in) | copy-start | bytes 1572868
  109.5 2.7 %copy-start.3 = (f32[64,16,128]{2,1,0:T(8,128)}, f32[64,16,128]{2,1,0:T(8,128)S(1)}, u32[]{:S(2)}) copy-start(f32[64,16,128]{2,1,0:T(8,128)S(1)} %collective-permute-done.12.refs_3_.j0_in) | copy-start | bytes 1572868
  109.6 2.7 %copy-start.4 = (f32[64,16,128]{2,1,0:T(8,128)}, f32[64,16,128]{2,1,0:T(8,128)S(1)}, u32[]{:S(2)}) copy-start(f32[64,16,128]{2,1,0:T(8,128)S(1)} %collective-permute-done.13.refs_4_.i2_in) | copy-start | bytes 1572868
  112.2 3.8 %copy-start.12 = (f32[8,48,512]{2,1,0:T(8,128)S(1)}, f32[8,48,512]{2,1,0:T(8,128)}, u32[]{:S(2)}) copy-start(f32[8,48,512]{2,1,0:T(8,128)} %get-tuple-element.50) | copy-start | bytes 2359300
  112.3 25.4 %all-to-all-start.1 = ((f32[8,128,512]{2,1,0:T(8,128)}), f32[8,128,512]{2,1,0:T(8,128)S(1)}, u32[]{:S(2)}, u32[]{:S(2)}) async-start(f32[8,128,512]{2,1,0:T(8,128)} %get-tuple-element.49), calls=%async_computation.1 | async-start | bytes 4194304 | tf_op jit(solution)/shard_map/all_to_all | solution.py:689
  116.0 20.6 %collective-permute-start.15 = (f32[8,48,512]{2,1,0:T(8,128)S(1)}, f32[8,48,512]{2,1,0:T(8,128)S(1)}, u32[]{:S(2)}, u32[]{:S(2)}) collective-permute-start(f32[8,48,512]{2,1,0:T(8,128)S(1)} %copy-done.12), channel_id=1, source_target_pairs={{16,0},{32,16},{48,32},{64,48},{80,64},{96,80},{112,96},{17,1},{33... | collective-permute-start | bytes 2359304 | tf_op jit(solution)/shard_map/ppermute | solution.py:693
  131.6 5.1 %collective-permute-start.16 = (f32[8,512]{1,0:T(8,128)S(1)}, f32[8,512]{1,0:T(8,128)S(1)}, u32[]{:S(2)}, u32[]{:S(2)}) collective-permute-start(f32[8,512]{1,0:T(8,128)S(1)} %gradient.1), channel_id=1, source_target_pairs={{0,12},{1,13},{2,14},{3,15},{4,8},{5,9},{6,10},{7,11},{8,4},{9,5},... | collective-permute-start | bytes 49160 | tf_op jit(solution)/shard_map/ppermute | solution.py:768
  138.8 25.2 %collective-permute-start.17 = (f32[8,80,512]{2,1,0:T(8,128)}, f32[8,80,512]{2,1,0:T(8,128)S(1)}, u32[]{:S(2)}, u32[]{:S(2)}) collective-permute-start(f32[8,80,512]{2,1,0:T(8,128)} %most_blocks.1), channel_id=1, source_target_pairs={{16,0},{32,16},{48,32},{64,48},{80,64},{96,80},{112,96},{17,1},{33... | collective-permute-start | bytes 3932168 | tf_op jit(solution)/shard_map/ppermute | solution.py:693
  147.0 19.2 %all-to-all-start.2 = ((f32[8,56,512]{2,1,0:T(8,128)}), f32[8,56,512]{2,1,0:T(8,128)}, u32[]{:S(2)}, u32[]{:S(2)}) async-start(f32[8,56,512]{2,1,0:T(8,128)} %join_blocks.1), calls=%async_computation.2 | async-start | bytes 1835008 | tf_op jit(solution)/shard_map/all_to_all | solution.py:689
